TPU v7x, 256 devices: a whole 4x4x8 slice. The times are simulated.
256 devices in a mesh: sec: 2 (over core), tok: 8 (over x, y_lo), voc: 16 (over y_hi, z).
Axes of the slice: x: 4, y: 4 (y_hi: 2, y_lo: 2; y = y_hi * 2 + y_lo), z: 8, core: 2. Of those that a mesh axis runs over, the one named last changes fastest.
Arguments:
- context: bfloat16 [512, 2048], P(('sec', 'tok'), 'voc'), may hold values from -6 to 6
- residual_in: bfloat16 [512, 4608], P(('sec', 'tok'), 'voc'), may hold values from -6 to 6
- out_proj: bfloat16 [2048, 4608], P('voc'), may hold values from -0.125 to 0.125
- post_gain: float32 [4608], P('voc'), may hold values from 0.25 to 1.75
- final_gain: float32 [4608], P('voc'), may hold values from 0.25 to 1.75
- teacher_head: bfloat16 [131072, 4608], P(('sec', 'tok', 'voc')), may hold values from -0.25 to 0.25
- student_hidden: bfloat16 [512, 3584], P(('sec', 'tok'), 'voc'), may hold values from -6 to 6
- student_gain: float32 [3584], replicated, may hold values from 0.25 to 1.75
- student_head: bfloat16 [131072, 3584], P(('sec', 'tok', 'voc')), may hold values from -0.3125 to 0.3125
- kl_weight: float32 [512], replicated, may hold values from 20 to 200
Outputs:
- token_kl: float32 [512], P(('sec', 'tok', 'voc'))
- grad_hidden: bfloat16 [512, 3584], P(('sec', 'tok'), 'voc')
- grad_head: bfloat16 [131072, 3584], P(('sec', 'tok', 'voc'))
All inputs are finite; a program needn't handle non-finite values.
Results may differ from a plain program's by a relative error of at most 0.014.
Values may be sent and summed in bfloat16 or wider, within the bound.
No kernel may reach another device: no remote copies, remote signals or barrier semaphores. Data moves between devices by JAX's collectives and lax.ppermute only.
A program may use at most 128 MiB of HBM per device.

v0:
```python
import jax
import jax.numpy as jnp
from jax import lax
from jax.sharding import PartitionSpec as P

epsilon = 1e-06
softcap = 30.0


def local(
    context,
    residual_in,
    out_proj,
    post_gain,
    final_gain,
    teacher_head,
    student_hidden,
    student_gain,
    student_head,
    kl_weight,
):
    voc_count = lax.axis_size("voc")
    row_groups = lax.axis_size(("sec", "tok"))
    all_count = voc_count * row_groups
    tok_rows = context.shape[0]
    teacher_cols = residual_in.shape[1]
    student_cols = student_hidden.shape[1]
    teacher_width = teacher_cols * voc_count
    student_width = student_cols * voc_count
    voc_rows = teacher_head.shape[0]
    all_tokens = tok_rows * row_groups
    attention = lax.psum_scatter(
        jnp.dot(context, out_proj, preferred_element_type=jnp.float32),
        "voc",
        scatter_dimension=1,
        tiled=True,
    )
    raw_student = student_hidden.astype(jnp.float32)
    gain_piece = lax.dynamic_slice_in_dim(
        student_gain, lax.axis_index("voc") * student_cols, student_cols
    )
    attention_sq = jnp.sum(attention * attention, axis=1)
    post_total, student_sq = lax.psum(
        (attention_sq, jnp.sum(raw_student * raw_student, axis=1)), "voc"
    )
    own_scale = lax.rsqrt(student_sq / student_width + epsilon)
    student_piece = (raw_student * own_scale[:, None] * gain_piece).astype(jnp.bfloat16)
    hidden = (
        residual_in.astype(jnp.float32)
        + attention * lax.rsqrt(post_total / teacher_width + epsilon)[:, None] * post_gain
    )
    final_total = lax.psum(jnp.sum(hidden * hidden, axis=1), "voc")
    teacher_piece = (
        hidden * lax.rsqrt(final_total / teacher_width + epsilon)[:, None] * final_gain
    ).astype(jnp.bfloat16)
    teacher_all, student_all = (
        lax.all_gather(teacher_piece, ("sec", "tok", "voc"), axis=0, tiled=True),
        lax.all_gather(student_piece, ("sec", "tok", "voc"), axis=0, tiled=True),
    )
    teacher_all = teacher_all.reshape(row_groups, voc_count, tok_rows, teacher_cols)
    student_all = student_all.reshape(row_groups, voc_count, tok_rows, student_cols)
    teacher_blocks = teacher_head.reshape(voc_rows, voc_count, teacher_cols)
    student_blocks = student_head.reshape(voc_rows, voc_count, student_cols)
    teacher_raw = jnp.einsum(
        "bwtd,vwd->btv", teacher_all, teacher_blocks, preferred_element_type=jnp.float32
    ).reshape(all_tokens, voc_rows)
    student_raw = jnp.einsum(
        "bwtd,vwd->btv", student_all, student_blocks, preferred_element_type=jnp.float32
    ).reshape(all_tokens, voc_rows)
    teacher_logit = softcap * jnp.tanh(teacher_raw / softcap)
    student_tanh = jnp.tanh(student_raw / softcap)
    student_logit = softcap * student_tanh
    teacher_exp = jnp.exp(teacher_logit)
    student_exp = jnp.exp(student_logit)
    kl_count = all_tokens // all_count
    kl_start = lax.axis_index(("sec", "tok", "voc")) * kl_count
    teacher_total, student_total = lax.psum(
        (jnp.sum(teacher_exp, axis=1), jnp.sum(student_exp, axis=1)), ("sec", "tok", "voc")
    )
    teacher_prob = teacher_exp / teacher_total[:, None]
    cross_term = lax.psum_scatter(
        jnp.sum(teacher_prob * (teacher_logit - student_logit), axis=1),
        ("sec", "tok", "voc"),
        scatter_dimension=0,
        tiled=True,
    )
    own_teacher = lax.dynamic_slice_in_dim(teacher_total, kl_start, kl_count)
    own_student = lax.dynamic_slice_in_dim(student_total, kl_start, kl_count)
    token_kl = cross_term + jnp.log(own_student) - jnp.log(own_teacher)
    student_prob = student_exp / student_total[:, None]
    logit_grad = (
        kl_weight[:, None] * (student_prob - teacher_prob) * (1.0 - student_tanh * student_tanh)
    ).astype(jnp.bfloat16)
    grad_blocks = logit_grad.reshape(row_groups, tok_rows, voc_rows)
    grad_head = (
        jnp.einsum("btv,bwtd->vwd", grad_blocks, student_all, preferred_element_type=jnp.float32)
        .reshape(voc_rows, student_width)
        .astype(jnp.bfloat16)
    )
    grad_rows = lax.psum_scatter(
        jnp.dot(logit_grad, student_head, preferred_element_type=jnp.float32),
        ("sec", "tok"),
        scatter_dimension=0,
        tiled=True,
    )
    grad_normed = lax.psum_scatter(grad_rows, "voc", scatter_dimension=1, tiled=True)
    inner_total = lax.psum(jnp.sum(raw_student * gain_piece * grad_normed, axis=1), "voc")
    cubed = own_scale * own_scale * own_scale
    grad_hidden = (
        own_scale[:, None] * gain_piece * grad_normed
        - raw_student * cubed[:, None] * inner_total[:, None] / student_width
    ).astype(jnp.bfloat16)
    return (token_kl, grad_hidden, grad_head)


def solution(mesh):
    return jax.shard_map(
        local,
        mesh=mesh,
        in_specs=(
            P(("sec", "tok"), "voc"),
            P(("sec", "tok"), "voc"),
            P("voc", None),
            P("voc"),
            P("voc"),
            P(("sec", "tok", "voc"), None),
            P(("sec", "tok"), "voc"),
            P(),
            P(("sec", "tok", "voc"), None),
            P(),
        ),
        out_specs=(
            P(("sec", "tok", "voc")),
            P(("sec", "tok"), "voc"),
            P(("sec", "tok", "voc"), None),
        ),
        check_vma=False,
    )
```

profile of v0, /device:TPU:32, one launch (start us, length us, event | category | flops | bytes accessed | tf_op | source)
XLA Modules:
  0.0 1720.8 jit_solution(6524048204806873108)
XLA Ops:
  7.2 0.0 copy-start
  7.2 0.0 copy-start.1
  7.2 0.0 copy-start.2
  7.2 0.0 copy-start.3
  7.2 0.0 reduce-scatter.10.cloned.1.call-start
  7.3 1.2 copy-done
  8.4 2.7 convolution_bitcast_fusion
  11.1 0.0 reduce-scatter.10.cloned.1.call-update
  11.2 0.0 all-gather.5.cloned.1.call-start
  11.2 0.8 dynamic_slice.9
  12.0 0.1 fusion.25
  12.1 213.2 %reduce-scatter.10.cloned.1.call-done = f32[288,32]{1,0:T(8,128)} async-done(((f32[4608,32]{1,0:T(8,128)}), f32[288,32]{1,0:T(8,128)}) %reduce-scatter.10.cloned.1.call-update) | async-done | bytes 36880
  225.3 1.0 copy.33
  226.3 0.1 multiply_reduce_fusion.2
  226.5 38.1 %psum.42 = f32[32]{0:T(128)S(1)} all-reduce(f32[32]{0:T(128)S(1)} %multiply_reduce_fusion.2), channel_id=1, replica_groups=mesh['sec'=2,'tok'=8,'voc'=16] {'voc'}, use_global_device_ids=true, to_apply=%region_2.0 | all-reduce | flops 32 | bytes 256 | tf_op jit(solution)/shard_map/psum | solution.py:43
  264.5 0.2 multiply_reduce_fusion.1
  264.7 39.1 %all-reduce.2 = (f32[32]{0:T(128)S(1)}, f32[32]{0:T(128)S(1)}) all-reduce(f32[32]{0:T(128)S(1)} %fusion.25, f32[32]{0:T(128)S(1)} %multiply_reduce_fusion.1), channel_id=1, replica_groups=mesh['sec'=2,'tok'=8,'voc'=16] {'voc'}, use_global_device_ids=true, to_apply=%region_8.0 | all-reduce | flops 64 | bytes 512 | tf_op jit(solution)/shard_map/psum | solution.py:43
  303.8 0.7 fusion.27
  304.5 0.0 all-gather.5.cloned.1.call-update
  304.5 0.0 all-gather.3.cloned.1.call-start
  304.6 0.7 multiply_convert_fusion.1
  305.3 0.0 all-gather.3.cloned.1.call-update
  305.3 0.0 reduce-scatter.8.cloned.1.call-start
  305.4 6.7 copy.26
  312.1 5.9 copy.29
  318.0 397.6 %all-gather.5.cloned.1.call-done = bf16[8192,224]{1,0:T(8,128)(2,1)} async-done(((bf16[32,224]{1,0:T(8,128)(2,1)}), bf16[8192,224]{1,0:T(8,128)(2,1)}) %all-gather.5.cloned.1.call-update) | async-done | bytes 3670032 | tf_op jit(solution)/shard_map/all_gather | solution.py:58
  715.6 7.1 copy.60
  722.8 410.2 %all-gather.3.cloned.1.call-done = bf16[8192,288]{1,0:T(8,128)(2,1)} async-done(((bf16[32,288]{1,0:T(8,128)(2,1)}), bf16[8192,288]{1,0:T(8,128)(2,1)}) %all-gather.3.cloned.1.call-update) | async-done | bytes 4718608 | tf_op jit(solution)/shard_map/all_gather | solution.py:57
  1133.0 5.6 copy.25
  1138.6 3.2 exponential_reduce_fusion.1
  1141.7 72.7 %psum.44 = f32[512]{0:T(512)S(1)} all-reduce(f32[512]{0:T(512)S(1)} %get-tuple-element.13), channel_id=1, replica_groups=mesh['sec'=2,'tok'=8,'voc'=16] {'sec','tok','voc'}, use_global_device_ids=true, to_apply=%region_6.0 | all-reduce | flops 512 | bytes 4096 | tf_op jit(solution)/shard_map/psum | solution.py:77
  1214.5 8.1 exponential_reduce_fusion
  1222.5 74.7 %all-reduce.1 = (f32[512]{0:T(512)S(1)}, f32[512]{0:T(512)S(1)}) all-reduce(f32[512]{0:T(512)S(1)} %get-tuple-element.4, f32[512]{0:T(512)S(1)} %get-tuple-element.3), channel_id=3, replica_groups=mesh['sec'=2,'tok'=8,'voc'=16] {'sec','tok','voc'}, use_global_device_ids=true, to_apply=%region_10.0.clone | all-reduce | flops 1024 | bytes 8192
  1297.2 1.7 multiply_convert_fusion
  1299.0 7.1 fusion.35
  1306.1 0.0 reduce-scatter.8.cloned.1.call-update
  1306.1 0.0 reduce-scatter.12.cloned.1.call-start
  1306.1 9.2 dot_general.36
  1315.3 0.6 fusion.34
  1315.9 147.6 %reduce-scatter.8.cloned.1.call-done = f32[32,3584]{1,0:T(8,128)} async-done(((f32[512,3584]{1,0:T(8,128)}), f32[32,3584]{1,0:T(8,128)}) %reduce-scatter.8.cloned.1.call-update) | async-done | bytes 458768 | tf_op jit(solution)/shard_map/reduce_scatter | solution.py:100
  1463.5 2.8 copy.34
  1466.3 0.0 reduce-scatter.12.cloned.1.call-update
  1466.4 6.0 bitcast_convert_fusion
  1472.3 202.1 %reduce-scatter.12.cloned.1.call-done = f32[224,32]{1,0:T(8,128)} async-done(((f32[3584,32]{1,0:T(8,128)}), f32[224,32]{1,0:T(8,128)}) %reduce-scatter.12.cloned.1.call-update) | async-done | bytes 28688
  1674.4 1.0 copy.35
  1675.4 0.1 fusion.33
  1675.5 38.1 %psum.47 = f32[32]{0:T(128)S(1)} all-reduce(f32[32]{0:T(128)S(1)} %fusion.33), channel_id=1, replica_groups=mesh['sec'=2,'tok'=8,'voc'=16] {'voc'}, use_global_device_ids=true, to_apply=%region_16.0 | all-reduce | flops 32 | bytes 256 | tf_op jit(solution)/shard_map/psum | solution.py:107
  1713.6 0.7 fusion.31
  (15 shorter events, 0.0 us)
Async XLA Ops:
  7.2 1.3 copy-start
  7.2 4.8 copy-start.1
  7.2 257.3 %copy-start.2 = (bf16[32,288]{1,0:T(8,128)(2,1)S(1)}, bf16[32,288]{1,0:T(8,128)(2,1)}, u32[]{:S(2)}) copy-start(bf16[32,288]{1,0:T(8,128)(2,1)} %param.11) | copy-start | bytes 55300
  7.2 257.3 %copy-start.3 = (f32[288]{0:T(512)S(1)}, f32[288]{0:T(512)}, u32[]{:S(2)}) copy-start(f32[288]{0:T(512)} %param.13) | copy-start | bytes 3460
  7.2 297.4 %copy-start.4 = (f32[288]{0:T(512)S(1)}, f32[288]{0:T(512)}, u32[]{:S(2)}) copy-start(f32[288]{0:T(512)} %param.14) | copy-start | bytes 3460
  7.2 218.1 %reduce-scatter.10.cloned.1.call-start = ((), (), s32[]{:S(2)}) async-start(), calls=%async_computation.6 | async-start | bytes 2506752
  11.2 704.5 %all-gather.5.cloned.1.call-start = ((), (), s32[]{:S(2)}) async-start(), calls=%async_computation.4 | async-start | bytes 4210688 | tf_op jit(solution)/shard_map/all_gather | solution.py:58
  304.5 828.4 %all-gather.3.cloned.1.call-start = ((), (), s32[]{:S(2)}) async-start(), calls=%async_computation.3 | async-start | bytes 6316032 | tf_op jit(solution)/shard_map/all_gather | solution.py:57
  305.3 1158.2 %reduce-scatter.8.cloned.1.call-start = ((), (), s32[]{:S(2)}) async-start(), calls=%async_computation.5 | async-start | bytes 7798784 | tf_op jit(solution)/shard_map/reduce_scatter | solution.py:100
  715.6 422.9 %slice-start = ((s8[4718592]{0:T(1024)(128)(4,1)}), s8[524288]{0:T(1024)(128)(4,1)S(1)}, s32[]{:S(2)}) async-start(s8[4718592]{0:T(1024)(128)(4,1)} %bitcast.52), calls=%async_computation.8 | async-start | bytes 1048576
  1133.0 5.6 slice-start.1
  1214.5 82.7 %copy-start.5 = (f32[512]{0:T(512)S(1)}, f32[512]{0:T(512)}, u32[]{:S(2)}) copy-start(f32[512]{0:T(512)} %param.19) | copy-start | bytes 6148
  1306.1 368.3 %reduce-scatter.12.cloned.1.call-start = ((), (), s32[]{:S(2)}) async-start(), calls=%async_computation.7 | async-start | bytes 1949696
Sparse Core Ops, SparseCore 0:
  12.6 212.7 reduce-scatter.9
  304.7 410.9 all-gather.4
  717.5 415.4 all-gather.2
  1306.2 157.2 reduce-scatter.7
  1467.2 207.1 reduce-scatter.11
where the time goes:
time: 1720 us
  waiting for transfers between devices  1370 us (80%)
  blocking collectives  263 us (15%)
  local copies, waits for them, and re-layouts  41.3 us (2%)
  matrix products  27 us (2%)
    unnamed x7, waiting for transfers between devices  415 us
    all_gather x1, waiting for transfers between devices, local(): lax.all_gather(teacher_piece, ('sec', 'tok', 'voc'), axis=0, tiled=True)  410 us
    all_gather x1, waiting for transfers between devices, local(): lax.all_gather(student_piece, ('sec', 'tok', 'voc'), axis=0, tiled=True)  398 us
    reduce_scatter x1, waiting for transfers between devices, local(): lax.psum_scatter(jnp.dot(logit_grad, student_head, preferred_element_type...  148 us
    psum x2, blocking collectives, local(): lax.psum((attention_sq, jnp.sum(raw_student * raw_student, axis=1)), 'voc')  77.2 us
    unnamed x1, blocking collectives  74.7 us
    psum x1, blocking collectives, local(): lax.psum((jnp.sum(teacher_exp, axis=1), jnp.sum(student_exp, axis=1)), ('...  72.7 us
    psum x1, blocking collectives, local(): lax.psum(jnp.sum(raw_student * gain_piece * grad_normed, axis=1), 'voc')  38.1 us
  transfers between devices with their start and end apart: 5, of which 5 were waited for; matrix products, arithmetic and copies ran while one was open for 2% of the time, Pallas kernels for 0%

commit v1 on v0

v1 whole, which is shorter than its diff:
```python
import jax
import jax.numpy as jnp
from jax import lax
from jax.sharding import Mesh
from jax.sharding import PartitionSpec as P

epsilon = 1e-06
softcap = 30.0
ROW = ("x", "yl")
VOC = ("yh", "z")
XY = ("x", "yl", "yh")
PLANE = ("x", "yl", "yh", "z")
bf16 = jnp.bfloat16
f32 = jnp.float32


def swap(value):
    return lax.ppermute(value, "c", [(0, 1), (1, 0)])


def spread(value, axes):
    count = lax.axis_size(axes)
    return lax.all_to_all(jnp.broadcast_to(value[None], (count, *value.shape)), axes, 0, 0)


def halves(value):
    high = lax.reduce_precision(value, 8, 7)
    return high.astype(bf16), (value - high).astype(bf16)


def dot_t(left, right):
    return lax.dot_general(left, right, (((1,), (1,)), ((), ())), preferred_element_type=f32)


def dot_0(left, right):
    return lax.dot_general(left, right, (((0,), (0,)), ((), ())), preferred_element_type=f32)


def local(
    context,
    residual_in,
    out_proj,
    post_gain,
    final_gain,
    teacher_head,
    student_hidden,
    student_gain,
    student_head,
    kl_weight,
):
    voc_count = lax.axis_size(VOC)
    row_count = lax.axis_size(ROW)
    rows = context.shape[0]
    teacher_cols = residual_in.shape[1]
    student_cols = student_hidden.shape[1]
    teacher_width = teacher_cols * voc_count
    student_width = student_cols * voc_count
    own = rows // voc_count
    half = rows * row_count
    voc_index = lax.axis_index(VOC)
    row_index = lax.axis_index(ROW)
    half_start = lax.axis_index("c") * half

    teacher_other = swap(teacher_head)
    student_other = swap(student_head)

    partial = jnp.dot(context, out_proj, preferred_element_type=f32).astype(bf16)
    raw_student = student_hidden.astype(f32)
    gains = jnp.stack(halves(jnp.concatenate([post_gain, final_gain])))
    squares = jnp.stack(halves(jnp.sum(raw_student * raw_student, axis=1)))
    shared = jnp.concatenate([gains, squares], axis=1)
    sent = jnp.concatenate(
        [
            partial.reshape(voc_count, own, teacher_width),
            residual_in.reshape(voc_count, own, teacher_cols),
            student_hidden.reshape(voc_count, own, student_cols),
            jnp.broadcast_to(shared[None], (voc_count, *shared.shape)),
        ],
        axis=2,
    )
    got = lax.all_to_all(sent, VOC, 0, 0)
    ends = [teacher_width, teacher_cols, student_cols, 2 * teacher_cols]
    at = [sum(ends[:i]) for i in range(5)]
    attention = jnp.sum(got[:, :, : at[1]].astype(f32), axis=0)
    residual = got[:, :, at[1] : at[2]].transpose(1, 0, 2).reshape(own, teacher_width)
    student_rows = got[:, :, at[2] : at[3]].transpose(1, 0, 2).reshape(own, student_width)
    gain_all = jnp.sum(got[:, :, at[3] : at[4]].astype(f32), axis=1)
    post_all = gain_all[:, :teacher_cols].reshape(teacher_width)
    final_all = gain_all[:, teacher_cols:].reshape(teacher_width)
    own_square = jnp.sum(got[:, :, at[4] :].astype(f32), axis=(0, 1))
    own_scale = lax.rsqrt(own_square / student_width + epsilon)

    post_scale = lax.rsqrt(jnp.mean(attention * attention, axis=1, keepdims=True) + epsilon)
    hidden = residual.astype(f32) + attention * post_scale * post_all
    final_scale = lax.rsqrt(jnp.mean(hidden * hidden, axis=1, keepdims=True) + epsilon)
    teacher_rows = (hidden * final_scale * final_all).astype(bf16)
    student_f = student_rows.astype(f32)
    row_scale = lax.rsqrt(jnp.mean(student_f * student_f, axis=1, keepdims=True) + epsilon)
    normed_rows = (student_f * row_scale * student_gain).astype(bf16)

    both = jnp.concatenate([teacher_rows, normed_rows], axis=1)
    both = spread(both, "z").reshape(-1, both.shape[1])
    both = spread(both, XY).reshape(half, -1)
    teacher_all = both[:, :teacher_width]
    student_all = both[:, teacher_width:]
    student_all_other = swap(student_all)

    def logits(teacher_rows_of, student_rows_of):
        teacher_logit = softcap * jnp.tanh(dot_t(teacher_all, teacher_rows_of) / softcap)
        student_tanh = jnp.tanh(dot_t(student_all, student_rows_of) / softcap)
        student_logit = softcap * student_tanh
        teacher_exp = jnp.exp(teacher_logit)
        student_exp = jnp.exp(student_logit)
        sums = jnp.stack(
            [
                jnp.sum(teacher_exp, axis=1),
                jnp.sum(student_exp, axis=1),
                jnp.sum(teacher_exp * (teacher_logit - student_logit), axis=1),
            ]
        )
        return teacher_exp, student_exp, student_tanh, sums

    mine = logits(teacher_head, student_head)
    others = logits(teacher_other, student_other)
    sums = (mine[3] + others[3]).reshape(-1, 128)
    totals = jnp.sum(spread(sums, PLANE), axis=0).reshape(3, half)
    teacher_total, student_total, mixed = totals[0], totals[1], totals[2]
    token_kl = mixed / teacher_total + jnp.log(student_total) - jnp.log(teacher_total)
    token_kl = lax.dynamic_slice_in_dim(token_kl, row_index * rows + voc_index * own, own)
    weight = lax.dynamic_slice_in_dim(kl_weight, half_start, half)

    def gradient(parts):
        teacher_prob = parts[0] / teacher_total[:, None]
        student_prob = parts[1] / student_total[:, None]
        return (
            weight[:, None] * (student_prob - teacher_prob) * (1.0 - parts[2] * parts[2])
        ).astype(bf16)

    grad_mine = gradient(mine)
    grad_others = gradient(others)
    grad_back = swap(grad_others)
    terms = (
        jnp.dot(grad_mine, student_head, preferred_element_type=f32)
        + jnp.dot(grad_others, student_other, preferred_element_type=f32)
    ).astype(bf16)
    parts = lax.all_to_all(terms.reshape(row_count, rows, student_width), ROW, 0, 0)
    grad_head = (dot_0(grad_mine, student_all) + dot_0(grad_back, student_all_other)).astype(bf16)
    grad_rows = jnp.sum(parts.astype(f32), axis=0)
    own_normed = lax.dynamic_slice_in_dim(student_all, row_index * rows, rows).astype(f32)
    inner = jnp.stack(halves(jnp.sum(own_normed * grad_rows, axis=1)), axis=1)
    last = jnp.concatenate(
        [
            grad_rows.astype(bf16).reshape(rows, voc_count, student_cols).transpose(1, 0, 2),
            jnp.broadcast_to(inner[None], (voc_count, *inner.shape)),
        ],
        axis=2,
    )
    last = jnp.sum(lax.all_to_all(last, VOC, 0, 0).astype(f32), axis=0)
    grad_normed = last[:, :student_cols]
    inner_total = jnp.sum(last[:, student_cols:], axis=1) / own_scale
    gain_piece = lax.dynamic_slice_in_dim(student_gain, voc_index * student_cols, student_cols)
    cubed = own_scale * own_scale * own_scale
    grad_hidden = (
        own_scale[:, None] * gain_piece * grad_normed
        - raw_student * cubed[:, None] * inner_total[:, None] / student_width
    ).astype(bf16)
    return (token_kl, grad_hidden, grad_head)


def solution(mesh):
    sec, tok, voc = mesh.devices.shape
    fine = Mesh(mesh.devices.reshape(sec, tok // 2, 2, 2, voc // 2), ("c", "x", "yl", "yh", "z"))
    row = ("c", "x", "yl")
    every = ("c", "x", "yl", "yh", "z")
    return jax.shard_map(
        local,
        mesh=fine,
        in_specs=(
            P(row, VOC),
            P(row, VOC),
            P(VOC, None),
            P(VOC),
            P(VOC),
            P(every, None),
            P(row, VOC),
            P(),
            P(every, None),
            P(),
        ),
        out_specs=(P(every), P(row, VOC), P(every, None)),
        check_vma=False,
    )
```

time: 1720 us -> 225 us (0.13)
  waiting for transfers between devices: 1370 us -> 90.6 us
  blocking collectives: 263 us -> 38 us
  starting transfers between devices: 0.21 us -> 36.9 us
  local copies, waits for them, and re-layouts: 41.3 us -> 13 us
    all_gather x2 -> x0, waiting for transfers between devices: 808 us -> none  [the longest x1 410 us: local(): lax.all_gather(teacher_piece, ('sec', 'tok', 'voc'), axis=0, tiled=True)]
    unnamed x7 -> x0, waiting for transfers between devices: 415 us -> none
    psum x4 -> x0, blocking collectives: 188 us -> none  [the longest x2 77.2 us: local(): lax.psum((attention_sq, jnp.sum(raw_student * raw_student, axis=1)), 'voc')]
    reduce_scatter x1 -> x0, waiting for transfers between devices: 148 us -> none  [local(): lax.psum_scatter(jnp.dot(logit_grad, student_head, preferred_element_type...]
    all_to_all x0 -> x4, waiting for transfers between devices: none -> 90.6 us  [the longest x2 74.7 us: spread(): lax.all_to_all(jnp.broadcast_to(value[None], (count, *value.shape)), axes...]
    unnamed x1 -> x0, blocking collectives: 74.7 us -> none
    all_to_all x0 -> x2, blocking collectives: none -> 38 us  [the longest x1 24.5 us: local(): got = lax.all_to_all(sent, VOC, 0, 0)]
    all_to_all x0 -> x4, starting transfers between devices: none -> 35.7 us  [the longest x2 27.2 us: spread(): lax.all_to_all(jnp.broadcast_to(value[None], (count, *value.shape)), axes...]
  transfers between devices with their start and end apart: 5 -> 8, of which waited for: 5 -> 4; matrix products, arithmetic and copies ran while one was open for 2% -> 14% of each run, Pallas kernels for 0% -> 0%
where the time goes in v1:
time: 225 us
  waiting for transfers between devices  90.6 us (40%)
  matrix products  39.9 us (18%)
  blocking collectives  38 us (17%)
  starting transfers between devices  36.9 us (16%)
  local copies, waits for them, and re-layouts  13 us (6%)
  other arithmetic  5.22 us (2%)
    all_to_all x2, waiting for transfers between devices, spread(): lax.all_to_all(jnp.broadcast_to(value[None], (count, *value.shape)), axes...  74.7 us
    all_to_all x2, starting transfers between devices, spread(): lax.all_to_all(jnp.broadcast_to(value[None], (count, *value.shape)), axes...  27.2 us
    all_to_all x1, blocking collectives, local(): got = lax.all_to_all(sent, VOC, 0, 0)  24.5 us
    dot_general x4, matrix products, dot_t(): lax.dot_general(left, right, (((1,), (1,)), ((), ())), preferred_element_...  17.9 us
    all_to_all x1, blocking collectives, spread(): lax.all_to_all(jnp.broadcast_to(value[None], (count, *value.shape)), axes...  13.5 us
    dot_general x2, matrix products, dot_0(): lax.dot_general(left, right, (((0,), (0,)), ((), ())), preferred_element_...  12.9 us
    all_to_all x1, waiting for transfers between devices, local(): lax.all_to_all(terms.reshape(row_count, rows, student_width), ROW, 0, 0)  12.1 us
    all_to_all x1, starting transfers between devices, local(): last = jnp.sum(lax.all_to_all(last, VOC, 0, 0).astype(f32), axis=0)  4.9 us
  transfers between devices with their start and end apart: 8, of which 4 were waited for; matrix products, arithmetic and copies ran while one was open for 14% of the time, Pallas kernels for 0%

profile of v1, /device:TPU:32, one launch (start us, length us, event | category | flops | bytes accessed | tf_op | source)
XLA Modules:
  0.0 224.6 jit_solution(2690797093353486486)
XLA Ops:
  0.7 0.8 reshape.222
  1.5 0.8 fusion.25
  2.3 1.0 convolution_convert_fusion
  3.3 0.1 reshape.220
  3.4 0.8 reshape.221
  4.2 0.7 concatenate.37
  4.9 0.7 concatenate.36
  5.8 0.9 concatenate.40
  6.6 24.5 %all_to_all.30 = bf16[16,2,5728]{2,1,0:T(2,128)(2,1)S(1)} all-to-all(bf16[16,2,5728]{2,1,0:T(2,128)(2,1)S(1)} %concatenate.40), channel_id=1, replica_groups=mesh['c'=2,'x'=4,'yl'=2,'yh'=2,'z'=8] {'yh','z'}, dimensions={0} | all-to-all | bytes 733184 | tf_op jit(solution)/shard_map/all_to_all | solution.py:81
  31.1 0.2 convert_reduce_fusion.1
  31.5 0.2 multiply_reduce_fusion.4
  31.8 0.2 fusion.30
  32.1 0.1 reshape.225
  32.2 0.1 convert_reduce_fusion.3
  32.5 0.2 multiply_reduce_fusion.3
  33.0 0.1 broadcast_in_dim.13
  33.1 13.5 %all_to_all.31 = bf16[8,2,8192]{2,1,0:T(2,128)(2,1)S(1)} all-to-all(bf16[8,2,8192]{2,1,0:T(2,128)(2,1)S(1)} %broadcast_in_dim.13), channel_id=1, replica_groups=mesh['c'=2,'x'=4,'yl'=2,'yh'=2,'z'=8] {'z'}, dimensions={0} | all-to-all | bytes 524288 | tf_op jit(solution)/shard_map/all_to_all | solution.py:23
  46.8 2.4 %broadcast_in_dim.15 = bf16[16,16,8192]{2,1,0:T(8,128)(2,1)} broadcast(bf16[16,8192]{1,0:T(8,128)(2,1)S(1)} %broadcast_in_dim.14), dimensions={1,2} | broadcast | bytes 4456448 | tf_op jit(solution)/shard_map/broadcast_in_dim | solution.py:23
  49.2 5.6 %all-to-all-start.2 = ((bf16[16,16,8192]{2,1,0:T(8,128)(2,1)}), bf16[16,16,8192]{2,1,0:T(8,128)(2,1)}, u32[]{:S(2)}, u32[]{:S(2)}) async-start(bf16[16,16,8192]{2,1,0:T(8,128)(2,1)} %broadcast_in_dim.15), calls=%async_computation.2 | async-start | bytes 8388608 | tf_op jit(solution)/shard_map/all_to_all | solution.py:23
  54.9 0.5 collective-permute-start.1
  55.4 56.6 %all-to-all-done.2 = bf16[16,16,8192]{2,1,0:T(8,128)(2,1)} async-done(((bf16[16,16,8192]{2,1,0:T(8,128)(2,1)}), bf16[16,16,8192]{2,1,0:T(8,128)(2,1)}, u32[]{:S(2)}, u32[]{:S(2)}) %all-to-all-start.2) | async-done | bytes 4194336 | tf_op jit(solution)/shard_map/all_to_all | solution.py:23
  112.0 3.7 %fusion.5 = f32[256,512]{1,0:T(8,128)S(1)} fusion(bf16[512,3584]{1,0:T(8,128)(2,1)} %param.18, bf16[256,8192]{1,0:T(8,128)(2,1)} %bitcast.3), kind=kOutput, calls=%fused_computation.11 | convolution fusion | flops 939655168 | bytes 6029312 | tf_op jit(solution)/shard_map/dot_general | solution.py:32
  115.8 3.9 %fusion.6 = f32[256,512]{1,0:T(8,128)S(1)} fusion(bf16[512,3584]{1,0:T(8,128)(2,1)} %collective-permute-done.1, bf16[256,8192]{1,0:T(8,128)(2,1)} %bitcast.3), kind=kOutput, calls=%fused_computation.12 | convolution fusion | flops 939655168 | bytes 6029312 | tf_op jit(solution)/shard_map/dot_general | solution.py:32
  119.7 5.4 %exponential_reduce_fusion.3 = (f32[256]{0:T(256)S(1)}, f32[256]{0:T(256)S(1)}, f32[256]{0:T(256)S(1)}, f32[256,512]{1,0:T(8,128)}) fusion(f32[256,512]{1,0:T(8,128)S(1)} %fusion.5, bf16[512,4608]{1,0:T(8,128)(2,1)} %param.15, bf16[256,8192]{1,0:T(8,128)(2,1)} %bitcast.3), kind=kOutput, calls=%fused_computation.28 | convolution fusion | flops 1209007360 | bytes 8129536 | tf_op jit(solution)/shard_map/dot_general | solution.py:32
  125.1 4.8 %exponential_reduce_fusion.2 = (f32[256]{0:T(256)S(1)}, f32[256]{0:T(256)S(1)}, f32[256]{0:T(256)S(1)}, f32[256,512]{1,0:T(8,128)S(1)}) fusion(f32[256,512]{1,0:T(8,128)S(1)} %fusion.6, bf16[512,4608]{1,0:T(8,128)(2,1)} %collective-permute-done, bf16[256,8192]{1,0:T(8,128)(2,1)} %bitcast.3), kind=kOutput, calls=%fused_computation.27 | convolution fusion | flops 1209007360 | bytes 8129536 | tf_op jit(solution)/shard_map/dot_general | solution.py:32
  129.9 0.8 broadcast_in_dim.16
  130.8 21.6 %all-to-all-start.3 = ((f32[128,6,128]{2,1,0:T(8,128)}), f32[128,6,128]{2,1,0:T(8,128)S(1)}, u32[]{:S(2)}, u32[]{:S(2)}) async-start(f32[128,6,128]{2,1,0:T(8,128)} %broadcast_in_dim.16), calls=%async_computation.3 | async-start | bytes 1048576 | tf_op jit(solution)/shard_map/all_to_all | solution.py:23
  152.5 18.2 %all-to-all-done.3 = f32[128,6,128]{2,1,0:T(8,128)S(1)} async-done(((f32[128,6,128]{2,1,0:T(8,128)}), f32[128,6,128]{2,1,0:T(8,128)S(1)}, u32[]{:S(2)}, u32[]{:S(2)}) %all-to-all-start.3) | async-done | bytes 393248 | tf_op jit(solution)/shard_map/all_to_all | solution.py:23
  170.7 0.1 reduce_sum.182
  170.8 3.6 %fusion.40 = f32[256,3584]{1,0:T(8,128)S(1)} fusion(bf16[512,3584]{1,0:T(8,128)(2,1)} %param.18, f32[256,512]{1,0:T(8,128)} %copy-done.2, f32[256,512]{1,0:T(8,128)} %get-tuple-element.24, f32[256]{0:T(256)S(1)} %get-tuple-element.14, f32[256]{0:T(256)S(1)} %get-tuple-element.13, f32[256]{0:T(256)S(1)} %dynamic_slice.14), kind=kOutput, calls=%fused_computation.80 | convolution fusion | flops 940703744 | bytes 8391680 | tf_op jit(solution)/shard_map/dot_general | solution.py:143
  174.5 0.3 multiply_convert_fusion
  174.8 4.6 %fusion = bf16[256,3584]{1,0:T(8,128)(2,1)} fusion(f32[256,3584]{1,0:T(8,128)S(1)} %fusion.40, bf16[256,512]{1,0:T(8,128)(2,1)S(1)} %multiply_convert_fusion, bf16[512,3584]{1,0:T(8,128)(2,1)} %collective-permute-done.1), kind=kOutput, calls=%fused_computation.3 | convolution fusion | flops 941359104 | bytes 9437184 | tf_op jit(solution)/shard_map/dot_general | solution.py:144
  179.3 3.6 %all-to-all-start.4 = ((bf16[8,32,3584]{2,1,0:T(8,128)(2,1)}), bf16[8,32,3584]{2,1,0:T(8,128)(2,1)S(1)}, u32[]{:S(2)}, u32[]{:S(2)}) async-start(bf16[8,32,3584]{2,1,0:T(8,128)(2,1)} %bitcast.13), calls=%async_computation.4 | async-start | bytes 3670016 | tf_op jit(solution)/shard_map/all_to_all | solution.py:146
  182.9 2.9 %slice.66 = bf16[256,3584]{1,0:T(8,128)(2,1)} slice(bf16[256,8192]{1,0:T(8,128)(2,1)} %bitcast.3), slice={[0:256], [4608:8192]} | slice | bytes 3670016 | tf_op jit(solution)/shard_map/slice | solution.py:105
  186.0 0.6 collective-permute-start.2
  186.6 0.6 dynamic_slice.12
  187.2 6.2 %fusion.36 = f32[512,3584]{1,0:T(8,128)} fusion(bf16[256,8192]{1,0:T(8,128)(2,1)} %bitcast.3, f32[256,512]{1,0:T(8,128)} %copy-done.2, f32[256,512]{1,0:T(8,128)} %get-tuple-element.24, f32[256]{0:T(256)S(1)} %get-tuple-element.14, f32[256]{0:T(256)S(1)} %get-tuple-element.13, f32[256]{0:T(256)S(1)} %dynamic_slice.14), kind=kOutput, calls=%fused_computation.76 | convolution fusion | flops 940703744 | bytes 10226688 | tf_op jit(solution)/shard_map/dot_general | solution.py:36
  193.4 12.1 %all-to-all-done.4 = bf16[8,32,3584]{2,1,0:T(8,128)(2,1)S(1)} async-done(((bf16[8,32,3584]{2,1,0:T(8,128)(2,1)}), bf16[8,32,3584]{2,1,0:T(8,128)(2,1)S(1)}, u32[]{:S(2)}, u32[]{:S(2)}) %all-to-all-start.4) | async-done | bytes 1835040 | tf_op jit(solution)/shard_map/all_to_all | solution.py:146
  205.4 0.3 convert_reduce_fusion
  205.7 1.1 fusion.41
  206.9 0.4 convert_element_type.162
  207.3 0.1 pad_maximum_fusion
  207.4 0.8 copy.35
  208.2 4.9 %all-to-all-start.5 = ((bf16[16,32,226]{2,1,0:T(8,128)(2,1)}), bf16[16,32,226]{2,1,0:T(8,128)(2,1)S(1)}, u32[]{:S(2)}, u32[]{:S(2)}) async-start(bf16[16,32,226]{2,1,0:T(8,128)(2,1)} %copy.35), calls=%async_computation.5 | async-start | bytes 524288 | tf_op jit(solution)/shard_map/all_to_all | solution.py:158
  213.1 6.7 %add_convert_fusion = bf16[512,3584]{1,0:T(8,128)(2,1)} fusion(f32[512,3584]{1,0:T(8,128)} %fusion.36, bf16[256,512]{1,0:T(8,128)(2,1)} %collective-permute-done.2, bf16[256,3584]{1,0:T(8,128)(2,1)} %collective-permute-done.3), kind=kOutput, calls=%fused_computation | convolution fusion | flops 943194112 | bytes 13107200 | tf_op jit(solution)/shard_map/dot_general | solution.py:36
  219.8 3.8 %all-to-all-done.5 = bf16[16,32,226]{2,1,0:T(8,128)(2,1)S(1)} async-done(((bf16[16,32,226]{2,1,0:T(8,128)(2,1)}), bf16[16,32,226]{2,1,0:T(8,128)(2,1)S(1)}, u32[]{:S(2)}, u32[]{:S(2)}) %all-to-all-start.5) | async-done | bytes 231456 | tf_op jit(solution)/shard_map/all_to_all | solution.py:158
  223.7 0.2 slice_reduce_fusion
  223.9 0.7 fusion.29
  (51 shorter events, 1.7 us)
Async XLA Ops:
  0.6 1.7 copy-start
  0.6 32.1 %copy-start.4 = (f32[3584]{0:T(1024)S(1)}, f32[3584]{0:T(1024)}, u32[]{:S(2)}) copy-start(f32[3584]{0:T(1024)} %param.17) | copy-start | bytes 43012
  49.2 62.8 %all-to-all-start.2 = ((bf16[16,16,8192]{2,1,0:T(8,128)(2,1)}), bf16[16,16,8192]{2,1,0:T(8,128)(2,1)}, u32[]{:S(2)}, u32[]{:S(2)}) async-start(bf16[16,16,8192]{2,1,0:T(8,128)(2,1)} %broadcast_in_dim.15), calls=%async_computation.2 | async-start | bytes 8388608 | tf_op jit(solution)/shard_map/all_to_all | solution.py:23
  54.8 70.3 %collective-permute-start = (bf16[512,4608]{1,0:T(8,128)(2,1)}, bf16[512,4608]{1,0:T(8,128)(2,1)}, u32[]{:S(2)}, u32[]{:S(2)}) collective-permute-start(bf16[512,4608]{1,0:T(8,128)(2,1)} %param.15), channel_id=1, source_target_pairs={{0,128},{128,0},{1,129},{129,1},{2,130},{130,2},{3,131},{131,3},{4... | collective-permute-start | bytes 14155784 | tf_op jit(solution)/shard_map/ppermute | solution.py:18
  54.9 60.8 %collective-permute-start.1 = (bf16[512,3584]{1,0:T(8,128)(2,1)}, bf16[512,3584]{1,0:T(8,128)(2,1)}, u32[]{:S(2)}, u32[]{:S(2)}) collective-permute-start(bf16[512,3584]{1,0:T(8,128)(2,1)} %param.18), channel_id=1, source_target_pairs={{0,128},{128,0},{1,129},{129,1},{2,130},{130,2},{3,131},{131,3},{4... | collective-permute-start | bytes 11010056 | tf_op jit(solution)/shard_map/ppermute | solution.py:18
  115.7 4.0 %copy-start.2 = (f32[256,512]{1,0:T(8,128)}, f32[256,512]{1,0:T(8,128)S(1)}, u32[]{:S(2)}) copy-start(f32[256,512]{1,0:T(8,128)S(1)} %fusion.5) | copy-start | bytes 1572868
  125.1 27.3 %copy-start.5 = (f32[512]{0:T(512)S(1)}, f32[512]{0:T(512)}, u32[]{:S(2)}) copy-start(f32[512]{0:T(512)} %param.19) | copy-start | bytes 6148
  130.8 39.9 %all-to-all-start.3 = ((f32[128,6,128]{2,1,0:T(8,128)}), f32[128,6,128]{2,1,0:T(8,128)S(1)}, u32[]{:S(2)}, u32[]{:S(2)}) async-start(f32[128,6,128]{2,1,0:T(8,128)} %broadcast_in_dim.16), calls=%async_computation.3 | async-start | bytes 1048576 | tf_op jit(solution)/shard_map/all_to_all | solution.py:23
  174.8 4.6 %copy-start.1 = (bf16[256,512]{1,0:T(8,128)(2,1)}, bf16[256,512]{1,0:T(8,128)(2,1)S(1)}, u32[]{:S(2)}) copy-start(bf16[256,512]{1,0:T(8,128)(2,1)S(1)} %multiply_convert_fusion) | copy-start | bytes 786436
  179.3 26.1 %all-to-all-start.4 = ((bf16[8,32,3584]{2,1,0:T(8,128)(2,1)}), bf16[8,32,3584]{2,1,0:T(8,128)(2,1)S(1)}, u32[]{:S(2)}, u32[]{:S(2)}) async-start(bf16[8,32,3584]{2,1,0:T(8,128)(2,1)} %bitcast.13), calls=%async_computation.4 | async-start | bytes 3670016 | tf_op jit(solution)/shard_map/all_to_all | solution.py:146
  185.8 27.3 %collective-permute-start.3 = (bf16[256,3584]{1,0:T(8,128)(2,1)}, bf16[256,3584]{1,0:T(8,128)(2,1)}, u32[]{:S(2)}, u32[]{:S(2)}) collective-permute-start(bf16[256,3584]{1,0:T(8,128)(2,1)} %slice.66), channel_id=1, source_target_pairs={{0,128},{128,0},{1,129},{129,1},{2,130},{130,2},{3,131},{131,3},{4... | collective-permute-start | bytes 5505032 | tf_op jit(solution)/shard_map/ppermute | solution.py:18
  186.0 27.1 %collective-permute-start.2 = (bf16[256,512]{1,0:T(8,128)(2,1)}, bf16[256,512]{1,0:T(8,128)(2,1)}, u32[]{:S(2)}, u32[]{:S(2)}) collective-permute-start(bf16[256,512]{1,0:T(8,128)(2,1)} %copy-done.1), channel_id=1, source_target_pairs={{0,128},{128,0},{1,129},{129,1},{2,130},{130,2},{3,131},{131,3},{4... | collective-permute-start | bytes 786440 | tf_op jit(solution)/shard_map/ppermute | solution.py:18
  208.2 15.5 %all-to-all-start.5 = ((bf16[16,32,226]{2,1,0:T(8,128)(2,1)}), bf16[16,32,226]{2,1,0:T(8,128)(2,1)S(1)}, u32[]{:S(2)}, u32[]{:S(2)}) async-start(bf16[16,32,226]{2,1,0:T(8,128)(2,1)} %copy.35), calls=%async_computation.5 | async-start | bytes 524288 | tf_op jit(solution)/shard_map/all_to_all | solution.py:158
  213.1 10.8 %copy-start.3 = (bf16[32,224]{1,0:T(8,128)(2,1)S(1)}, bf16[32,224]{1,0:T(8,128)(2,1)}, u32[]{:S(2)}) copy-start(bf16[32,224]{1,0:T(8,128)(2,1)} %param.16) | copy-start | bytes 43012

commit v2 on v1

v2 whole, which is shorter than its diff:
```python
import functools

import jax
import jax.numpy as jnp
from jax import lax
from jax.experimental import pallas as pl
from jax.experimental.pallas import tpu as pltpu
from jax.sharding import Mesh
from jax.sharding import PartitionSpec as P

epsilon = 1e-06
softcap = 30.0
ROW = ("x", "yl")
VOC = ("yh", "z")
XY = ("x", "yl", "yh")
bf16 = jnp.bfloat16
f32 = jnp.float32


def swap(value):
    return lax.ppermute(value, "c", [(0, 1), (1, 0)])


def spread(value, axes):
    count = lax.axis_size(axes)
    return lax.all_to_all(jnp.broadcast_to(value[None], (count, *value.shape)), axes, 0, 0)


def ring_step(right, left):
    count = lax.axis_size("z")
    return (
        lax.ppermute(right, "z", [(i, (i + 1) % count) for i in range(count)]),
        lax.ppermute(left, "z", [(i, (i - 1) % count) for i in range(count)]),
    )


def halves(value):
    high = lax.reduce_precision(value, 8, 7)
    return high.astype(bf16), (value - high).astype(bf16)


def dot_t(left, right):
    return lax.dot_general(left, right, (((1,), (1,)), ((), ())), preferred_element_type=f32)


def rows_kernel(cols, got, out):
    count, own, _ = got.shape
    width = out.shape[2]
    attention = jnp.zeros((own, width), f32)
    residual, post, final = [], [], []
    for i in range(count):
        attention += got[i, :, :width].astype(f32)
        rest = got[i, :, width:].astype(f32)
        residual.append(rest[:, :cols])
        gains = jnp.sum(rest[:, cols : 3 * cols], axis=0, keepdims=True)
        post.append(gains[:, :cols])
        final.append(gains[:, cols:])
    post_scale = lax.rsqrt(jnp.mean(attention * attention, axis=1, keepdims=True) + epsilon)
    hidden = jnp.concatenate(residual, axis=1) + attention * post_scale * jnp.concatenate(post, axis=1)
    final_scale = lax.rsqrt(jnp.mean(hidden * hidden, axis=1, keepdims=True) + epsilon)
    normed = (hidden * final_scale * jnp.concatenate(final, axis=1)).astype(bf16)
    for i in range(count):
        out[i] = normed


def own_rows(got, width, cols):
    vmem = pl.BlockSpec(memory_space=pltpu.VMEM)
    count, own, _ = got.shape
    return pl.pallas_call(
        functools.partial(rows_kernel, cols),
        out_shape=jax.ShapeDtypeStruct((count, own, width), bf16),
        in_specs=[vmem],
        out_specs=vmem,
        compiler_params=pltpu.CompilerParams(vmem_limit_bytes=56 * 2**20),
        cost_estimate=pl.CostEstimate(flops=got.size, bytes_accessed=4 * got.size, transcendentals=0),
    )(got)


def student_kernel(own_rows_count, gain, *refs):
    blocks = refs[:9]
    (own_head, other_head, normed_out, scale, own_tanh, other_tanh, sums) = refs[9:16]
    pieces, normed, held, tanhs, block_sem, sem = refs[16:]
    z_count, piece_rows, cols = pieces.shape
    z_index = lax.axis_index("z")
    copies = []
    for k, offset in enumerate((0, -1, 1, -2, 2, -3, 3, 4, 4)):
        place = pieces.at[lax.rem(z_index + (offset + z_count), z_count)]
        if k >= 7:
            place = place.at[pl.ds((k - 7) * (piece_rows // 2), piece_rows // 2)]
        copies.append(pltpu.make_async_copy(blocks[k], place, block_sem.at[k]))
        copies[k].start()
    chunk = held.shape[1]
    each = own_head.shape[0] // chunk
    heads = []
    for i in range(2 * each):
        head = own_head if i < each else other_head
        heads.append(
            pltpu.make_async_copy(head.at[pl.ds((i % each) * chunk, chunk)], held.at[i], sem.at[0, i])
        )
    for copy in copies:
        copy.wait()
    for copy in heads:
        copy.start()
    tokens, width = normed.shape
    highs = width // (z_count * cols)
    rows = own_rows_count
    for r in range(tokens // rows):
        raw = jnp.concatenate(
            [
                pieces[z, (r * highs + h) * rows : (r * highs + h + 1) * rows, :].astype(f32)
                for h in range(highs)
                for z in range(z_count)
            ],
            axis=1,
        )
        part_scale = lax.rsqrt(jnp.mean(raw * raw, axis=1, keepdims=True) + epsilon)
        part = pl.ds(r * rows, rows)
        scale[part, :] = part_scale
        normed[part, :] = (raw * part_scale * gain[...]).astype(bf16)
    stores = [pltpu.make_async_copy(normed, normed_out, sem.at[1, 2 * each])]
    stores[0].start()
    total = jnp.zeros((1, tokens), f32)
    for i in range(2 * each):
        part = pl.ds((i % each) * chunk, chunk)
        heads[i].wait()
        student = jnp.tanh(dot_t(held[i], normed[...]) * (1.0 / softcap))
        tanhs[i] = student
        out = own_tanh if i < each else other_tanh
        stores.append(pltpu.make_async_copy(tanhs.at[i], out.at[part], sem.at[1, i]))
        stores[-1].start()
        total += jnp.sum(jnp.exp(softcap * student), axis=0, keepdims=True)
    sums[...] = total
    for store in stores:
        store.wait()


def student_logits(rows, gain, blocks, own_head, other_head):
    count, width = own_head.shape
    piece_rows, cols = blocks[0].shape
    z_count = lax.axis_size("z")
    tokens = piece_rows * cols * z_count // width
    chunk = count // 2
    vmem = pl.BlockSpec(memory_space=pltpu.VMEM)
    anywhere = pl.BlockSpec(memory_space=pl.ANY)
    return pl.pallas_call(
        functools.partial(student_kernel, rows),
        out_shape=(
            jax.ShapeDtypeStruct((tokens, width), bf16),
            jax.ShapeDtypeStruct((tokens, 1), f32),
            jax.ShapeDtypeStruct((count, tokens), f32),
            jax.ShapeDtypeStruct((count, tokens), f32),
            jax.ShapeDtypeStruct((1, tokens), f32),
        ),
        in_specs=[vmem] + [anywhere] * 11,
        out_specs=(anywhere, vmem, anywhere, anywhere, vmem),
        scratch_shapes=[
            pltpu.VMEM((z_count, piece_rows, cols), bf16),
            pltpu.VMEM((tokens, width), bf16),
            pltpu.VMEM((4, chunk, width), bf16),
            pltpu.VMEM((4, chunk, tokens), f32),
            pltpu.SemaphoreType.DMA((9,)),
            pltpu.SemaphoreType.DMA((2, 5)),
        ],
        compiler_params=pltpu.CompilerParams(vmem_limit_bytes=56 * 2**20),
        cost_estimate=pl.CostEstimate(
            flops=4 * count * tokens * width,
            bytes_accessed=4 * count * width,
            transcendentals=4 * count * tokens,
        ),
    )(gain, *blocks, own_head, other_head)


def teacher_kernel(rows, own_head, other_head, own_tanh, other_tanh, own_exp, other_exp, sums):
    total = jnp.zeros((1, rows.shape[0]), f32)
    mixed = jnp.zeros((1, rows.shape[0]), f32)
    for head, tanh, out in ((own_head, own_tanh, own_exp), (other_head, other_tanh, other_exp)):
        logit = softcap * jnp.tanh(dot_t(rows[...], head[...]).T * (1.0 / softcap))
        grown = jnp.exp(logit)
        out[...] = grown
        total += jnp.sum(grown, axis=0, keepdims=True)
        mixed += jnp.sum(grown * (logit - softcap * tanh[...]), axis=0, keepdims=True)
    sums[...] = jnp.concatenate([total, mixed], axis=0)


def teacher_logits(rows, own_head, other_head, own_tanh, other_tanh):
    count, width = own_head.shape
    tokens = rows.shape[0]
    vmem = pl.BlockSpec(memory_space=pltpu.VMEM)
    return pl.pallas_call(
        teacher_kernel,
        out_shape=(
            jax.ShapeDtypeStruct((count, tokens), f32),
            jax.ShapeDtypeStruct((count, tokens), f32),
            jax.ShapeDtypeStruct((2, tokens), f32),
        ),
        in_specs=[vmem] * 5,
        out_specs=(vmem, vmem, vmem),
        compiler_params=pltpu.CompilerParams(vmem_limit_bytes=12 * 2**20),
        cost_estimate=pl.CostEstimate(
            flops=4 * count * tokens * width,
            bytes_accessed=4 * count * width,
            transcendentals=4 * count * tokens,
        ),
    )(rows, own_head, other_head, own_tanh, other_tanh)


def gradient_kernel(
    own_exp, other_exp, own_tanh, other_tanh, scales, own_head, other_head,
    own_grad, other_grad, terms, held, turned, sem,
):
    count = own_exp.shape[0]
    chunks, _, block = held.shape
    copies = []
    for i in range(chunks):
        columns = pl.ds(i * block, block)
        for j, head in enumerate((own_head, other_head)):
            copies.append(
                pltpu.make_async_copy(
                    head.at[:, columns], held.at[i, pl.ds(j * count, count)], sem.at[i, j]
                )
            )
            copies[-1].start()
    for start, exps, tanhs, grads in (
        (0, own_exp, own_tanh, own_grad),
        (count, other_exp, other_tanh, other_grad),
    ):
        student = tanhs[...]
        grad = (jnp.exp(softcap * student) * scales[0:1, :] - exps[...] * scales[1:2, :]) * (
            1.0 - student * student
        )
        grads[...] = grad.astype(bf16)
        turned[:, pl.ds(start, count)] = grad.T.astype(bf16)
    for i in range(chunks):
        copies[2 * i].wait()
        copies[2 * i + 1].wait()
        terms[:, pl.ds(i * block, block)] = jnp.dot(
            turned[...], held[i], preferred_element_type=f32
        ).astype(bf16)


def gradient_terms(own_exp, other_exp, own_tanh, other_tanh, scales, own_head, other_head):
    count, tokens = own_exp.shape
    width = own_head.shape[1]
    block = 512
    vmem = pl.BlockSpec(memory_space=pltpu.VMEM)
    anywhere = pl.BlockSpec(memory_space=pl.ANY)
    return pl.pallas_call(
        gradient_kernel,
        out_shape=(
            jax.ShapeDtypeStruct((count, tokens), bf16),
            jax.ShapeDtypeStruct((count, tokens), bf16),
            jax.ShapeDtypeStruct((tokens, width), bf16),
        ),
        in_specs=[vmem] * 5 + [anywhere] * 2,
        out_specs=(vmem, vmem, vmem),
        scratch_shapes=[
            pltpu.VMEM((width // block, 2 * count, block), bf16),
            pltpu.VMEM((tokens, 2 * count), bf16),
            pltpu.SemaphoreType.DMA((width // block, 2)),
        ],
        compiler_params=pltpu.CompilerParams(vmem_limit_bytes=56 * 2**20),
        cost_estimate=pl.CostEstimate(
            flops=4 * count * tokens * width,
            bytes_accessed=4 * count * width + 20 * count * tokens,
            transcendentals=2 * count * tokens,
        ),
    )(own_exp, other_exp, own_tanh, other_tanh, scales, own_head, other_head)


def reduced_kernel(parts, normed, out):
    total = parts[0].astype(f32)
    for i in range(1, parts.shape[0]):
        total += parts[i].astype(f32)
    inner = jnp.sum(normed[...].astype(f32) * total, axis=1, keepdims=True)
    high = inner.astype(bf16).astype(f32)
    count, rows, width = out.shape
    cols = total.shape[1] // count
    lane = lax.broadcasted_iota(jnp.int32, (rows, width - cols), 1)
    behind = jnp.where(lane == 0, high, jnp.where(lane == 1, inner - high, 0.0))
    for i in range(count):
        piece = jnp.concatenate([total[:, i * cols : (i + 1) * cols], behind], axis=1)
        out[i] = piece.astype(bf16)


def reduced_pieces(parts, normed, count, width):
    rows = normed.shape[0]
    vmem = pl.BlockSpec(memory_space=pltpu.VMEM)
    return pl.pallas_call(
        reduced_kernel,
        out_shape=jax.ShapeDtypeStruct((count, rows, width), bf16),
        in_specs=[vmem, vmem],
        out_specs=vmem,
        compiler_params=pltpu.CompilerParams(vmem_limit_bytes=56 * 2**20),
        cost_estimate=pl.CostEstimate(
            flops=parts.size, bytes_accessed=2 * parts.size, transcendentals=0
        ),
    )(parts, normed)


def local(
    context,
    residual_in,
    out_proj,
    post_gain,
    final_gain,
    teacher_head,
    student_hidden,
    student_gain,
    student_head,
    kl_weight,
):
    voc_count = lax.axis_size(VOC)
    row_count = lax.axis_size(ROW)
    rows = context.shape[0]
    teacher_cols = residual_in.shape[1]
    student_cols = student_hidden.shape[1]
    teacher_width = teacher_cols * voc_count
    student_width = student_cols * voc_count
    own = rows // voc_count
    half = rows * row_count
    voc_index = lax.axis_index(VOC)
    row_index = lax.axis_index(ROW)
    half_start = lax.axis_index("c") * half

    teacher_other = swap(teacher_head)
    student_other = swap(student_head)

    pieces = spread(student_hidden, XY).reshape(-1, student_cols)

    partial = jnp.dot(context, out_proj, preferred_element_type=f32).astype(bf16)
    raw_student = student_hidden.astype(f32)
    gains = jnp.stack(halves(jnp.concatenate([post_gain, final_gain])))
    sent = jnp.concatenate(
        [
            partial.reshape(voc_count, own, teacher_width),
            residual_in.reshape(voc_count, own, teacher_cols),
            jnp.broadcast_to(gains[None], (voc_count, *gains.shape)),
        ],
        axis=2,
    )
    got = lax.all_to_all(sent, VOC, 0, 0)
    teacher_rows = own_rows(got, teacher_width, teacher_cols)
    teacher_rows, pieces = lax.optimization_barrier((teacher_rows, pieces))
    right, left = ring_step(pieces, pieces)
    ring = [pieces, right, left]
    teacher_rows = lax.all_to_all(teacher_rows, VOC, 0, 0).reshape(rows, teacher_width)
    teacher_rows, right, left = lax.optimization_barrier((teacher_rows, right, left))
    right, left = ring_step(right, left)
    ring += [right, left]
    right, left = ring_step(right, left)
    ring += [right, left]
    cut = pieces.shape[0] // 2
    right, left = ring_step(right[:cut], left[cut:])
    ring += [right, left]
    teacher_all = spread(teacher_rows, ROW).reshape(half, teacher_width)

    student_all, student_scale, tanh_mine, tanh_others, student_sum = student_logits(
        rows, student_gain[None], ring, student_head, student_other
    )
    own_scale = lax.dynamic_slice_in_dim(student_scale[:, 0], row_index * rows, rows)
    exp_mine, exp_others, teacher_sums = teacher_logits(
        teacher_all, teacher_head, teacher_other, tanh_mine, tanh_others
    )
    sums = jnp.concatenate([teacher_sums, student_sum]).reshape(-1, 128)
    sums = jnp.sum(spread(sums, XY), axis=0)
    sums, student_tied = lax.optimization_barrier((sums, student_all))
    student_all_other = swap(student_tied)
    totals = jnp.sum(spread(sums, "z"), axis=0).reshape(3, half)
    teacher_total, mixed, student_total = totals[0], totals[1], totals[2]
    token_kl = mixed / teacher_total + jnp.log(student_total) - jnp.log(teacher_total)
    token_kl = lax.dynamic_slice_in_dim(token_kl, row_index * rows + voc_index * own, own)
    weight = lax.dynamic_slice_in_dim(kl_weight, half_start, half)
    scales = jnp.stack([weight / student_total, weight / teacher_total])

    grad_mine, grad_others, terms = gradient_terms(
        exp_mine, exp_others, tanh_mine, tanh_others, scales, student_head, student_other
    )
    grad_back = swap(grad_others)
    parts = lax.all_to_all(terms.reshape(row_count, rows, student_width), ROW, 0, 0)
    grad_head = (
        jnp.dot(grad_mine, student_all, preferred_element_type=f32)
        + jnp.dot(grad_back, student_all_other, preferred_element_type=f32)
    ).astype(bf16)
    own_normed = lax.dynamic_slice_in_dim(student_all, row_index * rows, rows)
    last = reduced_pieces(parts, own_normed, voc_count, 256)
    last = jnp.sum(lax.all_to_all(last, VOC, 0, 0).astype(f32), axis=0)
    grad_normed = last[:, :student_cols]
    inner_total = (last[:, student_cols] + last[:, student_cols + 1]) / own_scale
    gain_piece = lax.dynamic_slice_in_dim(student_gain, voc_index * student_cols, student_cols)
    cubed = own_scale * own_scale * own_scale
    grad_hidden = (
        own_scale[:, None] * gain_piece * grad_normed
        - raw_student * cubed[:, None] * inner_total[:, None] / student_width
    ).astype(bf16)
    return (token_kl, grad_hidden, grad_head)


def solution(mesh):
    sec, tok, voc = mesh.devices.shape
    fine = Mesh(mesh.devices.reshape(sec, tok // 2, 2, 2, voc // 2), ("c", "x", "yl", "yh", "z"))
    row = ("c", "x", "yl")
    every = ("c", "x", "yl", "yh", "z")
    return jax.shard_map(
        local,
        mesh=fine,
        in_specs=(
            P(row, VOC),
            P(row, VOC),
            P(VOC, None),
            P(VOC),
            P(VOC),
            P(every, None),
            P(row, VOC),
            P(),
            P(every, None),
            P(),
        ),
        out_specs=(P(every), P(row, VOC), P(every, None)),
        check_vma=False,
    )
```

time: 225 us -> 195 us (0.87)
  waiting for transfers between devices: 90.6 us -> 56.9 us
  matrix products: 39.9 us -> 6.7 us
  Pallas kernels: 0 us -> 26.8 us
  starting transfers between devices: 36.9 us -> 42.8 us
  local copies, waits for them, and re-layouts: 13 us -> 16.9 us
    all_to_all x2 -> x3, waiting for transfers between devices: 74.7 us -> 13.4 us  [spread(): lax.all_to_all(jnp.broadcast_to(value[None], (count, *value.shape)), axes...]
    dot_general x8 -> x2, matrix products: 39 us -> 5.72 us  [the longest x1 2.96 us: local(): jnp.dot(grad_mine, student_all, preferred_element_type=f32)]
    pallas_call x0 -> x5, Pallas kernels: none -> 26.8 us  [the longest x1 9.79 us: student_logits(): pl.pallas_call(functools.partial(student_kernel, rows), out_shape=(jax.Sh...]
    ppermute x0 -> x8, waiting for transfers between devices: none -> 12 us  [the longest x4 10.5 us: ring_step(): lax.ppermute(right, 'z', [(i, (i + 1) % count) for i in range(count)])]
    ppermute x0 -> x8, starting transfers between devices: none -> 10.4 us  [the longest x4 6.92 us: ring_step(): lax.ppermute(right, 'z', [(i, (i + 1) % count) for i in range(count)])]
    all_to_all x2 -> x3, starting transfers between devices: 27.2 us -> 16.9 us  [spread(): lax.all_to_all(jnp.broadcast_to(value[None], (count, *value.shape)), axes...]
    all_to_all x0 -> x1, waiting for transfers between devices: none -> 9.2 us  [local(): lax.all_to_all(teacher_rows, VOC, 0, 0).reshape(rows, teacher_width)]
    unnamed x12 -> x46, local copies, waits for them, and re-layouts: 0.03 us -> 8.51 us
  transfers between devices with their start and end apart: 8 -> 18, of which waited for: 4 -> 11; matrix products, arithmetic and copies ran while one was open for 14% -> 8% of each run, Pallas kernels for 0% -> 11%
where the time goes in v2:
time: 195 us; the launch traced here: 194 us
  waiting for transfers between devices  56.9 us (29%)
  starting transfers between devices  42.8 us (22%)
  blocking collectives  39.7 us (20%)
  Pallas kernels  26.8 us (14%)
  local copies, waits for them, and re-layouts  16.9 us (9%)
  matrix products  6.7 us (3%)
  other arithmetic  3.17 us (2%)
    all_to_all x1, blocking collectives, local(): got = lax.all_to_all(sent, VOC, 0, 0)  24.3 us
    all_to_all x1, waiting for transfers between devices, local(): lax.all_to_all(terms.reshape(row_count, rows, student_width), ROW, 0, 0)  17.5 us
    all_to_all x3, starting transfers between devices, spread(): lax.all_to_all(jnp.broadcast_to(value[None], (count, *value.shape)), axes...  16.9 us
    all_to_all x1, blocking collectives, spread(): lax.all_to_all(jnp.broadcast_to(value[None], (count, *value.shape)), axes...  15.4 us
    all_to_all x3, waiting for transfers between devices, spread(): lax.all_to_all(jnp.broadcast_to(value[None], (count, *value.shape)), axes...  13.4 us
    ppermute x4, waiting for transfers between devices, ring_step(): lax.ppermute(right, 'z', [(i, (i + 1) % count) for i in range(count)])  10.5 us
    pallas_call x1, Pallas kernels, student_logits(): pl.pallas_call(functools.partial(student_kernel, rows), out_shape=(jax.Sh...  9.79 us
    all_to_all x1, waiting for transfers between devices, local(): lax.all_to_all(teacher_rows, VOC, 0, 0).reshape(rows, teacher_width)  9.2 us
  transfers between devices with their start and end apart: 18, of which 11 were waited for; matrix products, arithmetic and copies ran while one was open for 8% of the time, Pallas kernels for 11%

profile of v2, /device:TPU:32, one launch (start us, length us, event | category | flops | bytes accessed | tf_op | source)
XLA Modules:
  0.0 194.1 jit_solution(18272968480659414952)
XLA Ops:
  1.3 0.6 copy-done
  1.9 1.0 convolution_convert_fusion
  3.2 0.8 concatenate.33
  4.1 24.3 %all_to_all.40.got = bf16[16,2,5472]{2,1,0:T(2,128)(2,1)} all-to-all(bf16[16,2,5472]{2,1,0:T(2,128)(2,1)S(1)} %concatenate.33), channel_id=1, replica_groups=mesh['c'=2,'x'=4,'yl'=2,'yh'=2,'z'=8] {'yh','z'}, dimensions={0} | all-to-all | bytes 700416 | tf_op jit(solution)/shard_map/all_to_all | solution.py:341
  28.4 0.7 broadcast_in_dim.15
  29.1 5.7 %all-to-all-start.1 = ((bf16[16,32,224]{2,1,0:T(8,128)(2,1)}), bf16[16,32,224]{2,1,0:T(8,128)(2,1)S(1)}, u32[]{:S(2)}, u32[]{:S(2)}) async-start(bf16[16,32,224]{2,1,0:T(8,128)(2,1)} %broadcast_in_dim.15), calls=%async_computation.1 | async-start | bytes 524288 | tf_op jit(solution)/shard_map/all_to_all | solution.py:26
  34.8 2.1 %shard_map.121 = bf16[16,2,4608]{2,1,0:T(2,128)(2,1)} custom-call(bf16[16,2,5472]{2,1,0:T(2,128)(2,1)} %all_to_all.40.got), custom_call_target="tpu_custom_call" | custom-call | flops 175104 | bytes 700416 | tf_op jit(solution)/shard_map/pallas_call | solution.py:69
  36.8 6.8 %all-to-all-done.1 = bf16[16,32,224]{2,1,0:T(8,128)(2,1)S(1)} async-done(((bf16[16,32,224]{2,1,0:T(8,128)(2,1)}), bf16[16,32,224]{2,1,0:T(8,128)(2,1)S(1)}, u32[]{:S(2)}, u32[]{:S(2)}) %all-to-all-start.1) | async-done | bytes 229408 | tf_op jit(solution)/shard_map/all_to_all | solution.py:26
  43.6 3.8 %all-to-all-start.2 = ((bf16[16,2,4608]{2,1,0:T(2,128)(2,1)}), bf16[16,2,4608]{2,1,0:T(2,128)(2,1)S(1)}, u32[]{:S(2)}, u32[]{:S(2)}) async-start(bf16[16,2,4608]{2,1,0:T(2,128)(2,1)} %shard_map.121), calls=%async_computation.2 | async-start | bytes 589824 | tf_op jit(solution)/shard_map/all_to_all | solution.py:346
  47.3 1.5 collective-permute-start
  49.4 9.2 %all-to-all-done.2 = bf16[16,2,4608]{2,1,0:T(2,128)(2,1)S(1)} async-done(((bf16[16,2,4608]{2,1,0:T(2,128)(2,1)}), bf16[16,2,4608]{2,1,0:T(2,128)(2,1)S(1)}, u32[]{:S(2)}, u32[]{:S(2)}) %all-to-all-start.2) | async-done | bytes 294944 | tf_op jit(solution)/shard_map/all_to_all | solution.py:346
  59.1 1.6 broadcast_in_dim.16
  60.8 3.6 %all-to-all-start.3 = ((bf16[8,32,4608]{2,1,0:T(8,128)(2,1)}), bf16[8,32,4608]{2,1,0:T(8,128)(2,1)S(1)}, u32[]{:S(2)}, u32[]{:S(2)}) async-start(bf16[8,32,4608]{2,1,0:T(8,128)(2,1)} %broadcast_in_dim.16), calls=%async_computation.3 | async-start | bytes 4718592 | tf_op jit(solution)/shard_map/all_to_all | solution.py:26
  64.4 2.1 %collective-permute-start.3 = (bf16[512,224]{1,0:T(8,128)(2,1)}, bf16[512,224]{1,0:T(8,128)(2,1)S(1)}, u32[]{:S(2)}, u32[]{:S(2)}) collective-permute-start(bf16[512,224]{1,0:T(8,128)(2,1)} %copy-done.12), channel_id=1, source_target_pairs={{0,1},{1,2},{2,3},{3,4},{4,5},{5,6},{6,7},{7,0},{8,9},{9,10},{10,1... | collective-permute-start | bytes 688136 | tf_op jit(solution)/shard_map/ppermute | solution.py:32
  66.5 4.9 %collective-permute-done.3.refs_3_ = bf16[512,224]{1,0:T(8,128)(2,1)S(1)} collective-permute-done((bf16[512,224]{1,0:T(8,128)(2,1)}, bf16[512,224]{1,0:T(8,128)(2,1)S(1)}, u32[]{:S(2)}, u32[]{:S(2)}) %collective-permute-start.3) | collective-permute-done | bytes 229408 | tf_op jit(solution)/shard_map/ppermute | solution.py:32
  71.4 1.9 %collective-permute-start.5 = (bf16[512,224]{1,0:T(8,128)(2,1)S(1)}, bf16[512,224]{1,0:T(8,128)(2,1)S(1)}, u32[]{:S(2)}, u32[]{:S(2)}) collective-permute-start(bf16[512,224]{1,0:T(8,128)(2,1)S(1)} %collective-permute-done.3.refs_3_), channel_id=1, source_target_pairs={{0,1},{1,2},{2,3},{3,4},{4,5},{5,6},{6,7},{7,0},{8,9},{9,10},{10,1... | collective-permute-start | bytes 688136 | tf_op jit(solution)/shard_map/ppermute | solution.py:32
  73.7 0.7 collective-permute-start.6
  74.4 4.3 %collective-permute-done.5.refs_5_ = bf16[512,224]{1,0:T(8,128)(2,1)S(1)} collective-permute-done((bf16[512,224]{1,0:T(8,128)(2,1)S(1)}, bf16[512,224]{1,0:T(8,128)(2,1)S(1)}, u32[]{:S(2)}, u32[]{:S(2)}) %collective-permute-start.5) | collective-permute-done | bytes 229408 | tf_op jit(solution)/shard_map/ppermute | solution.py:32
  78.7 1.4 collective-permute-start.7
  80.2 2.2 %collective-permute-start.8 = (bf16[256,224]{1,0:T(8,128)(2,1)S(1)}, bf16[256,224]{1,0:T(8,128)(2,1)S(1)}, u32[]{:S(2)}, u32[]{:S(2)}) collective-permute-start(bf16[256,224]{1,0:T(8,128)(2,1)S(1)} %slice.36), channel_id=1, source_target_pairs={{0,7},{1,0},{2,1},{3,2},{4,3},{5,4},{6,5},{7,6},{8,15},{9,8},{10,9... | collective-permute-start | bytes 344072 | tf_op jit(solution)/shard_map/ppermute | solution.py:33
  82.3 1.3 broadcast_in_dim.17.gain
  83.6 1.3 collective-permute-done.7.refs_7_
  85.0 0.8 collective-permute-done.8.refs_8_
  86.4 9.8 %shard_map.122 = (bf16[256,3584]{1,0:T(8,128)(2,1)}, f32[256,1]{1,0:T(8,128)}, f32[512,256]{1,0:T(8,128)}, f32[512,256]{1,0:T(8,128)}, f32[1,256]{1,0:T(1,128)}) custom-call(f32[1,3584]{1,0:T(1,128)} %broadcast_in_dim.17.gain, bf16[512,224]{1,0:T(8,128)(2,1)} %bitcast.32, bf16[512,224]{1,0:T(8,128)(2,1)} %copy-done.12, bf16[512,224]{1,0:T(8,128)(2,1)} %copy-done.13, ...), custom_call_target="tpu_custom_call" | custom-call | flops 1879048192 | bytes 7340032 | tf_op jit(solution)/shard_map/pallas_call | solution.py:145
  96.2 2.3 %copy-done.1 = bf16[512,4608]{1,0:T(8,128)(2,1)S(1)} copy-done((bf16[512,4608]{1,0:T(8,128)(2,1)S(1)}, bf16[512,4608]{1,0:T(8,128)(2,1)}, u32[]{:S(2)}) %copy-start.1) | copy-done | bytes 4718616
  98.6 1.0 copy-done.2
  99.6 1.0 copy-done.3
  100.6 5.2 %shard_map.123 = (f32[512,256]{1,0:T(8,128)S(1)}, f32[512,256]{1,0:T(8,128)S(1)}, f32[2,256]{1,0:T(2,128)S(1)}) custom-call(bf16[256,4608]{1,0:T(8,128)(2,1)S(1)} %bitcast.28, bf16[512,4608]{1,0:T(8,128)(2,1)S(1)} %copy-done.1, bf16[512,4608]{1,0:T(8,128)(2,1)} %collective-permute-done.2.other_head, f32[512,256]{1,0:T(8,128)S(1)} %copy-done.2, ...), custom_call_target="tpu_custom_call" | custom-call | flops 2415919104 | bytes 9437184 | tf_op jit(solution)/shard_map/pallas_call | solution.py:189
  105.8 0.8 copy-done.4
  106.6 0.8 copy-done.5
  107.4 15.4 %all_to_all.41 = f32[16,6,128]{2,1,0:T(8,128)S(1)} all-to-all(f32[16,6,128]{2,1,0:T(8,128)S(1)} %broadcast_in_dim.19), channel_id=1, replica_groups=mesh['c'=2,'x'=4,'yl'=2,'yh'=2,'z'=8] {'x','yl','yh'}, dimensions={0} | all-to-all | bytes 98304 | tf_op jit(solution)/shard_map/all_to_all | solution.py:26
  122.9 0.6 broadcast_in_dim.20
  123.5 7.6 %all-to-all-start.5 = ((f32[8,6,128]{2,1,0:T(8,128)}), f32[8,6,128]{2,1,0:T(8,128)S(1)}, u32[]{:S(2)}, u32[]{:S(2)}) async-start(f32[8,6,128]{2,1,0:T(8,128)} %broadcast_in_dim.20), calls=%async_computation.5 | async-start | bytes 65536 | tf_op jit(solution)/shard_map/all_to_all | solution.py:26
  131.1 6.6 %all-to-all-done.5 = f32[8,6,128]{2,1,0:T(8,128)S(1)} async-done(((f32[8,6,128]{2,1,0:T(8,128)}), f32[8,6,128]{2,1,0:T(8,128)S(1)}, u32[]{:S(2)}, u32[]{:S(2)}) %all-to-all-start.5) | async-done | bytes 24608 | tf_op jit(solution)/shard_map/all_to_all | solution.py:26
  137.7 0.8 bitcast_divide_fusion
  139.1 7.2 %shard_map.124 = (bf16[512,256]{1,0:T(8,128)(2,1)}, bf16[512,256]{1,0:T(8,128)(2,1)}, bf16[256,3584]{1,0:T(8,128)(2,1)}) custom-call(f32[512,256]{1,0:T(8,128)} %copy-done.4, f32[512,256]{1,0:T(8,128)} %copy-done.5, f32[512,256]{1,0:T(8,128)} %get-tuple-element.26.own_tanh, f32[512,256]{1,0:T(8,128)} %get-tuple-element.27.other_tanh, ...), custom_call_target="tpu_custom_call" | custom-call | flops 1879048192 | bytes 9961472 | tf_op jit(solution)/shard_map/pallas_call | solution.py:247
  146.2 3.6 %all-to-all-start.6 = ((bf16[8,32,3584]{2,1,0:T(8,128)(2,1)}), bf16[8,32,3584]{2,1,0:T(8,128)(2,1)S(1)}, u32[]{:S(2)}, u32[]{:S(2)}) async-start(bf16[8,32,3584]{2,1,0:T(8,128)(2,1)} %bitcast.29), calls=%async_computation.6 | async-start | bytes 3670016 | tf_op jit(solution)/shard_map/all_to_all | solution.py:379
  149.8 0.8 dynamic_slice.17
  150.6 1.7 constant_dynamic-slice_fusion.normed
  152.9 17.5 %all-to-all-done.6.parts = bf16[8,32,3584]{2,1,0:T(8,128)(2,1)S(1)} async-done(((bf16[8,32,3584]{2,1,0:T(8,128)(2,1)}), bf16[8,32,3584]{2,1,0:T(8,128)(2,1)S(1)}, u32[]{:S(2)}, u32[]{:S(2)}) %all-to-all-start.6) | async-done | bytes 1835040 | tf_op jit(solution)/shard_map/all_to_all | solution.py:379
  170.4 1.2 copy-done.6
  171.6 2.6 %shard_map.125 = bf16[16,32,256]{2,1,0:T(8,128)(2,1)} custom-call(bf16[8,32,3584]{2,1,0:T(8,128)(2,1)} %copy-done.6, bf16[32,3584]{1,0:T(8,128)(2,1)} %constant_dynamic-slice_fusion.normed), custom_call_target="tpu_custom_call" | custom-call | flops 917504 | bytes 1835008 | tf_op jit(solution)/shard_map/pallas_call | solution.py:288
  174.3 7.6 %all-to-all-start.7 = ((bf16[16,32,256]{2,1,0:T(8,128)(2,1)}), bf16[16,32,256]{2,1,0:T(8,128)(2,1)S(1)}, u32[]{:S(2)}, u32[]{:S(2)}) async-start(bf16[16,32,256]{2,1,0:T(8,128)(2,1)} %shard_map.125), calls=%async_computation.7 | async-start | bytes 524288 | tf_op jit(solution)/shard_map/all_to_all | solution.py:386
  181.9 2.8 %fusion.8 = f32[512,3584]{1,0:T(8,128)S(1)} fusion(bf16[512,256]{1,0:T(8,128)(2,1)S(1)} %collective-permute-done.10, bf16[256,3584]{1,0:T(8,128)(2,1)} %collective-permute-done.11), kind=kOutput, calls=%fused_computation.27 | convolution fusion | flops 939524096 | bytes 9437184 | tf_op jit(solution)/shard_map/dot_general | solution.py:382
  184.7 3.0 %add_convert_fusion = bf16[512,3584]{1,0:T(8,128)(2,1)} fusion(f32[512,3584]{1,0:T(8,128)S(1)} %fusion.8, bf16[512,256]{1,0:T(8,128)(2,1)S(1)} %copy-done.11, bf16[256,3584]{1,0:T(8,128)(2,1)S(1)} %copy-done.7), kind=kOutput, calls=%fused_computation | convolution fusion | flops 943194112 | bytes 13107200 | tf_op jit(solution)/shard_map/dot_general | solution.py:381
  187.6 4.8 %all-to-all-done.7 = bf16[16,32,256]{2,1,0:T(8,128)(2,1)S(1)} async-done(((bf16[16,32,256]{2,1,0:T(8,128)(2,1)}), bf16[16,32,256]{2,1,0:T(8,128)(2,1)S(1)}, u32[]{:S(2)}, u32[]{:S(2)}) %all-to-all-start.7) | async-done | bytes 262176 | tf_op jit(solution)/shard_map/all_to_all | solution.py:386
  192.4 0.9 dynamic-slice_reduce_fusion
  193.4 0.7 fusion.1
  (72 shorter events, 4.3 us)
Async XLA Ops:
  0.6 1.3 copy-start
  0.6 2.4 %copy-start.19 = (bf16[32,288]{1,0:T(8,128)(2,1)S(1)}, bf16[32,288]{1,0:T(8,128)(2,1)}, u32[]{:S(2)}) copy-start(bf16[32,288]{1,0:T(8,128)(2,1)} %param.11) | copy-start | bytes 55300
  0.7 2.4 %copy-start.20 = (f32[288]{0:T(512)S(1)}, f32[288]{0:T(512)}, u32[]{:S(2)}) copy-start(f32[288]{0:T(512)} %param.14) | copy-start | bytes 3460
  0.7 2.4 %copy-start.21 = (f32[288]{0:T(512)S(1)}, f32[288]{0:T(512)}, u32[]{:S(2)}) copy-start(f32[288]{0:T(512)} %param.13) | copy-start | bytes 3460
  0.7 27.7 %copy-start.18 = (bf16[32,224]{1,0:T(8,128)(2,1)S(1)}, bf16[32,224]{1,0:T(8,128)(2,1)}, u32[]{:S(2)}) copy-start(bf16[32,224]{1,0:T(8,128)(2,1)} %param.16) | copy-start | bytes 43012
  0.7 95.5 %collective-permute-start.2 = (bf16[512,4608]{1,0:T(8,128)(2,1)}, bf16[512,4608]{1,0:T(8,128)(2,1)}, u32[]{:S(2)}, u32[]{:S(2)}) collective-permute-start(bf16[512,4608]{1,0:T(8,128)(2,1)} %own_head.2), channel_id=1, source_target_pairs={{0,128},{128,0},{1,129},{129,1},{2,130},{130,2},{3,131},{131,3},{4... | collective-permute-start | bytes 14155784 | tf_op jit(solution)/shard_map/ppermute | solution.py:21
  0.8 85.0 %collective-permute-start.9 = (bf16[512,3584]{1,0:T(8,128)(2,1)}, bf16[512,3584]{1,0:T(8,128)(2,1)}, u32[]{:S(2)}, u32[]{:S(2)}) collective-permute-start(bf16[512,3584]{1,0:T(8,128)(2,1)} %own_head.3), channel_id=1, source_target_pairs={{0,128},{128,0},{1,129},{129,1},{2,130},{130,2},{3,131},{131,3},{4... | collective-permute-start | bytes 11010056 | tf_op jit(solution)/shard_map/ppermute | solution.py:21
  29.1 14.5 %all-to-all-start.1 = ((bf16[16,32,224]{2,1,0:T(8,128)(2,1)}), bf16[16,32,224]{2,1,0:T(8,128)(2,1)S(1)}, u32[]{:S(2)}, u32[]{:S(2)}) async-start(bf16[16,32,224]{2,1,0:T(8,128)(2,1)} %broadcast_in_dim.15), calls=%async_computation.1 | async-start | bytes 524288 | tf_op jit(solution)/shard_map/all_to_all | solution.py:26
  43.6 17.2 %copy-start.8 = (bf16[16,32,224]{2,1,0:T(8,128)(2,1)}, bf16[16,32,224]{2,1,0:T(8,128)(2,1)S(1)}, u32[]{:S(2)}) copy-start(bf16[16,32,224]{2,1,0:T(8,128)(2,1)S(1)} %all-to-all-done.1) | copy-start | bytes 688132
  43.6 15.0 %all-to-all-start.2 = ((bf16[16,2,4608]{2,1,0:T(2,128)(2,1)}), bf16[16,2,4608]{2,1,0:T(2,128)(2,1)S(1)}, u32[]{:S(2)}, u32[]{:S(2)}) async-start(bf16[16,2,4608]{2,1,0:T(2,128)(2,1)} %shard_map.121), calls=%async_computation.2 | async-start | bytes 589824 | tf_op jit(solution)/shard_map/all_to_all | solution.py:346
  47.3 11.3 %collective-permute-start = (bf16[512,224]{1,0:T(8,128)(2,1)S(1)}, bf16[512,224]{1,0:T(8,128)(2,1)S(1)}, u32[]{:S(2)}, u32[]{:S(2)}) collective-permute-start(bf16[512,224]{1,0:T(8,128)(2,1)S(1)} %bitcast.30), channel_id=1, source_target_pairs={{0,1},{1,2},{2,3},{3,4},{4,5},{5,6},{6,7},{7,0},{8,9},{9,10},{10,1... | collective-permute-start | bytes 688136 | tf_op jit(solution)/shard_map/ppermute | solution.py:32
  48.8 10.3 %collective-permute-start.1 = (bf16[512,224]{1,0:T(8,128)(2,1)S(1)}, bf16[512,224]{1,0:T(8,128)(2,1)S(1)}, u32[]{:S(2)}, u32[]{:S(2)}) collective-permute-start(bf16[512,224]{1,0:T(8,128)(2,1)S(1)} %bitcast.31), channel_id=1, source_target_pairs={{0,7},{1,0},{2,1},{3,2},{4,3},{5,4},{6,5},{7,6},{8,15},{9,8},{10,9... | collective-permute-start | bytes 688136 | tf_op jit(solution)/shard_map/ppermute | solution.py:33
  58.7 2.0 %copy-start.12 = (bf16[512,224]{1,0:T(8,128)(2,1)}, bf16[512,224]{1,0:T(8,128)(2,1)S(1)}, u32[]{:S(2)}) copy-start(bf16[512,224]{1,0:T(8,128)(2,1)S(1)} %collective-permute-done.refs_1_) | copy-start | bytes 688132
  59.1 1.6 copy-start.13
  60.8 35.5 %all-to-all-start.3 = ((bf16[8,32,4608]{2,1,0:T(8,128)(2,1)}), bf16[8,32,4608]{2,1,0:T(8,128)(2,1)S(1)}, u32[]{:S(2)}, u32[]{:S(2)}) async-start(bf16[8,32,4608]{2,1,0:T(8,128)(2,1)} %broadcast_in_dim.16), calls=%async_computation.3 | async-start | bytes 4718592 | tf_op jit(solution)/shard_map/all_to_all | solution.py:26
  64.4 7.0 %collective-permute-start.3 = (bf16[512,224]{1,0:T(8,128)(2,1)}, bf16[512,224]{1,0:T(8,128)(2,1)S(1)}, u32[]{:S(2)}, u32[]{:S(2)}) collective-permute-start(bf16[512,224]{1,0:T(8,128)(2,1)} %copy-done.12), channel_id=1, source_target_pairs={{0,1},{1,2},{2,3},{3,4},{4,5},{5,6},{6,7},{7,0},{8,9},{9,10},{10,1... | collective-permute-start | bytes 688136 | tf_op jit(solution)/shard_map/ppermute | solution.py:32
  66.5 7.2 %collective-permute-start.4 = (bf16[512,224]{1,0:T(8,128)(2,1)}, bf16[512,224]{1,0:T(8,128)(2,1)S(1)}, u32[]{:S(2)}, u32[]{:S(2)}) collective-permute-start(bf16[512,224]{1,0:T(8,128)(2,1)} %copy-done.13), channel_id=1, source_target_pairs={{0,7},{1,0},{2,1},{3,2},{4,3},{5,4},{6,5},{7,6},{8,15},{9,8},{10,9... | collective-permute-start | bytes 688136 | tf_op jit(solution)/shard_map/ppermute | solution.py:33
  71.4 14.4 %copy-start.14 = (bf16[512,224]{1,0:T(8,128)(2,1)}, bf16[512,224]{1,0:T(8,128)(2,1)S(1)}, u32[]{:S(2)}) copy-start(bf16[512,224]{1,0:T(8,128)(2,1)S(1)} %collective-permute-done.3.refs_3_) | copy-start | bytes 688132
  71.4 7.3 %collective-permute-start.5 = (bf16[512,224]{1,0:T(8,128)(2,1)S(1)}, bf16[512,224]{1,0:T(8,128)(2,1)S(1)}, u32[]{:S(2)}, u32[]{:S(2)}) collective-permute-start(bf16[512,224]{1,0:T(8,128)(2,1)S(1)} %collective-permute-done.3.refs_3_), channel_id=1, source_target_pairs={{0,1},{1,2},{2,3},{3,4},{4,5},{5,6},{6,7},{7,0},{8,9},{9,10},{10,1... | collective-permute-start | bytes 688136 | tf_op jit(solution)/shard_map/ppermute | solution.py:32
  73.7 12.1 %copy-start.15 = (bf16[512,224]{1,0:T(8,128)(2,1)}, bf16[512,224]{1,0:T(8,128)(2,1)S(1)}, u32[]{:S(2)}) copy-start(bf16[512,224]{1,0:T(8,128)(2,1)S(1)} %collective-permute-done.4.refs_4_) | copy-start | bytes 688132
  73.7 6.5 %collective-permute-start.6 = (bf16[512,224]{1,0:T(8,128)(2,1)S(1)}, bf16[512,224]{1,0:T(8,128)(2,1)S(1)}, u32[]{:S(2)}, u32[]{:S(2)}) collective-permute-start(bf16[512,224]{1,0:T(8,128)(2,1)S(1)} %collective-permute-done.4.refs_4_), channel_id=1, source_target_pairs={{0,7},{1,0},{2,1},{3,2},{4,3},{5,4},{6,5},{7,6},{8,15},{9,8},{10,9... | collective-permute-start | bytes 688136 | tf_op jit(solution)/shard_map/ppermute | solution.py:33
  78.7 7.1 %copy-start.9 = (bf16[512,224]{1,0:T(8,128)(2,1)}, bf16[512,224]{1,0:T(8,128)(2,1)S(1)}, u32[]{:S(2)}) copy-start(bf16[512,224]{1,0:T(8,128)(2,1)S(1)} %collective-permute-done.5.refs_5_) | copy-start | bytes 688132
  78.7 6.3 %collective-permute-start.7 = (bf16[256,224]{1,0:T(8,128)(2,1)S(1)}, bf16[256,224]{1,0:T(8,128)(2,1)S(1)}, u32[]{:S(2)}, u32[]{:S(2)}) collective-permute-start(bf16[256,224]{1,0:T(8,128)(2,1)S(1)} %slice.35), channel_id=1, source_target_pairs={{0,1},{1,2},{2,3},{3,4},{4,5},{5,6},{6,7},{7,0},{8,9},{9,10},{10,1... | collective-permute-start | bytes 344072 | tf_op jit(solution)/shard_map/ppermute | solution.py:32
  80.1 5.6 %copy-start.10 = (bf16[512,224]{1,0:T(8,128)(2,1)}, bf16[512,224]{1,0:T(8,128)(2,1)S(1)}, u32[]{:S(2)}) copy-start(bf16[512,224]{1,0:T(8,128)(2,1)S(1)} %collective-permute-done.6.refs_6_) | copy-start | bytes 688132
  80.2 5.6 %collective-permute-start.8 = (bf16[256,224]{1,0:T(8,128)(2,1)S(1)}, bf16[256,224]{1,0:T(8,128)(2,1)S(1)}, u32[]{:S(2)}, u32[]{:S(2)}) collective-permute-start(bf16[256,224]{1,0:T(8,128)(2,1)S(1)} %slice.36), channel_id=1, source_target_pairs={{0,7},{1,0},{2,1},{3,2},{4,3},{5,4},{6,5},{7,6},{8,15},{9,8},{10,9... | collective-permute-start | bytes 344072 | tf_op jit(solution)/shard_map/ppermute | solution.py:33
  85.0 0.8 copy-start.16
  85.7 0.6 copy-start.17
  96.2 2.3 %copy-start.1 = (bf16[512,4608]{1,0:T(8,128)(2,1)S(1)}, bf16[512,4608]{1,0:T(8,128)(2,1)}, u32[]{:S(2)}) copy-start(bf16[512,4608]{1,0:T(8,128)(2,1)} %own_head.2) | copy-start | bytes 14155780
  98.6 1.0 copy-start.2
  99.6 1.0 copy-start.3
  100.6 6.8 %copy-start.22 = (f32[1,256]{1,0:T(1,128)S(1)}, f32[1,256]{1,0:T(1,128)}, u32[]{:S(2)}) copy-start(f32[1,256]{1,0:T(1,128)} %get-tuple-element.29) | copy-start | bytes 3076
  105.8 0.8 copy-start.4
  106.6 0.8 copy-start.5
  123.5 14.2 %all-to-all-start.5 = ((f32[8,6,128]{2,1,0:T(8,128)}), f32[8,6,128]{2,1,0:T(8,128)S(1)}, u32[]{:S(2)}, u32[]{:S(2)}) async-start(f32[8,6,128]{2,1,0:T(8,128)} %broadcast_in_dim.20), calls=%async_computation.5 | async-start | bytes 65536 | tf_op jit(solution)/shard_map/all_to_all | solution.py:26
  131.1 50.7 %collective-permute-start.11 = (bf16[256,3584]{1,0:T(8,128)(2,1)}, bf16[256,3584]{1,0:T(8,128)(2,1)}, u32[]{:S(2)}, u32[]{:S(2)}) collective-permute-start(bf16[256,3584]{1,0:T(8,128)(2,1)} %get-tuple-element.38), channel_id=1, source_target_pairs={{0,128},{128,0},{1,129},{129,1},{2,130},{130,2},{3,131},{131,3},{4... | collective-permute-start | bytes 5505032 | tf_op jit(solution)/shard_map/ppermute | solution.py:21
  146.2 24.2 %all-to-all-start.6 = ((bf16[8,32,3584]{2,1,0:T(8,128)(2,1)}), bf16[8,32,3584]{2,1,0:T(8,128)(2,1)S(1)}, u32[]{:S(2)}, u32[]{:S(2)}) async-start(bf16[8,32,3584]{2,1,0:T(8,128)(2,1)} %bitcast.29), calls=%async_computation.6 | async-start | bytes 3670016 | tf_op jit(solution)/shard_map/all_to_all | solution.py:379
  150.6 31.2 %collective-permute-start.10 = (bf16[512,256]{1,0:T(8,128)(2,1)}, bf16[512,256]{1,0:T(8,128)(2,1)S(1)}, u32[]{:S(2)}, u32[]{:S(2)}) collective-permute-start(bf16[512,256]{1,0:T(8,128)(2,1)} %get-tuple-element.37), channel_id=1, source_target_pairs={{0,128},{128,0},{1,129},{129,1},{2,130},{130,2},{3,131},{131,3},{4... | collective-permute-start | bytes 786440 | tf_op jit(solution)/shard_map/ppermute | solution.py:21
  170.4 1.2 copy-start.6
  174.3 18.1 %all-to-all-start.7 = ((bf16[16,32,256]{2,1,0:T(8,128)(2,1)}), bf16[16,32,256]{2,1,0:T(8,128)(2,1)S(1)}, u32[]{:S(2)}, u32[]{:S(2)}) async-start(bf16[16,32,256]{2,1,0:T(8,128)(2,1)} %shard_map.125), calls=%async_computation.7 | async-start | bytes 524288 | tf_op jit(solution)/shard_map/all_to_all | solution.py:386
  181.8 2.8 %copy-start.7 = (bf16[256,3584]{1,0:T(8,128)(2,1)S(1)}, bf16[256,3584]{1,0:T(8,128)(2,1)}, u32[]{:S(2)}) copy-start(bf16[256,3584]{1,0:T(8,128)(2,1)} %get-tuple-element.38) | copy-start | bytes 5505028
  181.8 2.8 %copy-start.11 = (bf16[512,256]{1,0:T(8,128)(2,1)S(1)}, bf16[512,256]{1,0:T(8,128)(2,1)}, u32[]{:S(2)}) copy-start(bf16[512,256]{1,0:T(8,128)(2,1)} %get-tuple-element.36) | copy-start | bytes 786436

commit v3 on v2

--- a/solution.py
+++ b/solution.py
@@ -338,11 +338,11 @@
         ],
         axis=2,
     )
+    right, left = ring_step(pieces, pieces)
     got = lax.all_to_all(sent, VOC, 0, 0)
     teacher_rows = own_rows(got, teacher_width, teacher_cols)
-    teacher_rows, pieces = lax.optimization_barrier((teacher_rows, pieces))
-    right, left = ring_step(pieces, pieces)
     ring = [pieces, right, left]
+    teacher_rows, right, left = lax.optimization_barrier((teacher_rows, right, left))
     teacher_rows = lax.all_to_all(teacher_rows, VOC, 0, 0).reshape(rows, teacher_width)
     teacher_rows, right, left = lax.optimization_barrier((teacher_rows, right, left))
     right, left = ring_step(right, left)
@@ -362,10 +362,9 @@
         teacher_all, teacher_head, teacher_other, tanh_mine, tanh_others
     )
     sums = jnp.concatenate([teacher_sums, student_sum]).reshape(-1, 128)
-    sums = jnp.sum(spread(sums, XY), axis=0)
     sums, student_tied = lax.optimization_barrier((sums, student_all))
     student_all_other = swap(student_tied)
-    totals = jnp.sum(spread(sums, "z"), axis=0).reshape(3, half)
+    totals = jnp.sum(spread(sums, ("x", "yl", "yh", "z")), axis=0).reshape(3, half)
     teacher_total, mixed, student_total = totals[0], totals[1], totals[2]
     token_kl = mixed / teacher_total + jnp.log(student_total) - jnp.log(teacher_total)
     token_kl = lax.dynamic_slice_in_dim(token_kl, row_index * rows + voc_index * own, own)

time: 195 us -> 194 us (level)
  blocking collectives: 39.7 us -> 18.9 us
  waiting for transfers between devices: 56.9 us -> 63.9 us
  matrix products: 6.7 us -> 13.1 us
  starting transfers between devices: 42.8 us -> 48.4 us
    all_to_all x2 -> x1, blocking collectives: 39.7 us -> 18.9 us  [local(): lax.all_to_all(teacher_rows, VOC, 0, 0).reshape(rows, teacher_width)]
    all_to_all x3, waiting for transfers between devices: 13.4 us -> 21.5 us  [spread(): lax.all_to_all(jnp.broadcast_to(value[None], (count, *value.shape)), axes...]
    all_to_all x1, starting transfers between devices: 3.78 us -> 8.82 us  [local(): got = lax.all_to_all(sent, VOC, 0, 0)]
    all_to_all x3, starting transfers between devices: 16.9 us -> 21.4 us  [spread(): lax.all_to_all(jnp.broadcast_to(value[None], (count, *value.shape)), axes...]
    all_to_all x1, waiting for transfers between devices: 17.5 us -> 13 us  [local(): lax.all_to_all(terms.reshape(row_count, rows, student_width), ROW, 0, 0)]
    dot_general x1, matrix products: 2.96 us -> 6.61 us  [local(): jnp.dot(grad_mine, student_all, preferred_element_type=f32)]
    all_to_all x1, starting transfers between devices: 7.57 us -> 4.53 us  [local(): last = jnp.sum(lax.all_to_all(last, VOC, 0, 0).astype(f32), axis=0)]
    dot_general x1, matrix products: 2.76 us -> 5.51 us  [local(): jnp.dot(grad_back, student_all_other, preferred_element_type=f32)]
  transfers between devices with their start and end apart: 18 -> 18, of which waited for: 11 -> 9; matrix products, arithmetic and copies ran while one was open for 8% -> 12% of each run, Pallas kernels for 11% -> 10%
where the time goes in v3:
time: 194 us; the launch traced here: 192 us
  waiting for transfers between devices  63.9 us (33%)
  starting transfers between devices  48.4 us (25%)
  Pallas kernels  26.8 us (14%)
  blocking collectives  18.9 us (10%)
  local copies, waits for them, and re-layouts  17.7 us (9%)
  matrix products  13.1 us (7%)
  other arithmetic  2.59 us (1%)
    all_to_all x3, waiting for transfers between devices, spread(): lax.all_to_all(jnp.broadcast_to(value[None], (count, *value.shape)), axes...  21.5 us
    all_to_all x3, starting transfers between devices, spread(): lax.all_to_all(jnp.broadcast_to(value[None], (count, *value.shape)), axes...  21.4 us
    all_to_all x1, blocking collectives, local(): lax.all_to_all(teacher_rows, VOC, 0, 0).reshape(rows, teacher_width)  18.9 us
    all_to_all x1, waiting for transfers between devices, local(): lax.all_to_all(terms.reshape(row_count, rows, student_width), ROW, 0, 0)  13 us
    ppermute x4, waiting for transfers between devices, ring_step(): lax.ppermute(right, 'z', [(i, (i + 1) % count) for i in range(count)])  12.9 us
    all_to_all x1, waiting for transfers between devices, local(): got = lax.all_to_all(sent, VOC, 0, 0)  10.4 us
    pallas_call x1, Pallas kernels, student_logits(): pl.pallas_call(functools.partial(student_kernel, rows), out_shape=(jax.Sh...  9.8 us
    all_to_all x1, starting transfers between devices, local(): got = lax.all_to_all(sent, VOC, 0, 0)  8.82 us
  transfers between devices with their start and end apart: 18, of which 9 were waited for; matrix products, arithmetic and copies ran while one was open for 12% of the time, Pallas kernels for 10%

profile of v3, /device:TPU:32, one launch (start us, length us, event | category | flops | bytes accessed | tf_op | source)
XLA Modules:
  0.0 192.3 jit_solution(13466436182657914284)
XLA Ops:
  1.3 1.5 broadcast_in_dim.11
  2.7 7.0 %all-to-all-start.1 = ((bf16[16,32,224]{2,1,0:T(8,128)(2,1)}), bf16[16,32,224]{2,1,0:T(8,128)(2,1)S(1)}, u32[]{:S(2)}, u32[]{:S(2)}) async-start(bf16[16,32,224]{2,1,0:T(8,128)(2,1)} %broadcast_in_dim.11), calls=%async_computation.1 | async-start | bytes 524288 | tf_op jit(solution)/shard_map/all_to_all | solution.py:26
  9.8 1.0 convolution_convert_fusion
  11.1 1.9 concatenate.33
  13.0 5.9 %all-to-all-done.1 = bf16[16,32,224]{2,1,0:T(8,128)(2,1)S(1)} async-done(((bf16[16,32,224]{2,1,0:T(8,128)(2,1)}), bf16[16,32,224]{2,1,0:T(8,128)(2,1)S(1)}, u32[]{:S(2)}, u32[]{:S(2)}) %all-to-all-start.1) | async-done | bytes 229408 | tf_op jit(solution)/shard_map/all_to_all | solution.py:26
  18.8 8.8 %all-to-all-start = ((bf16[16,2,5472]{2,1,0:T(2,128)(2,1)}), bf16[16,2,5472]{2,1,0:T(2,128)(2,1)S(1)}, u32[]{:S(2)}, u32[]{:S(2)}) async-start(bf16[16,2,5472]{2,1,0:T(2,128)(2,1)} %concatenate.33), calls=%async_computation | async-start | bytes 704512 | tf_op jit(solution)/shard_map/all_to_all | solution.py:342
  27.7 1.5 collective-permute-start
  29.7 10.4 %all-to-all-done.got = bf16[16,2,5472]{2,1,0:T(2,128)(2,1)S(1)} async-done(((bf16[16,2,5472]{2,1,0:T(2,128)(2,1)}), bf16[16,2,5472]{2,1,0:T(2,128)(2,1)S(1)}, u32[]{:S(2)}, u32[]{:S(2)}) %all-to-all-start) | async-done | bytes 350240 | tf_op jit(solution)/shard_map/all_to_all | solution.py:342
  40.1 0.7 copy-done.7
  40.9 2.1 %shard_map.121 = bf16[16,2,4608]{2,1,0:T(2,128)(2,1)} custom-call(bf16[16,2,5472]{2,1,0:T(2,128)(2,1)} %copy-done.7), custom_call_target="tpu_custom_call" | custom-call | flops 175104 | bytes 700416 | tf_op jit(solution)/shard_map/pallas_call | solution.py:69
  43.0 18.9 %all_to_all.35 = bf16[16,2,4608]{2,1,0:T(2,128)(2,1)S(1)} all-to-all(bf16[16,2,4608]{2,1,0:T(2,128)(2,1)} %shard_map.121), channel_id=1, replica_groups=mesh['c'=2,'x'=4,'yl'=2,'yh'=2,'z'=8] {'yh','z'}, dimensions={0} | all-to-all | bytes 589824 | tf_op jit(solution)/shard_map/all_to_all | solution.py:346
  62.0 1.6 broadcast_in_dim.12
  63.6 3.7 %all-to-all-start.3 = ((bf16[8,32,4608]{2,1,0:T(8,128)(2,1)}), bf16[8,32,4608]{2,1,0:T(8,128)(2,1)S(1)}, u32[]{:S(2)}, u32[]{:S(2)}) async-start(bf16[8,32,4608]{2,1,0:T(8,128)(2,1)} %broadcast_in_dim.12), calls=%async_computation.3 | async-start | bytes 4718592 | tf_op jit(solution)/shard_map/all_to_all | solution.py:26
  67.3 1.0 collective-permute-start.3
  68.3 1.1 collective-permute-start.4
  69.3 5.6 %collective-permute-done.3.refs_3_ = bf16[512,224]{1,0:T(8,128)(2,1)S(1)} collective-permute-done((bf16[512,224]{1,0:T(8,128)(2,1)}, bf16[512,224]{1,0:T(8,128)(2,1)S(1)}, u32[]{:S(2)}, u32[]{:S(2)}) %collective-permute-start.3) | collective-permute-done | bytes 229408 | tf_op jit(solution)/shard_map/ppermute | solution.py:32
  74.9 1.7 collective-permute-start.5
  76.6 0.6 collective-permute-start.6
  77.2 5.5 %collective-permute-done.5.refs_5_ = bf16[512,224]{1,0:T(8,128)(2,1)S(1)} collective-permute-done((bf16[512,224]{1,0:T(8,128)(2,1)S(1)}, bf16[512,224]{1,0:T(8,128)(2,1)S(1)}, u32[]{:S(2)}, u32[]{:S(2)}) %collective-permute-start.5) | collective-permute-done | bytes 229408 | tf_op jit(solution)/shard_map/ppermute | solution.py:32
  82.7 1.8 collective-permute-start.7
  84.5 0.8 collective-permute-start.8
  85.3 0.6 broadcast_in_dim.13.gain
  85.9 1.9 collective-permute-done.7.refs_7_
  87.8 2.0 %collective-permute-done.8.refs_8_ = bf16[256,224]{1,0:T(8,128)(2,1)S(1)} collective-permute-done((bf16[256,224]{1,0:T(8,128)(2,1)S(1)}, bf16[256,224]{1,0:T(8,128)(2,1)S(1)}, u32[]{:S(2)}, u32[]{:S(2)}) %collective-permute-start.8) | collective-permute-done | bytes 114720 | tf_op jit(solution)/shard_map/ppermute | solution.py:33
  89.8 0.6 copy-done.17
  90.4 9.8 %shard_map.122 = (bf16[256,3584]{1,0:T(8,128)(2,1)}, f32[256,1]{1,0:T(8,128)}, f32[512,256]{1,0:T(8,128)}, f32[512,256]{1,0:T(8,128)}, f32[1,256]{1,0:T(1,128)}) custom-call(f32[1,3584]{1,0:T(1,128)} %broadcast_in_dim.13.gain, bf16[512,224]{1,0:T(8,128)(2,1)} %bitcast.32, bf16[512,224]{1,0:T(8,128)(2,1)} %copy-done.12, bf16[512,224]{1,0:T(8,128)(2,1)} %copy-done.13, ...), custom_call_target="tpu_custom_call" | custom-call | flops 1879048192 | bytes 7340032 | tf_op jit(solution)/shard_map/pallas_call | solution.py:145
  100.2 2.3 %copy-done.1 = bf16[512,4608]{1,0:T(8,128)(2,1)S(1)} copy-done((bf16[512,4608]{1,0:T(8,128)(2,1)S(1)}, bf16[512,4608]{1,0:T(8,128)(2,1)}, u32[]{:S(2)}) %copy-start.1) | copy-done | bytes 4718616
  102.5 1.0 copy-done.2
  103.6 1.0 copy-done.3
  104.6 5.2 %shard_map.123 = (f32[512,256]{1,0:T(8,128)S(1)}, f32[512,256]{1,0:T(8,128)S(1)}, f32[2,256]{1,0:T(2,128)S(1)}) custom-call(bf16[256,4608]{1,0:T(8,128)(2,1)S(1)} %bitcast.28, bf16[512,4608]{1,0:T(8,128)(2,1)S(1)} %copy-done.1, bf16[512,4608]{1,0:T(8,128)(2,1)} %collective-permute-done.2.other_head, f32[512,256]{1,0:T(8,128)S(1)} %copy-done.2, ...), custom_call_target="tpu_custom_call" | custom-call | flops 2415919104 | bytes 9437184 | tf_op jit(solution)/shard_map/pallas_call | solution.py:189
  109.8 0.8 copy-done.4
  110.6 0.8 copy-done.5
  111.4 0.8 broadcast_in_dim.14
  112.2 10.7 %all-to-all-start.4 = ((f32[128,6,128]{2,1,0:T(8,128)}), f32[128,6,128]{2,1,0:T(8,128)S(1)}, u32[]{:S(2)}, u32[]{:S(2)}) async-start(f32[128,6,128]{2,1,0:T(8,128)} %broadcast_in_dim.14), calls=%async_computation.4 | async-start | bytes 1048576 | tf_op jit(solution)/shard_map/all_to_all | solution.py:26
  123.0 15.7 %all-to-all-done.4 = f32[128,6,128]{2,1,0:T(8,128)S(1)} async-done(((f32[128,6,128]{2,1,0:T(8,128)}), f32[128,6,128]{2,1,0:T(8,128)S(1)}, u32[]{:S(2)}, u32[]{:S(2)}) %all-to-all-start.4) | async-done | bytes 393248 | tf_op jit(solution)/shard_map/all_to_all | solution.py:26
  138.9 0.6 pad_maximum_fusion.3.scales
  139.5 7.2 %shard_map.124 = (bf16[512,256]{1,0:T(8,128)(2,1)}, bf16[512,256]{1,0:T(8,128)(2,1)}, bf16[256,3584]{1,0:T(8,128)(2,1)}) custom-call(f32[512,256]{1,0:T(8,128)} %copy-done.4, f32[512,256]{1,0:T(8,128)} %copy-done.5, f32[512,256]{1,0:T(8,128)} %get-tuple-element.28.own_tanh, f32[512,256]{1,0:T(8,128)} %get-tuple-element.29.other_tanh, ...), custom_call_target="tpu_custom_call" | custom-call | flops 1879048192 | bytes 9961472 | tf_op jit(solution)/shard_map/pallas_call | solution.py:247
  146.7 3.7 %all-to-all-start.5 = ((bf16[8,32,3584]{2,1,0:T(8,128)(2,1)}), bf16[8,32,3584]{2,1,0:T(8,128)(2,1)S(1)}, u32[]{:S(2)}, u32[]{:S(2)}) async-start(bf16[8,32,3584]{2,1,0:T(8,128)(2,1)} %bitcast.29), calls=%async_computation.5 | async-start | bytes 3670016 | tf_op jit(solution)/shard_map/all_to_all | solution.py:378
  150.8 1.7 constant_dynamic-slice_fusion.normed
  153.1 5.5 %fusion.8 = f32[512,3584]{1,0:T(8,128)} fusion(bf16[512,256]{1,0:T(8,128)(2,1)S(1)} %collective-permute-done.10, bf16[256,3584]{1,0:T(8,128)(2,1)} %collective-permute-done.11), kind=kOutput, calls=%fused_computation.27 | convolution fusion | flops 939524096 | bytes 9437184 | tf_op jit(solution)/shard_map/dot_general | solution.py:381
  158.6 13.0 %all-to-all-done.5.parts = bf16[8,32,3584]{2,1,0:T(8,128)(2,1)S(1)} async-done(((bf16[8,32,3584]{2,1,0:T(8,128)(2,1)}), bf16[8,32,3584]{2,1,0:T(8,128)(2,1)S(1)}, u32[]{:S(2)}, u32[]{:S(2)}) %all-to-all-start.5) | async-done | bytes 1835040 | tf_op jit(solution)/shard_map/all_to_all | solution.py:378
  171.6 1.2 copy-done.6
  172.8 2.6 %shard_map.125 = bf16[16,32,256]{2,1,0:T(8,128)(2,1)} custom-call(bf16[8,32,3584]{2,1,0:T(8,128)(2,1)} %copy-done.6, bf16[32,3584]{1,0:T(8,128)(2,1)} %constant_dynamic-slice_fusion.normed), custom_call_target="tpu_custom_call" | custom-call | flops 917504 | bytes 1835008 | tf_op jit(solution)/shard_map/pallas_call | solution.py:288
  175.5 4.5 %all-to-all-start.6 = ((bf16[16,32,256]{2,1,0:T(8,128)(2,1)}), bf16[16,32,256]{2,1,0:T(8,128)(2,1)S(1)}, u32[]{:S(2)}, u32[]{:S(2)}) async-start(bf16[16,32,256]{2,1,0:T(8,128)(2,1)} %shard_map.125), calls=%async_computation.6 | async-start | bytes 524288 | tf_op jit(solution)/shard_map/all_to_all | solution.py:385
  180.0 6.6 %add_convert_fusion = bf16[512,3584]{1,0:T(8,128)(2,1)} fusion(f32[512,3584]{1,0:T(8,128)} %fusion.8, bf16[512,256]{1,0:T(8,128)(2,1)S(1)} %copy-done.11, bf16[256,3584]{1,0:T(8,128)(2,1)} %get-tuple-element.40), kind=kOutput, calls=%fused_computation | convolution fusion | flops 943194112 | bytes 13107200 | tf_op jit(solution)/shard_map/dot_general | solution.py:380
  186.6 4.0 %all-to-all-done.6 = bf16[16,32,256]{2,1,0:T(8,128)(2,1)S(1)} async-done(((bf16[16,32,256]{2,1,0:T(8,128)(2,1)}), bf16[16,32,256]{2,1,0:T(8,128)(2,1)S(1)}, u32[]{:S(2)}, u32[]{:S(2)}) %all-to-all-start.6) | async-done | bytes 262176 | tf_op jit(solution)/shard_map/all_to_all | solution.py:385
  190.7 0.9 dynamic-slice_reduce_fusion
  191.6 0.7 fusion.1
  (75 shorter events, 3.0 us)
Async XLA Ops:
  0.6 9.2 %copy-start = (bf16[128,4608]{1,0:T(8,128)(2,1)S(1)}, bf16[128,4608]{1,0:T(8,128)(2,1)}, u32[]{:S(2)}) copy-start(bf16[128,4608]{1,0:T(8,128)(2,1)} %param.12) | copy-start | bytes 3538948
  0.6 10.3 %copy-start.19 = (bf16[32,288]{1,0:T(8,128)(2,1)S(1)}, bf16[32,288]{1,0:T(8,128)(2,1)}, u32[]{:S(2)}) copy-start(bf16[32,288]{1,0:T(8,128)(2,1)} %param.11) | copy-start | bytes 55300
  0.7 10.3 %copy-start.21 = (f32[288]{0:T(512)S(1)}, f32[288]{0:T(512)}, u32[]{:S(2)}) copy-start(f32[288]{0:T(512)} %param.14) | copy-start | bytes 3460
  0.7 10.3 %copy-start.22 = (f32[288]{0:T(512)S(1)}, f32[288]{0:T(512)}, u32[]{:S(2)}) copy-start(f32[288]{0:T(512)} %param.13) | copy-start | bytes 3460
  0.7 99.5 %collective-permute-start.2 = (bf16[512,4608]{1,0:T(8,128)(2,1)}, bf16[512,4608]{1,0:T(8,128)(2,1)}, u32[]{:S(2)}, u32[]{:S(2)}) collective-permute-start(bf16[512,4608]{1,0:T(8,128)(2,1)} %own_head.2), channel_id=1, source_target_pairs={{0,128},{128,0},{1,129},{129,1},{2,130},{130,2},{3,131},{131,3},{4... | collective-permute-start | bytes 14155784 | tf_op jit(solution)/shard_map/ppermute | solution.py:21
  0.8 88.9 %collective-permute-start.9 = (bf16[512,3584]{1,0:T(8,128)(2,1)}, bf16[512,3584]{1,0:T(8,128)(2,1)}, u32[]{:S(2)}, u32[]{:S(2)}) collective-permute-start(bf16[512,3584]{1,0:T(8,128)(2,1)} %own_head.3), channel_id=1, source_target_pairs={{0,128},{128,0},{1,129},{129,1},{2,130},{130,2},{3,131},{131,3},{4... | collective-permute-start | bytes 11010056 | tf_op jit(solution)/shard_map/ppermute | solution.py:21
  2.7 16.1 %all-to-all-start.1 = ((bf16[16,32,224]{2,1,0:T(8,128)(2,1)}), bf16[16,32,224]{2,1,0:T(8,128)(2,1)S(1)}, u32[]{:S(2)}, u32[]{:S(2)}) async-start(bf16[16,32,224]{2,1,0:T(8,128)(2,1)} %broadcast_in_dim.11), calls=%async_computation.1 | async-start | bytes 524288 | tf_op jit(solution)/shard_map/all_to_all | solution.py:26
  18.8 44.7 %copy-start.8 = (bf16[16,32,224]{2,1,0:T(8,128)(2,1)}, bf16[16,32,224]{2,1,0:T(8,128)(2,1)S(1)}, u32[]{:S(2)}) copy-start(bf16[16,32,224]{2,1,0:T(8,128)(2,1)S(1)} %all-to-all-done.1) | copy-start | bytes 688132
  18.8 21.3 %all-to-all-start = ((bf16[16,2,5472]{2,1,0:T(2,128)(2,1)}), bf16[16,2,5472]{2,1,0:T(2,128)(2,1)S(1)}, u32[]{:S(2)}, u32[]{:S(2)}) async-start(bf16[16,2,5472]{2,1,0:T(2,128)(2,1)} %concatenate.33), calls=%async_computation | async-start | bytes 704512 | tf_op jit(solution)/shard_map/all_to_all | solution.py:342
  27.7 15.3 %collective-permute-start = (bf16[512,224]{1,0:T(8,128)(2,1)S(1)}, bf16[512,224]{1,0:T(8,128)(2,1)S(1)}, u32[]{:S(2)}, u32[]{:S(2)}) collective-permute-start(bf16[512,224]{1,0:T(8,128)(2,1)S(1)} %bitcast.30), channel_id=1, source_target_pairs={{0,1},{1,2},{2,3},{3,4},{4,5},{5,6},{6,7},{7,0},{8,9},{9,10},{10,1... | collective-permute-start | bytes 688136 | tf_op jit(solution)/shard_map/ppermute | solution.py:32
  29.1 13.8 %collective-permute-start.1 = (bf16[512,224]{1,0:T(8,128)(2,1)S(1)}, bf16[512,224]{1,0:T(8,128)(2,1)S(1)}, u32[]{:S(2)}, u32[]{:S(2)}) collective-permute-start(bf16[512,224]{1,0:T(8,128)(2,1)S(1)} %bitcast.31), channel_id=1, source_target_pairs={{0,7},{1,0},{2,1},{3,2},{4,3},{5,4},{6,5},{7,6},{8,15},{9,8},{10,9... | collective-permute-start | bytes 688136 | tf_op jit(solution)/shard_map/ppermute | solution.py:33
  40.1 0.7 copy-start.7
  42.9 20.6 %copy-start.12 = (bf16[512,224]{1,0:T(8,128)(2,1)}, bf16[512,224]{1,0:T(8,128)(2,1)S(1)}, u32[]{:S(2)}) copy-start(bf16[512,224]{1,0:T(8,128)(2,1)S(1)} %collective-permute-done.refs_1_) | copy-start | bytes 688132
  42.9 20.6 %copy-start.13 = (bf16[512,224]{1,0:T(8,128)(2,1)}, bf16[512,224]{1,0:T(8,128)(2,1)S(1)}, u32[]{:S(2)}) copy-start(bf16[512,224]{1,0:T(8,128)(2,1)S(1)} %collective-permute-done.1.refs_2_) | copy-start | bytes 688132
  63.6 21.7 %copy-start.20 = (f32[3584]{0:T(1024)S(1)}, f32[3584]{0:T(1024)}, u32[]{:S(2)}) copy-start(f32[3584]{0:T(1024)} %param.17) | copy-start | bytes 43012
  63.6 36.6 %all-to-all-start.3 = ((bf16[8,32,4608]{2,1,0:T(8,128)(2,1)}), bf16[8,32,4608]{2,1,0:T(8,128)(2,1)S(1)}, u32[]{:S(2)}, u32[]{:S(2)}) async-start(bf16[8,32,4608]{2,1,0:T(8,128)(2,1)} %broadcast_in_dim.12), calls=%async_computation.3 | async-start | bytes 4718592 | tf_op jit(solution)/shard_map/all_to_all | solution.py:26
  67.3 7.6 %collective-permute-start.3 = (bf16[512,224]{1,0:T(8,128)(2,1)}, bf16[512,224]{1,0:T(8,128)(2,1)S(1)}, u32[]{:S(2)}, u32[]{:S(2)}) collective-permute-start(bf16[512,224]{1,0:T(8,128)(2,1)} %copy-done.12), channel_id=1, source_target_pairs={{0,1},{1,2},{2,3},{3,4},{4,5},{5,6},{6,7},{7,0},{8,9},{9,10},{10,1... | collective-permute-start | bytes 688136 | tf_op jit(solution)/shard_map/ppermute | solution.py:32
  68.3 8.3 %collective-permute-start.4 = (bf16[512,224]{1,0:T(8,128)(2,1)}, bf16[512,224]{1,0:T(8,128)(2,1)S(1)}, u32[]{:S(2)}, u32[]{:S(2)}) collective-permute-start(bf16[512,224]{1,0:T(8,128)(2,1)} %copy-done.13), channel_id=1, source_target_pairs={{0,7},{1,0},{2,1},{3,2},{4,3},{5,4},{6,5},{7,6},{8,15},{9,8},{10,9... | collective-permute-start | bytes 688136 | tf_op jit(solution)/shard_map/ppermute | solution.py:33
  74.9 14.8 %copy-start.14 = (bf16[512,224]{1,0:T(8,128)(2,1)}, bf16[512,224]{1,0:T(8,128)(2,1)S(1)}, u32[]{:S(2)}) copy-start(bf16[512,224]{1,0:T(8,128)(2,1)S(1)} %collective-permute-done.3.refs_3_) | copy-start | bytes 688132
  74.9 7.8 %collective-permute-start.5 = (bf16[512,224]{1,0:T(8,128)(2,1)S(1)}, bf16[512,224]{1,0:T(8,128)(2,1)S(1)}, u32[]{:S(2)}, u32[]{:S(2)}) collective-permute-start(bf16[512,224]{1,0:T(8,128)(2,1)S(1)} %collective-permute-done.3.refs_3_), channel_id=1, source_target_pairs={{0,1},{1,2},{2,3},{3,4},{4,5},{5,6},{6,7},{7,0},{8,9},{9,10},{10,1... | collective-permute-start | bytes 688136 | tf_op jit(solution)/shard_map/ppermute | solution.py:32
  76.6 13.1 %copy-start.15 = (bf16[512,224]{1,0:T(8,128)(2,1)}, bf16[512,224]{1,0:T(8,128)(2,1)S(1)}, u32[]{:S(2)}) copy-start(bf16[512,224]{1,0:T(8,128)(2,1)S(1)} %collective-permute-done.4.refs_4_) | copy-start | bytes 688132
  76.6 7.9 %collective-permute-start.6 = (bf16[512,224]{1,0:T(8,128)(2,1)S(1)}, bf16[512,224]{1,0:T(8,128)(2,1)S(1)}, u32[]{:S(2)}, u32[]{:S(2)}) collective-permute-start(bf16[512,224]{1,0:T(8,128)(2,1)S(1)} %collective-permute-done.4.refs_4_), channel_id=1, source_target_pairs={{0,7},{1,0},{2,1},{3,2},{4,3},{5,4},{6,5},{7,6},{8,15},{9,8},{10,9... | collective-permute-start | bytes 688136 | tf_op jit(solution)/shard_map/ppermute | solution.py:33
  82.7 7.0 %copy-start.9 = (bf16[512,224]{1,0:T(8,128)(2,1)}, bf16[512,224]{1,0:T(8,128)(2,1)S(1)}, u32[]{:S(2)}) copy-start(bf16[512,224]{1,0:T(8,128)(2,1)S(1)} %collective-permute-done.5.refs_5_) | copy-start | bytes 688132
  82.7 5.0 %collective-permute-start.7 = (bf16[256,224]{1,0:T(8,128)(2,1)S(1)}, bf16[256,224]{1,0:T(8,128)(2,1)S(1)}, u32[]{:S(2)}, u32[]{:S(2)}) collective-permute-start(bf16[256,224]{1,0:T(8,128)(2,1)S(1)} %slice.35), channel_id=1, source_target_pairs={{0,1},{1,2},{2,3},{3,4},{4,5},{5,6},{6,7},{7,0},{8,9},{9,10},{10,1... | collective-permute-start | bytes 344072 | tf_op jit(solution)/shard_map/ppermute | solution.py:32
  84.5 5.3 %copy-start.10 = (bf16[512,224]{1,0:T(8,128)(2,1)}, bf16[512,224]{1,0:T(8,128)(2,1)S(1)}, u32[]{:S(2)}) copy-start(bf16[512,224]{1,0:T(8,128)(2,1)S(1)} %collective-permute-done.6.refs_6_) | copy-start | bytes 688132
  84.5 5.2 %collective-permute-start.8 = (bf16[256,224]{1,0:T(8,128)(2,1)S(1)}, bf16[256,224]{1,0:T(8,128)(2,1)S(1)}, u32[]{:S(2)}, u32[]{:S(2)}) collective-permute-start(bf16[256,224]{1,0:T(8,128)(2,1)S(1)} %slice.36), channel_id=1, source_target_pairs={{0,7},{1,0},{2,1},{3,2},{4,3},{5,4},{6,5},{7,6},{8,15},{9,8},{10,9... | collective-permute-start | bytes 344072 | tf_op jit(solution)/shard_map/ppermute | solution.py:33
  87.8 2.0 %copy-start.16 = (bf16[256,224]{1,0:T(8,128)(2,1)}, bf16[256,224]{1,0:T(8,128)(2,1)S(1)}, u32[]{:S(2)}) copy-start(bf16[256,224]{1,0:T(8,128)(2,1)S(1)} %collective-permute-done.7.refs_7_) | copy-start | bytes 344068
  89.7 0.6 copy-start.17
  100.2 2.3 %copy-start.1 = (bf16[512,4608]{1,0:T(8,128)(2,1)S(1)}, bf16[512,4608]{1,0:T(8,128)(2,1)}, u32[]{:S(2)}) copy-start(bf16[512,4608]{1,0:T(8,128)(2,1)} %own_head.2) | copy-start | bytes 14155780
  102.5 1.0 copy-start.2
  103.6 1.0 copy-start.3
  104.6 6.8 %copy-start.23 = (f32[1,256]{1,0:T(1,128)S(1)}, f32[1,256]{1,0:T(1,128)}, u32[]{:S(2)}) copy-start(f32[1,256]{1,0:T(1,128)} %get-tuple-element.31) | copy-start | bytes 3076
  109.8 0.8 copy-start.4
  110.6 0.8 copy-start.5
  111.4 27.5 %copy-start.24 = (f32[512]{0:T(512)S(1)}, f32[512]{0:T(512)}, u32[]{:S(2)}) copy-start(f32[512]{0:T(512)} %param.19) | copy-start | bytes 6148
  112.2 26.5 %all-to-all-start.4 = ((f32[128,6,128]{2,1,0:T(8,128)}), f32[128,6,128]{2,1,0:T(8,128)S(1)}, u32[]{:S(2)}, u32[]{:S(2)}) async-start(f32[128,6,128]{2,1,0:T(8,128)} %broadcast_in_dim.14), calls=%async_computation.4 | async-start | bytes 1048576 | tf_op jit(solution)/shard_map/all_to_all | solution.py:26
  122.9 30.2 %collective-permute-start.11 = (bf16[256,3584]{1,0:T(8,128)(2,1)}, bf16[256,3584]{1,0:T(8,128)(2,1)}, u32[]{:S(2)}, u32[]{:S(2)}) collective-permute-start(bf16[256,3584]{1,0:T(8,128)(2,1)} %get-tuple-element.40), channel_id=1, source_target_pairs={{0,128},{128,0},{1,129},{129,1},{2,130},{130,2},{3,131},{131,3},{4... | collective-permute-start | bytes 5505032 | tf_op jit(solution)/shard_map/ppermute | solution.py:21
  146.7 3.8 %copy-start.25 = (bf16[512,256]{1,0:T(8,128)(2,1)S(1)}, bf16[512,256]{1,0:T(8,128)(2,1)}, u32[]{:S(2)}) copy-start(bf16[512,256]{1,0:T(8,128)(2,1)} %get-tuple-element.39) | copy-start | bytes 786436
  146.7 24.9 %all-to-all-start.5 = ((bf16[8,32,3584]{2,1,0:T(8,128)(2,1)}), bf16[8,32,3584]{2,1,0:T(8,128)(2,1)S(1)}, u32[]{:S(2)}, u32[]{:S(2)}) async-start(bf16[8,32,3584]{2,1,0:T(8,128)(2,1)} %bitcast.29), calls=%async_computation.5 | async-start | bytes 3670016 | tf_op jit(solution)/shard_map/all_to_all | solution.py:378
  150.5 2.5 %collective-permute-start.10 = (bf16[512,256]{1,0:T(8,128)(2,1)S(1)}, bf16[512,256]{1,0:T(8,128)(2,1)S(1)}, u32[]{:S(2)}, u32[]{:S(2)}) collective-permute-start(bf16[512,256]{1,0:T(8,128)(2,1)S(1)} %copy-done.25), channel_id=1, source_target_pairs={{0,128},{128,0},{1,129},{129,1},{2,130},{130,2},{3,131},{131,3},{4... | collective-permute-start | bytes 786440 | tf_op jit(solution)/shard_map/ppermute | solution.py:21
  158.6 21.4 %copy-start.11 = (bf16[512,256]{1,0:T(8,128)(2,1)S(1)}, bf16[512,256]{1,0:T(8,128)(2,1)}, u32[]{:S(2)}) copy-start(bf16[512,256]{1,0:T(8,128)(2,1)} %get-tuple-element.38) | copy-start | bytes 786436
  171.6 1.2 copy-start.6
  175.5 15.2 %all-to-all-start.6 = ((bf16[16,32,256]{2,1,0:T(8,128)(2,1)}), bf16[16,32,256]{2,1,0:T(8,128)(2,1)S(1)}, u32[]{:S(2)}, u32[]{:S(2)}) async-start(bf16[16,32,256]{2,1,0:T(8,128)(2,1)} %shard_map.125), calls=%async_computation.6 | async-start | bytes 524288 | tf_op jit(solution)/shard_map/all_to_all | solution.py:385
  180.0 11.6 %copy-start.18 = (bf16[32,224]{1,0:T(8,128)(2,1)S(1)}, bf16[32,224]{1,0:T(8,128)(2,1)}, u32[]{:S(2)}) copy-start(bf16[32,224]{1,0:T(8,128)(2,1)} %param.16) | copy-start | bytes 43012

commit v4 on v3

--- a/solution.py
+++ b/solution.py
@@ -170,15 +170,24 @@
     )(gain, *blocks, own_head, other_head)
 
 
-def teacher_kernel(rows, own_head, other_head, own_tanh, other_tanh, own_exp, other_exp, sums):
+def teacher_kernel(
+    rows, own_head, other_head, own_tanh, other_tanh, own_exp, other_exp, sums, tanhs, sem
+):
+    loads = [
+        pltpu.make_async_copy(own_tanh, tanhs.at[0], sem.at[0]),
+        pltpu.make_async_copy(other_tanh, tanhs.at[1], sem.at[1]),
+    ]
+    for load in loads:
+        load.start()
     total = jnp.zeros((1, rows.shape[0]), f32)
     mixed = jnp.zeros((1, rows.shape[0]), f32)
-    for head, tanh, out in ((own_head, own_tanh, own_exp), (other_head, other_tanh, other_exp)):
+    for i, (head, out) in enumerate(((own_head, own_exp), (other_head, other_exp))):
         logit = softcap * jnp.tanh(dot_t(rows[...], head[...]).T * (1.0 / softcap))
         grown = jnp.exp(logit)
         out[...] = grown
+        loads[i].wait()
         total += jnp.sum(grown, axis=0, keepdims=True)
-        mixed += jnp.sum(grown * (logit - softcap * tanh[...]), axis=0, keepdims=True)
+        mixed += jnp.sum(grown * (logit - softcap * tanhs[i]), axis=0, keepdims=True)
     sums[...] = jnp.concatenate([total, mixed], axis=0)
 
 
@@ -193,8 +202,9 @@
             jax.ShapeDtypeStruct((count, tokens), f32),
             jax.ShapeDtypeStruct((2, tokens), f32),
         ),
-        in_specs=[vmem] * 5,
+        in_specs=[vmem] * 3 + [pl.BlockSpec(memory_space=pl.ANY)] * 2,
         out_specs=(vmem, vmem, vmem),
+        scratch_shapes=[pltpu.VMEM((2, count, tokens), f32), pltpu.SemaphoreType.DMA((2,))],
         compiler_params=pltpu.CompilerParams(vmem_limit_bytes=12 * 2**20),
         cost_estimate=pl.CostEstimate(
             flops=4 * count * tokens * width,

time: 194 us -> 194 us (level)
  no operation moved by 1% of the time
where the time goes in v4:
time: 194 us; the launch traced here: 193 us
  waiting for transfers between devices  63.9 us (33%)
  starting transfers between devices  48.4 us (25%)
  Pallas kernels  27.4 us (14%)
  blocking collectives  18.9 us (10%)
  local copies, waits for them, and re-layouts  17.7 us (9%)
  matrix products  13.1 us (7%)
  other arithmetic  2.59 us (1%)
    all_to_all x3, waiting for transfers between devices, spread(): lax.all_to_all(jnp.broadcast_to(value[None], (count, *value.shape)), axes...  21.5 us
    all_to_all x3, starting transfers between devices, spread(): lax.all_to_all(jnp.broadcast_to(value[None], (count, *value.shape)), axes...  21.4 us
    all_to_all x1, blocking collectives, local(): lax.all_to_all(teacher_rows, VOC, 0, 0).reshape(rows, teacher_width)  18.9 us
    all_to_all x1, waiting for transfers between devices, local(): lax.all_to_all(terms.reshape(row_count, rows, student_width), ROW, 0, 0)  13 us
    ppermute x4, waiting for transfers between devices, ring_step(): lax.ppermute(right, 'z', [(i, (i + 1) % count) for i in range(count)])  12.9 us
    all_to_all x1, waiting for transfers between devices, local(): got = lax.all_to_all(sent, VOC, 0, 0)  10.4 us
    pallas_call x1, Pallas kernels, student_logits(): pl.pallas_call(functools.partial(student_kernel, rows), out_shape=(jax.Sh...  9.8 us
    all_to_all x1, starting transfers between devices, local(): got = lax.all_to_all(sent, VOC, 0, 0)  8.82 us
  transfers between devices with their start and end apart: 18, of which 9 were waited for; matrix products, arithmetic and copies ran while one was open for 12% of the time, Pallas kernels for 10%

profile of v4, /device:TPU:32, one launch (start us, length us, event | category | flops | bytes accessed | tf_op | source)
XLA Modules:
  0.0 192.9 jit_solution(8014119585815709528)
XLA Ops:
  1.3 1.5 broadcast_in_dim.11
  2.7 7.0 %all-to-all-start.1 = ((bf16[16,32,224]{2,1,0:T(8,128)(2,1)}), bf16[16,32,224]{2,1,0:T(8,128)(2,1)S(1)}, u32[]{:S(2)}, u32[]{:S(2)}) async-start(bf16[16,32,224]{2,1,0:T(8,128)(2,1)} %broadcast_in_dim.11), calls=%async_computation.1 | async-start | bytes 524288 | tf_op jit(solution)/shard_map/all_to_all | solution.py:26
  9.8 1.0 convolution_convert_fusion
  11.1 1.9 concatenate.33
  13.0 5.9 %all-to-all-done.1 = bf16[16,32,224]{2,1,0:T(8,128)(2,1)S(1)} async-done(((bf16[16,32,224]{2,1,0:T(8,128)(2,1)}), bf16[16,32,224]{2,1,0:T(8,128)(2,1)S(1)}, u32[]{:S(2)}, u32[]{:S(2)}) %all-to-all-start.1) | async-done | bytes 229408 | tf_op jit(solution)/shard_map/all_to_all | solution.py:26
  18.8 8.8 %all-to-all-start = ((bf16[16,2,5472]{2,1,0:T(2,128)(2,1)}), bf16[16,2,5472]{2,1,0:T(2,128)(2,1)S(1)}, u32[]{:S(2)}, u32[]{:S(2)}) async-start(bf16[16,2,5472]{2,1,0:T(2,128)(2,1)} %concatenate.33), calls=%async_computation | async-start | bytes 704512 | tf_op jit(solution)/shard_map/all_to_all | solution.py:352
  27.7 1.5 collective-permute-start
  29.7 10.4 %all-to-all-done.got = bf16[16,2,5472]{2,1,0:T(2,128)(2,1)S(1)} async-done(((bf16[16,2,5472]{2,1,0:T(2,128)(2,1)}), bf16[16,2,5472]{2,1,0:T(2,128)(2,1)S(1)}, u32[]{:S(2)}, u32[]{:S(2)}) %all-to-all-start) | async-done | bytes 350240 | tf_op jit(solution)/shard_map/all_to_all | solution.py:352
  40.1 0.7 copy-done.7
  40.9 2.1 %shard_map.121 = bf16[16,2,4608]{2,1,0:T(2,128)(2,1)} custom-call(bf16[16,2,5472]{2,1,0:T(2,128)(2,1)} %copy-done.7), custom_call_target="tpu_custom_call" | custom-call | flops 175104 | bytes 700416 | tf_op jit(solution)/shard_map/pallas_call | solution.py:69
  43.0 18.9 %all_to_all.35 = bf16[16,2,4608]{2,1,0:T(2,128)(2,1)S(1)} all-to-all(bf16[16,2,4608]{2,1,0:T(2,128)(2,1)} %shard_map.121), channel_id=1, replica_groups=mesh['c'=2,'x'=4,'yl'=2,'yh'=2,'z'=8] {'yh','z'}, dimensions={0} | all-to-all | bytes 589824 | tf_op jit(solution)/shard_map/all_to_all | solution.py:356
  62.0 1.6 broadcast_in_dim.12
  63.6 3.7 %all-to-all-start.3 = ((bf16[8,32,4608]{2,1,0:T(8,128)(2,1)}), bf16[8,32,4608]{2,1,0:T(8,128)(2,1)S(1)}, u32[]{:S(2)}, u32[]{:S(2)}) async-start(bf16[8,32,4608]{2,1,0:T(8,128)(2,1)} %broadcast_in_dim.12), calls=%async_computation.3 | async-start | bytes 4718592 | tf_op jit(solution)/shard_map/all_to_all | solution.py:26
  67.3 1.0 collective-permute-start.3
  68.3 1.1 collective-permute-start.4
  69.3 5.6 %collective-permute-done.3.refs_3_ = bf16[512,224]{1,0:T(8,128)(2,1)S(1)} collective-permute-done((bf16[512,224]{1,0:T(8,128)(2,1)}, bf16[512,224]{1,0:T(8,128)(2,1)S(1)}, u32[]{:S(2)}, u32[]{:S(2)}) %collective-permute-start.3) | collective-permute-done | bytes 229408 | tf_op jit(solution)/shard_map/ppermute | solution.py:32
  74.9 1.7 collective-permute-start.5
  76.6 0.6 collective-permute-start.6
  77.2 5.5 %collective-permute-done.5.refs_5_ = bf16[512,224]{1,0:T(8,128)(2,1)S(1)} collective-permute-done((bf16[512,224]{1,0:T(8,128)(2,1)S(1)}, bf16[512,224]{1,0:T(8,128)(2,1)S(1)}, u32[]{:S(2)}, u32[]{:S(2)}) %collective-permute-start.5) | collective-permute-done | bytes 229408 | tf_op jit(solution)/shard_map/ppermute | solution.py:32
  82.7 1.8 collective-permute-start.7
  84.5 0.8 collective-permute-start.8
  85.3 0.6 broadcast_in_dim.13.gain
  85.9 1.9 collective-permute-done.7.refs_7_
  87.8 2.0 %collective-permute-done.8.refs_8_ = bf16[256,224]{1,0:T(8,128)(2,1)S(1)} collective-permute-done((bf16[256,224]{1,0:T(8,128)(2,1)S(1)}, bf16[256,224]{1,0:T(8,128)(2,1)S(1)}, u32[]{:S(2)}, u32[]{:S(2)}) %collective-permute-start.8) | collective-permute-done | bytes 114720 | tf_op jit(solution)/shard_map/ppermute | solution.py:33
  89.8 0.6 copy-done.17
  90.4 9.8 %shard_map.122 = (bf16[256,3584]{1,0:T(8,128)(2,1)}, f32[256,1]{1,0:T(8,128)}, f32[512,256]{1,0:T(8,128)}, f32[512,256]{1,0:T(8,128)}, f32[1,256]{1,0:T(1,128)}) custom-call(f32[1,3584]{1,0:T(1,128)} %broadcast_in_dim.13.gain, bf16[512,224]{1,0:T(8,128)(2,1)} %bitcast.32, bf16[512,224]{1,0:T(8,128)(2,1)} %copy-done.12, bf16[512,224]{1,0:T(8,128)(2,1)} %copy-done.13, ...), custom_call_target="tpu_custom_call" | custom-call | flops 1879048192 | bytes 7340032 | tf_op jit(solution)/shard_map/pallas_call | solution.py:145
  100.2 2.3 %copy-done.1 = bf16[512,4608]{1,0:T(8,128)(2,1)S(1)} copy-done((bf16[512,4608]{1,0:T(8,128)(2,1)S(1)}, bf16[512,4608]{1,0:T(8,128)(2,1)}, u32[]{:S(2)}) %copy-start.1) | copy-done | bytes 4718616
  102.5 1.0 copy-done.2
  103.6 1.0 copy-done.3
  104.6 5.7 %shard_map.123 = (f32[512,256]{1,0:T(8,128)S(1)}, f32[512,256]{1,0:T(8,128)S(1)}, f32[2,256]{1,0:T(2,128)S(1)}) custom-call(bf16[256,4608]{1,0:T(8,128)(2,1)S(1)} %bitcast.28, bf16[512,4608]{1,0:T(8,128)(2,1)S(1)} %copy-done.1, bf16[512,4608]{1,0:T(8,128)(2,1)} %collective-permute-done.2.other_head, f32[512,256]{1,0:T(8,128)S(1)} %copy-done.2, ...), custom_call_target="tpu_custom_call" | custom-call | flops 2415919104 | bytes 9437184 | tf_op jit(solution)/shard_map/pallas_call | solution.py:198
  110.4 0.8 copy-done.4
  111.1 0.8 copy-done.5
  112.0 0.8 broadcast_in_dim.14
  112.8 10.7 %all-to-all-start.4 = ((f32[128,6,128]{2,1,0:T(8,128)}), f32[128,6,128]{2,1,0:T(8,128)S(1)}, u32[]{:S(2)}, u32[]{:S(2)}) async-start(f32[128,6,128]{2,1,0:T(8,128)} %broadcast_in_dim.14), calls=%async_computation.4 | async-start | bytes 1048576 | tf_op jit(solution)/shard_map/all_to_all | solution.py:26
  123.6 15.7 %all-to-all-done.4 = f32[128,6,128]{2,1,0:T(8,128)S(1)} async-done(((f32[128,6,128]{2,1,0:T(8,128)}), f32[128,6,128]{2,1,0:T(8,128)S(1)}, u32[]{:S(2)}, u32[]{:S(2)}) %all-to-all-start.4) | async-done | bytes 393248 | tf_op jit(solution)/shard_map/all_to_all | solution.py:26
  139.5 0.6 pad_maximum_fusion.3.scales
  140.1 7.2 %shard_map.124 = (bf16[512,256]{1,0:T(8,128)(2,1)}, bf16[512,256]{1,0:T(8,128)(2,1)}, bf16[256,3584]{1,0:T(8,128)(2,1)}) custom-call(f32[512,256]{1,0:T(8,128)} %copy-done.4, f32[512,256]{1,0:T(8,128)} %copy-done.5, f32[512,256]{1,0:T(8,128)} %get-tuple-element.28.own_tanh, f32[512,256]{1,0:T(8,128)} %get-tuple-element.29.other_tanh, ...), custom_call_target="tpu_custom_call" | custom-call | flops 1879048192 | bytes 9961472 | tf_op jit(solution)/shard_map/pallas_call | solution.py:257
  147.2 3.7 %all-to-all-start.5 = ((bf16[8,32,3584]{2,1,0:T(8,128)(2,1)}), bf16[8,32,3584]{2,1,0:T(8,128)(2,1)S(1)}, u32[]{:S(2)}, u32[]{:S(2)}) async-start(bf16[8,32,3584]{2,1,0:T(8,128)(2,1)} %bitcast.29), calls=%async_computation.5 | async-start | bytes 3670016 | tf_op jit(solution)/shard_map/all_to_all | solution.py:388
  151.3 1.7 constant_dynamic-slice_fusion.normed
  153.6 5.5 %fusion.8 = f32[512,3584]{1,0:T(8,128)} fusion(bf16[512,256]{1,0:T(8,128)(2,1)S(1)} %collective-permute-done.10, bf16[256,3584]{1,0:T(8,128)(2,1)} %collective-permute-done.11), kind=kOutput, calls=%fused_computation.27 | convolution fusion | flops 939524096 | bytes 9437184 | tf_op jit(solution)/shard_map/dot_general | solution.py:391
  159.1 13.0 %all-to-all-done.5.parts = bf16[8,32,3584]{2,1,0:T(8,128)(2,1)S(1)} async-done(((bf16[8,32,3584]{2,1,0:T(8,128)(2,1)}), bf16[8,32,3584]{2,1,0:T(8,128)(2,1)S(1)}, u32[]{:S(2)}, u32[]{:S(2)}) %all-to-all-start.5) | async-done | bytes 1835040 | tf_op jit(solution)/shard_map/all_to_all | solution.py:388
  172.2 1.2 copy-done.6
  173.4 2.6 %shard_map.125 = bf16[16,32,256]{2,1,0:T(8,128)(2,1)} custom-call(bf16[8,32,3584]{2,1,0:T(8,128)(2,1)} %copy-done.6, bf16[32,3584]{1,0:T(8,128)(2,1)} %constant_dynamic-slice_fusion.normed), custom_call_target="tpu_custom_call" | custom-call | flops 917504 | bytes 1835008 | tf_op jit(solution)/shard_map/pallas_call | solution.py:298
  176.0 4.5 %all-to-all-start.6 = ((bf16[16,32,256]{2,1,0:T(8,128)(2,1)}), bf16[16,32,256]{2,1,0:T(8,128)(2,1)S(1)}, u32[]{:S(2)}, u32[]{:S(2)}) async-start(bf16[16,32,256]{2,1,0:T(8,128)(2,1)} %shard_map.125), calls=%async_computation.6 | async-start | bytes 524288 | tf_op jit(solution)/shard_map/all_to_all | solution.py:395
  180.6 6.6 %add_convert_fusion = bf16[512,3584]{1,0:T(8,128)(2,1)} fusion(f32[512,3584]{1,0:T(8,128)} %fusion.8, bf16[512,256]{1,0:T(8,128)(2,1)S(1)} %copy-done.11, bf16[256,3584]{1,0:T(8,128)(2,1)} %get-tuple-element.40), kind=kOutput, calls=%fused_computation | convolution fusion | flops 943194112 | bytes 13107200 | tf_op jit(solution)/shard_map/dot_general | solution.py:390
  187.2 4.0 %all-to-all-done.6 = bf16[16,32,256]{2,1,0:T(8,128)(2,1)S(1)} async-done(((bf16[16,32,256]{2,1,0:T(8,128)(2,1)}), bf16[16,32,256]{2,1,0:T(8,128)(2,1)S(1)}, u32[]{:S(2)}, u32[]{:S(2)}) %all-to-all-start.6) | async-done | bytes 262176 | tf_op jit(solution)/shard_map/all_to_all | solution.py:395
  191.2 0.9 dynamic-slice_reduce_fusion
  192.2 0.7 fusion.1
  (75 shorter events, 3.0 us)
Async XLA Ops:
  0.6 9.2 %copy-start = (bf16[128,4608]{1,0:T(8,128)(2,1)S(1)}, bf16[128,4608]{1,0:T(8,128)(2,1)}, u32[]{:S(2)}) copy-start(bf16[128,4608]{1,0:T(8,128)(2,1)} %param.12) | copy-start | bytes 3538948
  0.6 10.3 %copy-start.19 = (bf16[32,288]{1,0:T(8,128)(2,1)S(1)}, bf16[32,288]{1,0:T(8,128)(2,1)}, u32[]{:S(2)}) copy-start(bf16[32,288]{1,0:T(8,128)(2,1)} %param.11) | copy-start | bytes 55300
  0.7 10.3 %copy-start.21 = (f32[288]{0:T(512)S(1)}, f32[288]{0:T(512)}, u32[]{:S(2)}) copy-start(f32[288]{0:T(512)} %param.14) | copy-start | bytes 3460
  0.7 10.3 %copy-start.22 = (f32[288]{0:T(512)S(1)}, f32[288]{0:T(512)}, u32[]{:S(2)}) copy-start(f32[288]{0:T(512)} %param.13) | copy-start | bytes 3460
  0.7 99.5 %collective-permute-start.2 = (bf16[512,4608]{1,0:T(8,128)(2,1)}, bf16[512,4608]{1,0:T(8,128)(2,1)}, u32[]{:S(2)}, u32[]{:S(2)}) collective-permute-start(bf16[512,4608]{1,0:T(8,128)(2,1)} %own_head.2), channel_id=1, source_target_pairs={{0,128},{128,0},{1,129},{129,1},{2,130},{130,2},{3,131},{131,3},{4... | collective-permute-start | bytes 14155784 | tf_op jit(solution)/shard_map/ppermute | solution.py:21
  0.8 88.9 %collective-permute-start.9 = (bf16[512,3584]{1,0:T(8,128)(2,1)}, bf16[512,3584]{1,0:T(8,128)(2,1)}, u32[]{:S(2)}, u32[]{:S(2)}) collective-permute-start(bf16[512,3584]{1,0:T(8,128)(2,1)} %own_head.3), channel_id=1, source_target_pairs={{0,128},{128,0},{1,129},{129,1},{2,130},{130,2},{3,131},{131,3},{4... | collective-permute-start | bytes 11010056 | tf_op jit(solution)/shard_map/ppermute | solution.py:21
  2.7 16.1 %all-to-all-start.1 = ((bf16[16,32,224]{2,1,0:T(8,128)(2,1)}), bf16[16,32,224]{2,1,0:T(8,128)(2,1)S(1)}, u32[]{:S(2)}, u32[]{:S(2)}) async-start(bf16[16,32,224]{2,1,0:T(8,128)(2,1)} %broadcast_in_dim.11), calls=%async_computation.1 | async-start | bytes 524288 | tf_op jit(solution)/shard_map/all_to_all | solution.py:26
  18.8 44.7 %copy-start.8 = (bf16[16,32,224]{2,1,0:T(8,128)(2,1)}, bf16[16,32,224]{2,1,0:T(8,128)(2,1)S(1)}, u32[]{:S(2)}) copy-start(bf16[16,32,224]{2,1,0:T(8,128)(2,1)S(1)} %all-to-all-done.1) | copy-start | bytes 688132
  18.8 21.3 %all-to-all-start = ((bf16[16,2,5472]{2,1,0:T(2,128)(2,1)}), bf16[16,2,5472]{2,1,0:T(2,128)(2,1)S(1)}, u32[]{:S(2)}, u32[]{:S(2)}) async-start(bf16[16,2,5472]{2,1,0:T(2,128)(2,1)} %concatenate.33), calls=%async_computation | async-start | bytes 704512 | tf_op jit(solution)/shard_map/all_to_all | solution.py:352
  27.7 15.3 %collective-permute-start = (bf16[512,224]{1,0:T(8,128)(2,1)S(1)}, bf16[512,224]{1,0:T(8,128)(2,1)S(1)}, u32[]{:S(2)}, u32[]{:S(2)}) collective-permute-start(bf16[512,224]{1,0:T(8,128)(2,1)S(1)} %bitcast.30), channel_id=1, source_target_pairs={{0,1},{1,2},{2,3},{3,4},{4,5},{5,6},{6,7},{7,0},{8,9},{9,10},{10,1... | collective-permute-start | bytes 688136 | tf_op jit(solution)/shard_map/ppermute | solution.py:32
  29.1 13.8 %collective-permute-start.1 = (bf16[512,224]{1,0:T(8,128)(2,1)S(1)}, bf16[512,224]{1,0:T(8,128)(2,1)S(1)}, u32[]{:S(2)}, u32[]{:S(2)}) collective-permute-start(bf16[512,224]{1,0:T(8,128)(2,1)S(1)} %bitcast.31), channel_id=1, source_target_pairs={{0,7},{1,0},{2,1},{3,2},{4,3},{5,4},{6,5},{7,6},{8,15},{9,8},{10,9... | collective-permute-start | bytes 688136 | tf_op jit(solution)/shard_map/ppermute | solution.py:33
  40.1 0.7 copy-start.7
  42.9 20.6 %copy-start.12 = (bf16[512,224]{1,0:T(8,128)(2,1)}, bf16[512,224]{1,0:T(8,128)(2,1)S(1)}, u32[]{:S(2)}) copy-start(bf16[512,224]{1,0:T(8,128)(2,1)S(1)} %collective-permute-done.refs_1_) | copy-start | bytes 688132
  42.9 20.6 %copy-start.13 = (bf16[512,224]{1,0:T(8,128)(2,1)}, bf16[512,224]{1,0:T(8,128)(2,1)S(1)}, u32[]{:S(2)}) copy-start(bf16[512,224]{1,0:T(8,128)(2,1)S(1)} %collective-permute-done.1.refs_2_) | copy-start | bytes 688132
  63.6 21.7 %copy-start.20 = (f32[3584]{0:T(1024)S(1)}, f32[3584]{0:T(1024)}, u32[]{:S(2)}) copy-start(f32[3584]{0:T(1024)} %param.17) | copy-start | bytes 43012
  63.6 36.6 %all-to-all-start.3 = ((bf16[8,32,4608]{2,1,0:T(8,128)(2,1)}), bf16[8,32,4608]{2,1,0:T(8,128)(2,1)S(1)}, u32[]{:S(2)}, u32[]{:S(2)}) async-start(bf16[8,32,4608]{2,1,0:T(8,128)(2,1)} %broadcast_in_dim.12), calls=%async_computation.3 | async-start | bytes 4718592 | tf_op jit(solution)/shard_map/all_to_all | solution.py:26
  67.3 7.6 %collective-permute-start.3 = (bf16[512,224]{1,0:T(8,128)(2,1)}, bf16[512,224]{1,0:T(8,128)(2,1)S(1)}, u32[]{:S(2)}, u32[]{:S(2)}) collective-permute-start(bf16[512,224]{1,0:T(8,128)(2,1)} %copy-done.12), channel_id=1, source_target_pairs={{0,1},{1,2},{2,3},{3,4},{4,5},{5,6},{6,7},{7,0},{8,9},{9,10},{10,1... | collective-permute-start | bytes 688136 | tf_op jit(solution)/shard_map/ppermute | solution.py:32
  68.3 8.3 %collective-permute-start.4 = (bf16[512,224]{1,0:T(8,128)(2,1)}, bf16[512,224]{1,0:T(8,128)(2,1)S(1)}, u32[]{:S(2)}, u32[]{:S(2)}) collective-permute-start(bf16[512,224]{1,0:T(8,128)(2,1)} %copy-done.13), channel_id=1, source_target_pairs={{0,7},{1,0},{2,1},{3,2},{4,3},{5,4},{6,5},{7,6},{8,15},{9,8},{10,9... | collective-permute-start | bytes 688136 | tf_op jit(solution)/shard_map/ppermute | solution.py:33
  74.9 14.8 %copy-start.14 = (bf16[512,224]{1,0:T(8,128)(2,1)}, bf16[512,224]{1,0:T(8,128)(2,1)S(1)}, u32[]{:S(2)}) copy-start(bf16[512,224]{1,0:T(8,128)(2,1)S(1)} %collective-permute-done.3.refs_3_) | copy-start | bytes 688132
  74.9 7.8 %collective-permute-start.5 = (bf16[512,224]{1,0:T(8,128)(2,1)S(1)}, bf16[512,224]{1,0:T(8,128)(2,1)S(1)}, u32[]{:S(2)}, u32[]{:S(2)}) collective-permute-start(bf16[512,224]{1,0:T(8,128)(2,1)S(1)} %collective-permute-done.3.refs_3_), channel_id=1, source_target_pairs={{0,1},{1,2},{2,3},{3,4},{4,5},{5,6},{6,7},{7,0},{8,9},{9,10},{10,1... | collective-permute-start | bytes 688136 | tf_op jit(solution)/shard_map/ppermute | solution.py:32
  76.6 13.1 %copy-start.15 = (bf16[512,224]{1,0:T(8,128)(2,1)}, bf16[512,224]{1,0:T(8,128)(2,1)S(1)}, u32[]{:S(2)}) copy-start(bf16[512,224]{1,0:T(8,128)(2,1)S(1)} %collective-permute-done.4.refs_4_) | copy-start | bytes 688132
  76.6 7.9 %collective-permute-start.6 = (bf16[512,224]{1,0:T(8,128)(2,1)S(1)}, bf16[512,224]{1,0:T(8,128)(2,1)S(1)}, u32[]{:S(2)}, u32[]{:S(2)}) collective-permute-start(bf16[512,224]{1,0:T(8,128)(2,1)S(1)} %collective-permute-done.4.refs_4_), channel_id=1, source_target_pairs={{0,7},{1,0},{2,1},{3,2},{4,3},{5,4},{6,5},{7,6},{8,15},{9,8},{10,9... | collective-permute-start | bytes 688136 | tf_op jit(solution)/shard_map/ppermute | solution.py:33
  82.7 7.0 %copy-start.9 = (bf16[512,224]{1,0:T(8,128)(2,1)}, bf16[512,224]{1,0:T(8,128)(2,1)S(1)}, u32[]{:S(2)}) copy-start(bf16[512,224]{1,0:T(8,128)(2,1)S(1)} %collective-permute-done.5.refs_5_) | copy-start | bytes 688132
  82.7 5.0 %collective-permute-start.7 = (bf16[256,224]{1,0:T(8,128)(2,1)S(1)}, bf16[256,224]{1,0:T(8,128)(2,1)S(1)}, u32[]{:S(2)}, u32[]{:S(2)}) collective-permute-start(bf16[256,224]{1,0:T(8,128)(2,1)S(1)} %slice.35), channel_id=1, source_target_pairs={{0,1},{1,2},{2,3},{3,4},{4,5},{5,6},{6,7},{7,0},{8,9},{9,10},{10,1... | collective-permute-start | bytes 344072 | tf_op jit(solution)/shard_map/ppermute | solution.py:32
  84.5 5.3 %copy-start.10 = (bf16[512,224]{1,0:T(8,128)(2,1)}, bf16[512,224]{1,0:T(8,128)(2,1)S(1)}, u32[]{:S(2)}) copy-start(bf16[512,224]{1,0:T(8,128)(2,1)S(1)} %collective-permute-done.6.refs_6_) | copy-start | bytes 688132
  84.5 5.2 %collective-permute-start.8 = (bf16[256,224]{1,0:T(8,128)(2,1)S(1)}, bf16[256,224]{1,0:T(8,128)(2,1)S(1)}, u32[]{:S(2)}, u32[]{:S(2)}) collective-permute-start(bf16[256,224]{1,0:T(8,128)(2,1)S(1)} %slice.36), channel_id=1, source_target_pairs={{0,7},{1,0},{2,1},{3,2},{4,3},{5,4},{6,5},{7,6},{8,15},{9,8},{10,9... | collective-permute-start | bytes 344072 | tf_op jit(solution)/shard_map/ppermute | solution.py:33
  87.8 2.0 %copy-start.16 = (bf16[256,224]{1,0:T(8,128)(2,1)}, bf16[256,224]{1,0:T(8,128)(2,1)S(1)}, u32[]{:S(2)}) copy-start(bf16[256,224]{1,0:T(8,128)(2,1)S(1)} %collective-permute-done.7.refs_7_) | copy-start | bytes 344068
  89.7 0.6 copy-start.17
  100.2 2.3 %copy-start.1 = (bf16[512,4608]{1,0:T(8,128)(2,1)S(1)}, bf16[512,4608]{1,0:T(8,128)(2,1)}, u32[]{:S(2)}) copy-start(bf16[512,4608]{1,0:T(8,128)(2,1)} %own_head.2) | copy-start | bytes 14155780
  102.5 1.0 copy-start.2
  103.6 1.0 copy-start.3
  104.6 7.3 %copy-start.23 = (f32[1,256]{1,0:T(1,128)S(1)}, f32[1,256]{1,0:T(1,128)}, u32[]{:S(2)}) copy-start(f32[1,256]{1,0:T(1,128)} %get-tuple-element.31) | copy-start | bytes 3076
  110.3 0.8 copy-start.4
  111.1 0.8 copy-start.5
  111.9 27.5 %copy-start.24 = (f32[512]{0:T(512)S(1)}, f32[512]{0:T(512)}, u32[]{:S(2)}) copy-start(f32[512]{0:T(512)} %param.19) | copy-start | bytes 6148
  112.8 26.5 %all-to-all-start.4 = ((f32[128,6,128]{2,1,0:T(8,128)}), f32[128,6,128]{2,1,0:T(8,128)S(1)}, u32[]{:S(2)}, u32[]{:S(2)}) async-start(f32[128,6,128]{2,1,0:T(8,128)} %broadcast_in_dim.14), calls=%async_computation.4 | async-start | bytes 1048576 | tf_op jit(solution)/shard_map/all_to_all | solution.py:26
  123.5 30.2 %collective-permute-start.11 = (bf16[256,3584]{1,0:T(8,128)(2,1)}, bf16[256,3584]{1,0:T(8,128)(2,1)}, u32[]{:S(2)}, u32[]{:S(2)}) collective-permute-start(bf16[256,3584]{1,0:T(8,128)(2,1)} %get-tuple-element.40), channel_id=1, source_target_pairs={{0,128},{128,0},{1,129},{129,1},{2,130},{130,2},{3,131},{131,3},{4... | collective-permute-start | bytes 5505032 | tf_op jit(solution)/shard_map/ppermute | solution.py:21
  147.2 3.8 %copy-start.25 = (bf16[512,256]{1,0:T(8,128)(2,1)S(1)}, bf16[512,256]{1,0:T(8,128)(2,1)}, u32[]{:S(2)}) copy-start(bf16[512,256]{1,0:T(8,128)(2,1)} %get-tuple-element.39) | copy-start | bytes 786436
  147.2 24.9 %all-to-all-start.5 = ((bf16[8,32,3584]{2,1,0:T(8,128)(2,1)}), bf16[8,32,3584]{2,1,0:T(8,128)(2,1)S(1)}, u32[]{:S(2)}, u32[]{:S(2)}) async-start(bf16[8,32,3584]{2,1,0:T(8,128)(2,1)} %bitcast.29), calls=%async_computation.5 | async-start | bytes 3670016 | tf_op jit(solution)/shard_map/all_to_all | solution.py:388
  151.1 2.5 %collective-permute-start.10 = (bf16[512,256]{1,0:T(8,128)(2,1)S(1)}, bf16[512,256]{1,0:T(8,128)(2,1)S(1)}, u32[]{:S(2)}, u32[]{:S(2)}) collective-permute-start(bf16[512,256]{1,0:T(8,128)(2,1)S(1)} %copy-done.25), channel_id=1, source_target_pairs={{0,128},{128,0},{1,129},{129,1},{2,130},{130,2},{3,131},{131,3},{4... | collective-permute-start | bytes 786440 | tf_op jit(solution)/shard_map/ppermute | solution.py:21
  159.1 21.4 %copy-start.11 = (bf16[512,256]{1,0:T(8,128)(2,1)S(1)}, bf16[512,256]{1,0:T(8,128)(2,1)}, u32[]{:S(2)}) copy-start(bf16[512,256]{1,0:T(8,128)(2,1)} %get-tuple-element.38) | copy-start | bytes 786436
  172.2 1.2 copy-start.6
  176.0 15.2 %all-to-all-start.6 = ((bf16[16,32,256]{2,1,0:T(8,128)(2,1)}), bf16[16,32,256]{2,1,0:T(8,128)(2,1)S(1)}, u32[]{:S(2)}, u32[]{:S(2)}) async-start(bf16[16,32,256]{2,1,0:T(8,128)(2,1)} %shard_map.125), calls=%async_computation.6 | async-start | bytes 524288 | tf_op jit(solution)/shard_map/all_to_all | solution.py:395
  180.6 11.6 %copy-start.18 = (bf16[32,224]{1,0:T(8,128)(2,1)S(1)}, bf16[32,224]{1,0:T(8,128)(2,1)}, u32[]{:S(2)}) copy-start(bf16[32,224]{1,0:T(8,128)(2,1)} %param.16) | copy-start | bytes 43012

commit v5 on v3

--- a/solution.py
+++ b/solution.py
@@ -13,6 +13,7 @@
 ROW = ("x", "yl")
 VOC = ("yh", "z")
 XY = ("x", "yl", "yh")
+PLANE = ("x", "yl", "yh", "z")
 bf16 = jnp.bfloat16
 f32 = jnp.float32
 
@@ -170,7 +171,9 @@
     )(gain, *blocks, own_head, other_head)
 
 
-def teacher_kernel(rows, own_head, other_head, own_tanh, other_tanh, own_exp, other_exp, sums):
+def teacher_kernel(
+    rows, own_head, other_head, own_tanh, other_tanh, student_sum, own_exp, other_exp, sums
+):
     total = jnp.zeros((1, rows.shape[0]), f32)
     mixed = jnp.zeros((1, rows.shape[0]), f32)
     for head, tanh, out in ((own_head, own_tanh, own_exp), (other_head, other_tanh, other_exp)):
@@ -179,10 +182,15 @@
         out[...] = grown
         total += jnp.sum(grown, axis=0, keepdims=True)
         mixed += jnp.sum(grown * (logit - softcap * tanh[...]), axis=0, keepdims=True)
-    sums[...] = jnp.concatenate([total, mixed], axis=0)
-
-
-def teacher_logits(rows, own_head, other_head, own_tanh, other_tanh):
+    pieces = [
+        row[:, i : i + 128]
+        for row in (total, mixed, student_sum[...])
+        for i in range(0, row.shape[1], 128)
+    ]
+    sums[...] = jnp.broadcast_to(jnp.concatenate(pieces, axis=0)[None], sums.shape)
+
+
+def teacher_logits(rows, own_head, other_head, own_tanh, other_tanh, student_sum, plane):
     count, width = own_head.shape
     tokens = rows.shape[0]
     vmem = pl.BlockSpec(memory_space=pltpu.VMEM)
@@ -191,9 +199,9 @@
         out_shape=(
             jax.ShapeDtypeStruct((count, tokens), f32),
             jax.ShapeDtypeStruct((count, tokens), f32),
-            jax.ShapeDtypeStruct((2, tokens), f32),
-        ),
-        in_specs=[vmem] * 5,
+            jax.ShapeDtypeStruct((plane, 3 * tokens // 128, 128), f32),
+        ),
+        in_specs=[vmem] * 6,
         out_specs=(vmem, vmem, vmem),
         compiler_params=pltpu.CompilerParams(vmem_limit_bytes=12 * 2**20),
         cost_estimate=pl.CostEstimate(
@@ -201,11 +209,11 @@
             bytes_accessed=4 * count * width,
             transcendentals=4 * count * tokens,
         ),
-    )(rows, own_head, other_head, own_tanh, other_tanh)
+    )(rows, own_head, other_head, own_tanh, other_tanh, student_sum)
 
 
 def gradient_kernel(
-    own_exp, other_exp, own_tanh, other_tanh, scales, own_head, other_head,
+    own_exp, other_exp, own_tanh, other_tanh, sums, weight, own_head, other_head,
     own_grad, other_grad, terms, held, turned, sem,
 ):
     count = own_exp.shape[0]
@@ -220,12 +228,18 @@
                 )
             )
             copies[-1].start()
+    totals = jnp.sum(sums[...], axis=0)
+    each = totals.shape[0] // 3
+    teacher_total = jnp.concatenate([totals[k : k + 1] for k in range(each)], axis=1)
+    student_total = jnp.concatenate([totals[k : k + 1] for k in range(2 * each, 3 * each)], axis=1)
+    student_factor = weight[...] / student_total
+    teacher_factor = weight[...] / teacher_total
     for start, exps, tanhs, grads in (
         (0, own_exp, own_tanh, own_grad),
         (count, other_exp, other_tanh, other_grad),
     ):
         student = tanhs[...]
-        grad = (jnp.exp(softcap * student) * scales[0:1, :] - exps[...] * scales[1:2, :]) * (
+        grad = (jnp.exp(softcap * student) * student_factor - exps[...] * teacher_factor) * (
             1.0 - student * student
         )
         grads[...] = grad.astype(bf16)
@@ -238,7 +252,7 @@
         ).astype(bf16)
 
 
-def gradient_terms(own_exp, other_exp, own_tanh, other_tanh, scales, own_head, other_head):
+def gradient_terms(own_exp, other_exp, own_tanh, other_tanh, sums, weight, own_head, other_head):
     count, tokens = own_exp.shape
     width = own_head.shape[1]
     block = 512
@@ -251,7 +265,7 @@
             jax.ShapeDtypeStruct((count, tokens), bf16),
             jax.ShapeDtypeStruct((tokens, width), bf16),
         ),
-        in_specs=[vmem] * 5 + [anywhere] * 2,
+        in_specs=[vmem] * 6 + [anywhere] * 2,
         out_specs=(vmem, vmem, vmem),
         scratch_shapes=[
             pltpu.VMEM((width // block, 2 * count, block), bf16),
@@ -264,7 +278,7 @@
             bytes_accessed=4 * count * width + 20 * count * tokens,
             transcendentals=2 * count * tokens,
         ),
-    )(own_exp, other_exp, own_tanh, other_tanh, scales, own_head, other_head)
+    )(own_exp, other_exp, own_tanh, other_tanh, sums, weight, own_head, other_head)
 
 
 def reduced_kernel(parts, normed, out):
@@ -358,21 +372,26 @@
         rows, student_gain[None], ring, student_head, student_other
     )
     own_scale = lax.dynamic_slice_in_dim(student_scale[:, 0], row_index * rows, rows)
-    exp_mine, exp_others, teacher_sums = teacher_logits(
-        teacher_all, teacher_head, teacher_other, tanh_mine, tanh_others
-    )
-    sums = jnp.concatenate([teacher_sums, student_sum]).reshape(-1, 128)
+    exp_mine, exp_others, sums = teacher_logits(
+        teacher_all,
+        teacher_head,
+        teacher_other,
+        tanh_mine,
+        tanh_others,
+        student_sum,
+        lax.axis_size(PLANE),
+    )
     sums, student_tied = lax.optimization_barrier((sums, student_all))
     student_all_other = swap(student_tied)
-    totals = jnp.sum(spread(sums, ("x", "yl", "yh", "z")), axis=0).reshape(3, half)
+    sums = lax.all_to_all(sums, PLANE, 0, 0)
+    totals = jnp.sum(sums, axis=0).reshape(3, half)
     teacher_total, mixed, student_total = totals[0], totals[1], totals[2]
     token_kl = mixed / teacher_total + jnp.log(student_total) - jnp.log(teacher_total)
     token_kl = lax.dynamic_slice_in_dim(token_kl, row_index * rows + voc_index * own, own)
     weight = lax.dynamic_slice_in_dim(kl_weight, half_start, half)
-    scales = jnp.stack([weight / student_total, weight / teacher_total])
 
     grad_mine, grad_others, terms = gradient_terms(
-        exp_mine, exp_others, tanh_mine, tanh_others, scales, student_head, student_other
+        exp_mine, exp_others, tanh_mine, tanh_others, sums, weight[None], student_head, student_other
     )
     grad_back = swap(grad_others)
     parts = lax.all_to_all(terms.reshape(row_count, rows, student_width), ROW, 0, 0)

time: 194 us -> 195 us (level)
  local copies, waits for them, and re-layouts: 17.7 us -> 23.1 us
  waiting for transfers between devices: 63.9 us -> 59.1 us
    all_to_all x3 -> x2, waiting for transfers between devices: 21.5 us -> 3.81 us  [spread(): lax.all_to_all(jnp.broadcast_to(value[None], (count, *value.shape)), axes...]
    all_to_all x0 -> x1, waiting for transfers between devices: none -> 14.4 us  [local(): sums = lax.all_to_all(sums, PLANE, 0, 0)]
    all_to_all x0 -> x1, starting transfers between devices: none -> 11.3 us  [local(): sums = lax.all_to_all(sums, PLANE, 0, 0)]
    all_to_all x3 -> x2, starting transfers between devices: 21.4 us -> 11.1 us  [spread(): lax.all_to_all(jnp.broadcast_to(value[None], (count, *value.shape)), axes...]
    unnamed x52 -> x50, local copies, waits for them, and re-layouts: 8.64 us -> 10.9 us
  transfers between devices with their start and end apart: 18 -> 18, of which waited for: 9 -> 9; matrix products, arithmetic and copies ran while one was open for 12% -> 13% of each run, Pallas kernels for 10% -> 10%
where the time goes in v5:
time: 195 us; the launch traced here: 194 us
  waiting for transfers between devices  59.1 us (30%)
  starting transfers between devices  49.3 us (25%)
  Pallas kernels  27 us (14%)
  local copies, waits for them, and re-layouts  23.1 us (12%)
  blocking collectives  18.9 us (10%)
  matrix products  13.2 us (7%)
    all_to_all x1, blocking collectives, local(): lax.all_to_all(teacher_rows, VOC, 0, 0).reshape(rows, teacher_width)  18.9 us
    all_to_all x1, waiting for transfers between devices, local(): sums = lax.all_to_all(sums, PLANE, 0, 0)  14.4 us
    ppermute x4, waiting for transfers between devices, ring_step(): lax.ppermute(right, 'z', [(i, (i + 1) % count) for i in range(count)])  12.8 us
    all_to_all x1, waiting for transfers between devices, local(): lax.all_to_all(terms.reshape(row_count, rows, student_width), ROW, 0, 0)  11.5 us
    all_to_all x1, starting transfers between devices, local(): sums = lax.all_to_all(sums, PLANE, 0, 0)  11.3 us
    all_to_all x2, starting transfers between devices, spread(): lax.all_to_all(jnp.broadcast_to(value[None], (count, *value.shape)), axes...  11.1 us
    unnamed x50, local copies, waits for them, and re-layouts  10.9 us
    all_to_all x1, waiting for transfers between devices, local(): got = lax.all_to_all(sent, VOC, 0, 0)  10.4 us
  transfers between devices with their start and end apart: 18, of which 9 were waited for; matrix products, arithmetic and copies ran while one was open for 13% of the time, Pallas kernels for 10%

profile of v5, /device:TPU:32, one launch (start us, length us, event | category | flops | bytes accessed | tf_op | source)
XLA Modules:
  0.0 193.5 jit_solution(11286769332798451372)
XLA Ops:
  1.2 1.5 broadcast_in_dim.11
  2.7 7.0 %all-to-all-start.1 = ((bf16[16,32,224]{2,1,0:T(8,128)(2,1)}), bf16[16,32,224]{2,1,0:T(8,128)(2,1)S(1)}, u32[]{:S(2)}, u32[]{:S(2)}) async-start(bf16[16,32,224]{2,1,0:T(8,128)(2,1)} %broadcast_in_dim.11), calls=%async_computation.1 | async-start | bytes 524288 | tf_op jit(solution)/shard_map/all_to_all | solution.py:27
  9.7 0.7 concatenate.27
  10.4 0.7 concatenate.28
  11.1 0.8 reshape.113
  11.9 1.0 convolution_convert_fusion
  13.1 1.9 concatenate.30
  15.0 3.8 %all-to-all-done.1 = bf16[16,32,224]{2,1,0:T(8,128)(2,1)S(1)} async-done(((bf16[16,32,224]{2,1,0:T(8,128)(2,1)}), bf16[16,32,224]{2,1,0:T(8,128)(2,1)S(1)}, u32[]{:S(2)}, u32[]{:S(2)}) %all-to-all-start.1) | async-done | bytes 229408 | tf_op jit(solution)/shard_map/all_to_all | solution.py:27
  18.8 8.8 %all-to-all-start = ((bf16[16,2,5472]{2,1,0:T(2,128)(2,1)}), bf16[16,2,5472]{2,1,0:T(2,128)(2,1)S(1)}, u32[]{:S(2)}, u32[]{:S(2)}) async-start(bf16[16,2,5472]{2,1,0:T(2,128)(2,1)} %concatenate.30), calls=%async_computation | async-start | bytes 704512 | tf_op jit(solution)/shard_map/all_to_all | solution.py:356
  27.8 1.8 collective-permute-start
  29.7 10.4 %all-to-all-done.got = bf16[16,2,5472]{2,1,0:T(2,128)(2,1)S(1)} async-done(((bf16[16,2,5472]{2,1,0:T(2,128)(2,1)}), bf16[16,2,5472]{2,1,0:T(2,128)(2,1)S(1)}, u32[]{:S(2)}, u32[]{:S(2)}) %all-to-all-start) | async-done | bytes 350240 | tf_op jit(solution)/shard_map/all_to_all | solution.py:356
  40.1 0.7 copy-done.11
  40.8 2.1 %shard_map.121 = bf16[16,2,4608]{2,1,0:T(2,128)(2,1)} custom-call(bf16[16,2,5472]{2,1,0:T(2,128)(2,1)} %copy-done.11), custom_call_target="tpu_custom_call" | custom-call | flops 175104 | bytes 700416 | tf_op jit(solution)/shard_map/pallas_call | solution.py:70
  42.9 18.9 %all_to_all.35 = bf16[16,2,4608]{2,1,0:T(2,128)(2,1)S(1)} all-to-all(bf16[16,2,4608]{2,1,0:T(2,128)(2,1)} %shard_map.121), channel_id=1, replica_groups=mesh['c'=2,'x'=4,'yl'=2,'yh'=2,'z'=8] {'yh','z'}, dimensions={0} | all-to-all | bytes 589824 | tf_op jit(solution)/shard_map/all_to_all | solution.py:360
  61.9 1.6 broadcast_in_dim.12
  63.5 4.1 %all-to-all-start.3 = ((bf16[8,32,4608]{2,1,0:T(8,128)(2,1)}), bf16[8,32,4608]{2,1,0:T(8,128)(2,1)S(1)}, u32[]{:S(2)}, u32[]{:S(2)}) async-start(bf16[8,32,4608]{2,1,0:T(8,128)(2,1)} %broadcast_in_dim.12), calls=%async_computation.3 | async-start | bytes 4718592 | tf_op jit(solution)/shard_map/all_to_all | solution.py:27
  67.6 1.0 collective-permute-start.3
  68.7 1.0 collective-permute-start.4
  69.7 5.4 %collective-permute-done.3.refs_3_ = bf16[512,224]{1,0:T(8,128)(2,1)S(1)} collective-permute-done((bf16[512,224]{1,0:T(8,128)(2,1)}, bf16[512,224]{1,0:T(8,128)(2,1)S(1)}, u32[]{:S(2)}, u32[]{:S(2)}) %collective-permute-start.3) | collective-permute-done | bytes 229408 | tf_op jit(solution)/shard_map/ppermute | solution.py:33
  75.1 1.9 collective-permute-start.5
  77.4 5.5 %collective-permute-done.5.refs_5_ = bf16[512,224]{1,0:T(8,128)(2,1)S(1)} collective-permute-done((bf16[512,224]{1,0:T(8,128)(2,1)S(1)}, bf16[512,224]{1,0:T(8,128)(2,1)S(1)}, u32[]{:S(2)}, u32[]{:S(2)}) %collective-permute-start.5) | collective-permute-done | bytes 229408 | tf_op jit(solution)/shard_map/ppermute | solution.py:33
  82.9 1.9 collective-permute-start.7
  86.1 1.9 collective-permute-done.7.refs_7_
  87.9 2.1 %collective-permute-done.8.refs_8_ = bf16[256,224]{1,0:T(8,128)(2,1)S(1)} collective-permute-done((bf16[256,224]{1,0:T(8,128)(2,1)S(1)}, bf16[256,224]{1,0:T(8,128)(2,1)S(1)}, u32[]{:S(2)}, u32[]{:S(2)}) %collective-permute-start.8) | collective-permute-done | bytes 114720 | tf_op jit(solution)/shard_map/ppermute | solution.py:34
  90.7 9.8 %shard_map.122 = (bf16[256,3584]{1,0:T(8,128)(2,1)}, f32[256,1]{1,0:T(8,128)}, f32[512,256]{1,0:T(8,128)}, f32[512,256]{1,0:T(8,128)}, f32[1,256]{1,0:T(1,128)}) custom-call(f32[1,3584]{1,0:T(1,128)} %broadcast_in_dim.13.gain, bf16[512,224]{1,0:T(8,128)(2,1)} %bitcast.16, bf16[512,224]{1,0:T(8,128)(2,1)} %copy-done.17, bf16[512,224]{1,0:T(8,128)(2,1)} %copy-done.16, ...), custom_call_target="tpu_custom_call" | custom-call | flops 1879048192 | bytes 7340032 | tf_op jit(solution)/shard_map/pallas_call | solution.py:146
  100.6 2.3 %copy-done.1 = bf16[512,4608]{1,0:T(8,128)(2,1)S(1)} copy-done((bf16[512,4608]{1,0:T(8,128)(2,1)S(1)}, bf16[512,4608]{1,0:T(8,128)(2,1)}, u32[]{:S(2)}) %copy-start.1) | copy-done | bytes 4718616
  102.9 1.0 copy-done.2
  103.9 1.0 copy-done.3
  105.7 5.2 %shard_map.123 = (f32[512,256]{1,0:T(8,128)S(1)}, f32[512,256]{1,0:T(8,128)S(1)}, f32[128,6,128]{2,1,0:T(8,128)S(1)}) custom-call(bf16[256,4608]{1,0:T(8,128)(2,1)S(1)} %bitcast.12, bf16[512,4608]{1,0:T(8,128)(2,1)S(1)} %copy-done.1, bf16[512,4608]{1,0:T(8,128)(2,1)} %collective-permute-done.2.other_head, f32[512,256]{1,0:T(8,128)S(1)} %copy-done.2, ...), custom_call_target="tpu_custom_call" | custom-call | flops 2415919104 | bytes 9437184 | tf_op jit(solution)/shard_map/pallas_call | solution.py:197
  110.9 0.8 copy-done.4
  111.7 0.8 copy-done.5
  112.5 0.8 copy-done.6
  113.3 11.3 %all-to-all-start.4 = ((f32[128,6,128]{2,1,0:T(8,128)}), f32[128,6,128]{2,1,0:T(8,128)S(1)}, u32[]{:S(2)}, u32[]{:S(2)}) async-start(f32[128,6,128]{2,1,0:T(8,128)} %copy-done.6), calls=%async_computation.4 | async-start | bytes 1048576 | tf_op jit(solution)/shard_map/all_to_all | solution.py:386
  124.7 1.3 dynamic_slice.18
  126.0 14.4 %all-to-all-done.4.sums = f32[128,6,128]{2,1,0:T(8,128)S(1)} async-done(((f32[128,6,128]{2,1,0:T(8,128)}), f32[128,6,128]{2,1,0:T(8,128)S(1)}, u32[]{:S(2)}, u32[]{:S(2)}) %all-to-all-start.4) | async-done | bytes 393248 | tf_op jit(solution)/shard_map/all_to_all | solution.py:386
  140.4 0.8 copy-done.9
  141.2 7.3 %shard_map.124 = (bf16[512,256]{1,0:T(8,128)(2,1)}, bf16[512,256]{1,0:T(8,128)(2,1)}, bf16[256,3584]{1,0:T(8,128)(2,1)}) custom-call(f32[512,256]{1,0:T(8,128)} %copy-done.4, f32[512,256]{1,0:T(8,128)} %copy-done.5, f32[512,256]{1,0:T(8,128)} %get-tuple-element.28.own_tanh, f32[512,256]{1,0:T(8,128)} %get-tuple-element.29.other_tanh, ...), custom_call_target="tpu_custom_call" | custom-call | flops 1879048192 | bytes 9961472 | tf_op jit(solution)/shard_map/pallas_call | solution.py:261
  148.6 3.7 %all-to-all-start.5 = ((bf16[8,32,3584]{2,1,0:T(8,128)(2,1)}), bf16[8,32,3584]{2,1,0:T(8,128)(2,1)S(1)}, u32[]{:S(2)}, u32[]{:S(2)}) async-start(bf16[8,32,3584]{2,1,0:T(8,128)(2,1)} %bitcast.13), calls=%async_computation.5 | async-start | bytes 3670016 | tf_op jit(solution)/shard_map/all_to_all | solution.py:397
  153.0 1.7 constant_dynamic-slice_fusion.normed
  155.4 5.6 %fusion.6 = f32[512,3584]{1,0:T(8,128)} fusion(bf16[512,256]{1,0:T(8,128)(2,1)} %collective-permute-done.10, bf16[256,3584]{1,0:T(8,128)(2,1)} %collective-permute-done.11), kind=kOutput, calls=%fused_computation.19 | convolution fusion | flops 939524096 | bytes 9437184 | tf_op jit(solution)/shard_map/dot_general | solution.py:400
  161.0 11.5 %all-to-all-done.5.parts = bf16[8,32,3584]{2,1,0:T(8,128)(2,1)S(1)} async-done(((bf16[8,32,3584]{2,1,0:T(8,128)(2,1)}), bf16[8,32,3584]{2,1,0:T(8,128)(2,1)S(1)}, u32[]{:S(2)}, u32[]{:S(2)}) %all-to-all-start.5) | async-done | bytes 1835040 | tf_op jit(solution)/shard_map/all_to_all | solution.py:397
  172.6 1.2 copy-done.8
  173.8 2.6 %shard_map.125 = bf16[16,32,256]{2,1,0:T(8,128)(2,1)} custom-call(bf16[8,32,3584]{2,1,0:T(8,128)(2,1)} %copy-done.8, bf16[32,3584]{1,0:T(8,128)(2,1)} %constant_dynamic-slice_fusion.normed), custom_call_target="tpu_custom_call" | custom-call | flops 917504 | bytes 1835008 | tf_op jit(solution)/shard_map/pallas_call | solution.py:302
  176.4 4.8 %all-to-all-start.6 = ((bf16[16,32,256]{2,1,0:T(8,128)(2,1)}), bf16[16,32,256]{2,1,0:T(8,128)(2,1)S(1)}, u32[]{:S(2)}, u32[]{:S(2)}) async-start(bf16[16,32,256]{2,1,0:T(8,128)(2,1)} %shard_map.125), calls=%async_computation.6 | async-start | bytes 524288 | tf_op jit(solution)/shard_map/all_to_all | solution.py:404
  181.2 6.6 %add_convert_fusion = bf16[512,3584]{1,0:T(8,128)(2,1)} fusion(f32[512,3584]{1,0:T(8,128)} %fusion.6, bf16[512,256]{1,0:T(8,128)(2,1)S(1)} %copy-done.15, bf16[256,3584]{1,0:T(8,128)(2,1)} %get-tuple-element.40), kind=kOutput, calls=%fused_computation | convolution fusion | flops 943194112 | bytes 13107200 | tf_op jit(solution)/shard_map/dot_general | solution.py:399
  187.8 4.0 %all-to-all-done.6 = bf16[16,32,256]{2,1,0:T(8,128)(2,1)S(1)} async-done(((bf16[16,32,256]{2,1,0:T(8,128)(2,1)}), bf16[16,32,256]{2,1,0:T(8,128)(2,1)S(1)}, u32[]{:S(2)}, u32[]{:S(2)}) %all-to-all-start.6) | async-done | bytes 262176 | tf_op jit(solution)/shard_map/all_to_all | solution.py:404
  191.9 0.9 dynamic-slice_reduce_fusion
  192.8 0.7 fusion.1
  (70 shorter events, 5.7 us)
Async XLA Ops:
  0.6 11.2 %copy-start = (bf16[128,4608]{1,0:T(8,128)(2,1)S(1)}, bf16[128,4608]{1,0:T(8,128)(2,1)}, u32[]{:S(2)}) copy-start(bf16[128,4608]{1,0:T(8,128)(2,1)} %param.12) | copy-start | bytes 3538948
  0.6 99.9 %collective-permute-start.2 = (bf16[512,4608]{1,0:T(8,128)(2,1)}, bf16[512,4608]{1,0:T(8,128)(2,1)}, u32[]{:S(2)}, u32[]{:S(2)}) collective-permute-start(bf16[512,4608]{1,0:T(8,128)(2,1)} %own_head.2), channel_id=1, source_target_pairs={{0,128},{128,0},{1,129},{129,1},{2,130},{130,2},{3,131},{131,3},{4... | collective-permute-start | bytes 14155784 | tf_op jit(solution)/shard_map/ppermute | solution.py:22
  0.7 89.3 %collective-permute-start.9 = (bf16[512,3584]{1,0:T(8,128)(2,1)}, bf16[512,3584]{1,0:T(8,128)(2,1)}, u32[]{:S(2)}, u32[]{:S(2)}) collective-permute-start(bf16[512,3584]{1,0:T(8,128)(2,1)} %own_head.3), channel_id=1, source_target_pairs={{0,128},{128,0},{1,129},{129,1},{2,130},{130,2},{3,131},{131,3},{4... | collective-permute-start | bytes 11010056 | tf_op jit(solution)/shard_map/ppermute | solution.py:22
  2.7 16.1 %all-to-all-start.1 = ((bf16[16,32,224]{2,1,0:T(8,128)(2,1)}), bf16[16,32,224]{2,1,0:T(8,128)(2,1)S(1)}, u32[]{:S(2)}, u32[]{:S(2)}) async-start(bf16[16,32,224]{2,1,0:T(8,128)(2,1)} %broadcast_in_dim.11), calls=%async_computation.1 | async-start | bytes 524288 | tf_op jit(solution)/shard_map/all_to_all | solution.py:27
  18.8 44.7 %copy-start.12 = (bf16[16,32,224]{2,1,0:T(8,128)(2,1)}, bf16[16,32,224]{2,1,0:T(8,128)(2,1)S(1)}, u32[]{:S(2)}) copy-start(bf16[16,32,224]{2,1,0:T(8,128)(2,1)S(1)} %all-to-all-done.1) | copy-start | bytes 688132
  18.8 21.3 %all-to-all-start = ((bf16[16,2,5472]{2,1,0:T(2,128)(2,1)}), bf16[16,2,5472]{2,1,0:T(2,128)(2,1)S(1)}, u32[]{:S(2)}, u32[]{:S(2)}) async-start(bf16[16,2,5472]{2,1,0:T(2,128)(2,1)} %concatenate.30), calls=%async_computation | async-start | bytes 704512 | tf_op jit(solution)/shard_map/all_to_all | solution.py:356
  27.6 15.3 %collective-permute-start.1 = (bf16[512,224]{1,0:T(8,128)(2,1)S(1)}, bf16[512,224]{1,0:T(8,128)(2,1)S(1)}, u32[]{:S(2)}, u32[]{:S(2)}) collective-permute-start(bf16[512,224]{1,0:T(8,128)(2,1)S(1)} %bitcast.14), channel_id=1, source_target_pairs={{0,7},{1,0},{2,1},{3,2},{4,3},{5,4},{6,5},{7,6},{8,15},{9,8},{10,9... | collective-permute-start | bytes 688136 | tf_op jit(solution)/shard_map/ppermute | solution.py:34
  27.8 15.1 %collective-permute-start = (bf16[512,224]{1,0:T(8,128)(2,1)S(1)}, bf16[512,224]{1,0:T(8,128)(2,1)S(1)}, u32[]{:S(2)}, u32[]{:S(2)}) collective-permute-start(bf16[512,224]{1,0:T(8,128)(2,1)S(1)} %bitcast.15), channel_id=1, source_target_pairs={{0,1},{1,2},{2,3},{3,4},{4,5},{5,6},{6,7},{7,0},{8,9},{9,10},{10,1... | collective-permute-start | bytes 688136 | tf_op jit(solution)/shard_map/ppermute | solution.py:33
  40.1 0.7 copy-start.11
  42.9 20.6 %copy-start.16 = (bf16[512,224]{1,0:T(8,128)(2,1)}, bf16[512,224]{1,0:T(8,128)(2,1)S(1)}, u32[]{:S(2)}) copy-start(bf16[512,224]{1,0:T(8,128)(2,1)S(1)} %collective-permute-done.1.refs_2_) | copy-start | bytes 688132
  42.9 20.6 %copy-start.17 = (bf16[512,224]{1,0:T(8,128)(2,1)}, bf16[512,224]{1,0:T(8,128)(2,1)S(1)}, u32[]{:S(2)}) copy-start(bf16[512,224]{1,0:T(8,128)(2,1)S(1)} %collective-permute-done.refs_1_) | copy-start | bytes 688132
  63.5 21.9 %copy-start.23 = (f32[3584]{0:T(1024)S(1)}, f32[3584]{0:T(1024)}, u32[]{:S(2)}) copy-start(f32[3584]{0:T(1024)} %param.17) | copy-start | bytes 43012
  63.5 37.0 %all-to-all-start.3 = ((bf16[8,32,4608]{2,1,0:T(8,128)(2,1)}), bf16[8,32,4608]{2,1,0:T(8,128)(2,1)S(1)}, u32[]{:S(2)}, u32[]{:S(2)}) async-start(bf16[8,32,4608]{2,1,0:T(8,128)(2,1)} %broadcast_in_dim.12), calls=%async_computation.3 | async-start | bytes 4718592 | tf_op jit(solution)/shard_map/all_to_all | solution.py:27
  67.6 7.5 %collective-permute-start.3 = (bf16[512,224]{1,0:T(8,128)(2,1)}, bf16[512,224]{1,0:T(8,128)(2,1)S(1)}, u32[]{:S(2)}, u32[]{:S(2)}) collective-permute-start(bf16[512,224]{1,0:T(8,128)(2,1)} %copy-done.17), channel_id=1, source_target_pairs={{0,1},{1,2},{2,3},{3,4},{4,5},{5,6},{6,7},{7,0},{8,9},{9,10},{10,1... | collective-permute-start | bytes 688136 | tf_op jit(solution)/shard_map/ppermute | solution.py:33
  68.7 8.3 %collective-permute-start.4 = (bf16[512,224]{1,0:T(8,128)(2,1)}, bf16[512,224]{1,0:T(8,128)(2,1)S(1)}, u32[]{:S(2)}, u32[]{:S(2)}) collective-permute-start(bf16[512,224]{1,0:T(8,128)(2,1)} %copy-done.16), channel_id=1, source_target_pairs={{0,7},{1,0},{2,1},{3,2},{4,3},{5,4},{6,5},{7,6},{8,15},{9,8},{10,9... | collective-permute-start | bytes 688136 | tf_op jit(solution)/shard_map/ppermute | solution.py:34
  75.1 15.0 %copy-start.18 = (bf16[512,224]{1,0:T(8,128)(2,1)}, bf16[512,224]{1,0:T(8,128)(2,1)S(1)}, u32[]{:S(2)}) copy-start(bf16[512,224]{1,0:T(8,128)(2,1)S(1)} %collective-permute-done.3.refs_3_) | copy-start | bytes 688132
  75.1 7.8 %collective-permute-start.5 = (bf16[512,224]{1,0:T(8,128)(2,1)S(1)}, bf16[512,224]{1,0:T(8,128)(2,1)S(1)}, u32[]{:S(2)}, u32[]{:S(2)}) collective-permute-start(bf16[512,224]{1,0:T(8,128)(2,1)S(1)} %collective-permute-done.3.refs_3_), channel_id=1, source_target_pairs={{0,1},{1,2},{2,3},{3,4},{4,5},{5,6},{6,7},{7,0},{8,9},{9,10},{10,1... | collective-permute-start | bytes 688136 | tf_op jit(solution)/shard_map/ppermute | solution.py:33
  77.0 13.1 %copy-start.19 = (bf16[512,224]{1,0:T(8,128)(2,1)}, bf16[512,224]{1,0:T(8,128)(2,1)S(1)}, u32[]{:S(2)}) copy-start(bf16[512,224]{1,0:T(8,128)(2,1)S(1)} %collective-permute-done.4.refs_4_) | copy-start | bytes 688132
  77.0 7.9 %collective-permute-start.6 = (bf16[512,224]{1,0:T(8,128)(2,1)S(1)}, bf16[512,224]{1,0:T(8,128)(2,1)S(1)}, u32[]{:S(2)}, u32[]{:S(2)}) collective-permute-start(bf16[512,224]{1,0:T(8,128)(2,1)S(1)} %collective-permute-done.4.refs_4_), channel_id=1, source_target_pairs={{0,7},{1,0},{2,1},{3,2},{4,3},{5,4},{6,5},{7,6},{8,15},{9,8},{10,9... | collective-permute-start | bytes 688136 | tf_op jit(solution)/shard_map/ppermute | solution.py:34
  82.9 7.2 %copy-start.13 = (bf16[512,224]{1,0:T(8,128)(2,1)}, bf16[512,224]{1,0:T(8,128)(2,1)S(1)}, u32[]{:S(2)}) copy-start(bf16[512,224]{1,0:T(8,128)(2,1)S(1)} %collective-permute-done.5.refs_5_) | copy-start | bytes 688132
  82.9 5.0 %collective-permute-start.7 = (bf16[256,224]{1,0:T(8,128)(2,1)S(1)}, bf16[256,224]{1,0:T(8,128)(2,1)S(1)}, u32[]{:S(2)}, u32[]{:S(2)}) collective-permute-start(bf16[256,224]{1,0:T(8,128)(2,1)S(1)} %slice.35), channel_id=1, source_target_pairs={{0,1},{1,2},{2,3},{3,4},{4,5},{5,6},{6,7},{7,0},{8,9},{9,10},{10,1... | collective-permute-start | bytes 344072 | tf_op jit(solution)/shard_map/ppermute | solution.py:33
  84.8 5.3 %copy-start.14 = (bf16[512,224]{1,0:T(8,128)(2,1)}, bf16[512,224]{1,0:T(8,128)(2,1)S(1)}, u32[]{:S(2)}) copy-start(bf16[512,224]{1,0:T(8,128)(2,1)S(1)} %collective-permute-done.6.refs_6_) | copy-start | bytes 688132
  84.8 5.2 %collective-permute-start.8 = (bf16[256,224]{1,0:T(8,128)(2,1)S(1)}, bf16[256,224]{1,0:T(8,128)(2,1)S(1)}, u32[]{:S(2)}, u32[]{:S(2)}) collective-permute-start(bf16[256,224]{1,0:T(8,128)(2,1)S(1)} %slice.36), channel_id=1, source_target_pairs={{0,7},{1,0},{2,1},{3,2},{4,3},{5,4},{6,5},{7,6},{8,15},{9,8},{10,9... | collective-permute-start | bytes 344072 | tf_op jit(solution)/shard_map/ppermute | solution.py:34
  87.9 2.2 %copy-start.20 = (bf16[256,224]{1,0:T(8,128)(2,1)}, bf16[256,224]{1,0:T(8,128)(2,1)S(1)}, u32[]{:S(2)}) copy-start(bf16[256,224]{1,0:T(8,128)(2,1)S(1)} %collective-permute-done.7.refs_7_) | copy-start | bytes 344068
  90.1 0.6 copy-start.21
  100.6 2.3 %copy-start.1 = (bf16[512,4608]{1,0:T(8,128)(2,1)S(1)}, bf16[512,4608]{1,0:T(8,128)(2,1)}, u32[]{:S(2)}) copy-start(bf16[512,4608]{1,0:T(8,128)(2,1)} %own_head.2) | copy-start | bytes 14155780
  102.9 1.0 copy-start.2
  103.9 1.0 copy-start.3
  105.0 0.7 copy-start.7
  110.8 0.8 copy-start.4
  111.7 0.8 copy-start.5
  112.5 0.8 copy-start.6
  113.3 27.2 %all-to-all-start.4 = ((f32[128,6,128]{2,1,0:T(8,128)}), f32[128,6,128]{2,1,0:T(8,128)S(1)}, u32[]{:S(2)}, u32[]{:S(2)}) async-start(f32[128,6,128]{2,1,0:T(8,128)} %copy-done.6), calls=%async_computation.4 | async-start | bytes 1048576 | tf_op jit(solution)/shard_map/all_to_all | solution.py:386
  124.6 30.9 %collective-permute-start.11 = (bf16[256,3584]{1,0:T(8,128)(2,1)}, bf16[256,3584]{1,0:T(8,128)(2,1)}, u32[]{:S(2)}, u32[]{:S(2)}) collective-permute-start(bf16[256,3584]{1,0:T(8,128)(2,1)} %get-tuple-element.40), channel_id=1, source_target_pairs={{0,128},{128,0},{1,129},{129,1},{2,130},{130,2},{3,131},{131,3},{4... | collective-permute-start | bytes 5505032 | tf_op jit(solution)/shard_map/ppermute | solution.py:22
  140.4 0.8 copy-start.9
  148.6 6.1 %copy-start.10 = (f32[128,6,128]{2,1,0:T(8,128)S(1)}, f32[128,6,128]{2,1,0:T(8,128)}, u32[]{:S(2)}) copy-start(f32[128,6,128]{2,1,0:T(8,128)} %copy-done.9) | copy-start | bytes 1179652
  148.6 24.0 %all-to-all-start.5 = ((bf16[8,32,3584]{2,1,0:T(8,128)(2,1)}), bf16[8,32,3584]{2,1,0:T(8,128)(2,1)S(1)}, u32[]{:S(2)}, u32[]{:S(2)}) async-start(bf16[8,32,3584]{2,1,0:T(8,128)(2,1)} %bitcast.13), calls=%async_computation.5 | async-start | bytes 3670016 | tf_op jit(solution)/shard_map/all_to_all | solution.py:397
  153.0 2.4 %collective-permute-start.10 = (bf16[512,256]{1,0:T(8,128)(2,1)}, bf16[512,256]{1,0:T(8,128)(2,1)}, u32[]{:S(2)}, u32[]{:S(2)}) collective-permute-start(bf16[512,256]{1,0:T(8,128)(2,1)} %get-tuple-element.39), channel_id=1, source_target_pairs={{0,128},{128,0},{1,129},{129,1},{2,130},{130,2},{3,131},{131,3},{4... | collective-permute-start | bytes 786440 | tf_op jit(solution)/shard_map/ppermute | solution.py:22
  161.0 20.2 %copy-start.15 = (bf16[512,256]{1,0:T(8,128)(2,1)S(1)}, bf16[512,256]{1,0:T(8,128)(2,1)}, u32[]{:S(2)}) copy-start(bf16[512,256]{1,0:T(8,128)(2,1)} %get-tuple-element.38) | copy-start | bytes 786436
  172.6 1.2 copy-start.8
  176.4 15.4 %all-to-all-start.6 = ((bf16[16,32,256]{2,1,0:T(8,128)(2,1)}), bf16[16,32,256]{2,1,0:T(8,128)(2,1)S(1)}, u32[]{:S(2)}, u32[]{:S(2)}) async-start(bf16[16,32,256]{2,1,0:T(8,128)(2,1)} %shard_map.125), calls=%async_computation.6 | async-start | bytes 524288 | tf_op jit(solution)/shard_map/all_to_all | solution.py:404
  181.2 11.6 %copy-start.22 = (bf16[32,224]{1,0:T(8,128)(2,1)S(1)}, bf16[32,224]{1,0:T(8,128)(2,1)}, u32[]{:S(2)}) copy-start(bf16[32,224]{1,0:T(8,128)(2,1)} %param.16) | copy-start | bytes 43012
  181.2 11.6 %copy-start.24 = (f32[224]{0:T(256)S(1)}, f32[224]{0:T(256)}, u32[]{:S(2)}) copy-start(f32[224]{0:T(256)} %dynamic_slice.17) | copy-start | bytes 2692
